TPU v7x, 32 devices: a whole 2x2x4 slice. The times are simulated.
32 devices in a mesh: section: 2 (over x), dp: 4 (over z), mp: 4 (over y, core).
Axes of the slice: x: 2, y: 2, z: 4, core: 2. Of those that a mesh axis runs over, the one named last changes fastest.
Arguments:
- inputs: bfloat16 [2, 8, 128, 4096], P('section', 'dp'), may hold values from -6 to 6
- norm_gains: bfloat16 [2, 4096], P('section'), may hold values from 0.5 to 1.5
- weights: bfloat16 [2, 4096, 4, 4096], P('section', 'dp', None, 'mp'), may hold values from -0.09375 to 0.09375
- cotangent: bfloat16 [8, 128, 4096], P('dp'), may hold values from -6 to 6
- lengths: int32 [2, 8], P(None, 'dp'), may hold values from 32 to 128, as said below
- dp_noise: float32 [2, 4096, 4, 4096], P('section', 'dp', None, 'mp'), may hold values from -6 to 6
Outputs:
- noisy_grad: float32 [2, 4096, 4, 4096], P('section', 'dp', None, 'mp')
- clip_scale: float32 [8], P('dp')
Inputs may be any that keep to these rules, and one draw needn't show every extreme that they name: `lengths`: the first example of each row has length 128.
All inputs are finite; a program needn't handle non-finite values.
Results may differ from a plain program's by a relative error of at most 0.024.
Values may be sent and summed in bfloat16 or wider, within the bound.
No kernel may reach another device: no remote copies, remote signals or barrier semaphores. Data moves between devices by JAX's collectives and lax.ppermute only.
A program may use at most 320 MiB of HBM per device.

v0:
```python
import jax
import jax.numpy as jnp
from jax import lax
from jax.sharding import PartitionSpec as P

D = 4096
HEADS = 64
HEAD = 64


def from_partner(x, axis, distance):
    return lax.ppermute(x, axis, [(i, i ^ 1 << distance) for i in range(lax.axis_size(axis))])


def rms_norm(values_in, gain_row):
    value32 = values_in.astype(jnp.float32)
    inverse = lax.rsqrt(jnp.mean(value32 * value32, axis=-1, keepdims=True) + 1e-06)
    return (value32 * inverse * gain_row.astype(jnp.float32)).astype(jnp.bfloat16)


def project(left, right):
    return jnp.dot(left, right, preferred_element_type=jnp.float32).astype(jnp.bfloat16)


def attend(queries, key_proj, value_proj, key_mask):
    seq_len = queries.shape[0]
    query_heads = queries.reshape(seq_len, -1, HEAD)
    key_heads = key_proj.reshape(seq_len, -1, HEAD)
    value_heads = value_proj.reshape(seq_len, -1, HEAD)
    scores = jnp.einsum(
        "shd,thd->hst", query_heads, key_heads, preferred_element_type=jnp.float32
    ) * HEAD ** (-0.5)
    scores = jnp.where(key_mask[None, None, :], scores, -jnp.inf)
    attn_probs = jax.nn.softmax(scores, axis=-1)
    probs_low = attn_probs.astype(jnp.bfloat16)
    context = jnp.einsum("hst,thd->shd", probs_low, value_heads, preferred_element_type=jnp.float32)
    return (attn_probs, context.reshape(seq_len, -1).astype(jnp.bfloat16))


def attend_back(queries, key_proj, value_proj, attn_probs, grad_ctx):
    seq_len = queries.shape[0]
    query_heads = queries.reshape(seq_len, -1, HEAD)
    key_heads = key_proj.reshape(seq_len, -1, HEAD)
    value_heads = value_proj.reshape(seq_len, -1, HEAD)
    grad_heads = grad_ctx.reshape(seq_len, -1, HEAD)
    grad_probs = jnp.einsum(
        "shd,thd->hst", grad_heads, value_heads, preferred_element_type=jnp.float32
    )
    inner_sum = jnp.sum(grad_probs * attn_probs, axis=-1, keepdims=True)
    grad_scores = (attn_probs * (grad_probs - inner_sum) * HEAD ** (-0.5)).astype(jnp.bfloat16)
    probs_low = attn_probs.astype(jnp.bfloat16)
    grad_query = jnp.einsum(
        "hst,thd->shd", grad_scores, key_heads, preferred_element_type=jnp.float32
    )
    grad_key = jnp.einsum(
        "hst,shd->thd", grad_scores, query_heads, preferred_element_type=jnp.float32
    )
    grad_value = jnp.einsum(
        "hst,shd->thd", probs_low, grad_heads, preferred_element_type=jnp.float32
    )
    return (
        grad_query.reshape(seq_len, -1).astype(jnp.bfloat16),
        grad_key.reshape(seq_len, -1).astype(jnp.bfloat16),
        grad_value.reshape(seq_len, -1).astype(jnp.bfloat16),
    )


def gram(matrix):
    return jnp.dot(matrix, matrix.T, preferred_element_type=jnp.float32)


def ghost(normed, kv_rows, grad_query, grad_key, grad_value, grad_out, context):
    first = jnp.sum(gram(normed) * gram(grad_query))
    second = jnp.sum(gram(kv_rows) * (gram(grad_key) + gram(grad_value)))
    third = jnp.sum(gram(grad_out) * gram(context))
    return first + second + third


def get_row(buffer, index):
    return lax.dynamic_index_in_dim(buffer, index, 0, keepdims=False)


def put_row(buffer, value, index, valid):
    current = get_row(buffer, index)
    return lax.dynamic_update_index_in_dim(buffer, jnp.where(valid, value, current), index, 0)


def per_device(inputs, norm_gains, weights, cotangent, lengths, dp_noise):
    section_index = lax.axis_index("section")
    is_dec = section_index == 1
    micro_count = inputs.shape[1]
    seq_len = inputs.shape[2]
    width = inputs.shape[3]
    gathered = lax.all_gather(weights, "dp", axis=1, tiled=True)[0]
    inner_dev = gathered.shape[2]
    own_inputs = inputs[0]
    gain_row = norm_gains[0]
    positions = jnp.arange(seq_len)
    wide_zero = jnp.zeros((micro_count, seq_len, width), jnp.bfloat16)
    thin_zero = jnp.zeros((micro_count, seq_len, inner_dev), jnp.bfloat16)
    normed_buf, kv_buf, gout_buf = (wide_zero, wide_zero, wide_zero)
    query_buf, key_buf, value_buf, context_buf = (thin_zero, thin_zero, thin_zero, thin_zero)
    gq_buf, gk_buf, gv_buf = (thin_zero, thin_zero, thin_zero)
    probs_buf = jnp.zeros((micro_count, inner_dev // HEAD, seq_len, seq_len), jnp.float32)
    norm_parts = jnp.zeros((micro_count,), jnp.float32)
    incoming = jnp.zeros((seq_len, width), jnp.bfloat16)
    for step_num in range(micro_count + 2):
        fwd_mb = step_num - section_index
        fwd_ok = (fwd_mb >= 0) & (fwd_mb < micro_count)
        fwd_idx = jnp.clip(fwd_mb, 0, micro_count - 1)
        rows_now = get_row(own_inputs, fwd_idx)
        normed = rms_norm(rows_now, gain_row)
        kv_rows = jnp.where(is_dec, incoming, normed)
        queries = project(normed, gathered[:, 0])
        key_proj = project(kv_rows, gathered[:, 1])
        value_proj = project(kv_rows, gathered[:, 2])
        key_mask = positions < get_row(lengths[0], fwd_idx)
        attn_probs, context_new = attend(queries, key_proj, value_proj, key_mask)
        normed_buf = put_row(normed_buf, normed, fwd_idx, fwd_ok)
        kv_buf = put_row(kv_buf, kv_rows, fwd_idx, fwd_ok)
        query_buf = put_row(query_buf, queries, fwd_idx, fwd_ok)
        key_buf = put_row(key_buf, key_proj, fwd_idx, fwd_ok)
        value_buf = put_row(value_buf, value_proj, fwd_idx, fwd_ok)
        probs_buf = put_row(probs_buf, attn_probs, fwd_idx, fwd_ok)
        context_buf = put_row(context_buf, context_new, fwd_idx, fwd_ok)
        bwd_mb = step_num - 2 + section_index
        bwd_ok = (bwd_mb >= 0) & (bwd_mb < micro_count)
        bwd_idx = jnp.clip(bwd_mb, 0, micro_count - 1)
        dec_mask = (positions < get_row(lengths[1], bwd_idx)).astype(jnp.bfloat16)
        cot_rows = get_row(cotangent, bwd_idx) * dec_mask[:, None]
        grad_out = jnp.where(is_dec, cot_rows, incoming)
        grad_ctx = project(grad_out, gathered[:, 3])
        back_query = get_row(query_buf, bwd_idx)
        back_key = get_row(key_buf, bwd_idx)
        back_value = get_row(value_buf, bwd_idx)
        back_context = get_row(context_buf, bwd_idx)
        grad_query, grad_key, grad_value = attend_back(
            back_query, back_key, back_value, get_row(probs_buf, bwd_idx), grad_ctx
        )
        sq_part = ghost(
            get_row(normed_buf, bwd_idx),
            get_row(kv_buf, bwd_idx),
            grad_query,
            grad_key,
            grad_value,
            grad_out,
            back_context,
        )
        gout_buf = put_row(gout_buf, grad_out, bwd_idx, bwd_ok)
        gq_buf = put_row(gq_buf, grad_query, bwd_idx, bwd_ok)
        gk_buf = put_row(gk_buf, grad_key, bwd_idx, bwd_ok)
        gv_buf = put_row(gv_buf, grad_value, bwd_idx, bwd_ok)
        slot_hit = bwd_ok & (jnp.arange(micro_count) == bwd_idx)
        norm_parts = jnp.where(slot_hit, sq_part, norm_parts)
        if step_num < micro_count + 1:
            relay_term = lax.cond(
                is_dec,
                lambda: jnp.einsum(
                    "sj,dj->sd", grad_key, gathered[:, 1], preferred_element_type=jnp.float32
                )
                + jnp.einsum(
                    "sj,dj->sd", grad_value, gathered[:, 2], preferred_element_type=jnp.float32
                ),
                lambda: jnp.einsum(
                    "sj,dj->sd", context_new, gathered[:, 3], preferred_element_type=jnp.float32
                ),
            )
            residual = jnp.where(is_dec, 0.0, rows_now.astype(jnp.float32))
            summed_rows = lax.psum(relay_term.astype(jnp.bfloat16), "mp").astype(jnp.float32)
            payload = (summed_rows + residual).astype(jnp.bfloat16)
            incoming = from_partner(payload, "section", 0)
    sq_norm = lax.psum(norm_parts, ("section", "mp"))
    bound = jnp.sqrt(jnp.float32(8.0 * D * HEADS * HEAD))
    clip_scale = bound / (jnp.sqrt(sq_norm) + 0.01 * bound)
    totals = jnp.zeros((weights.shape[1] * lax.axis_size("dp"), 4, inner_dev), jnp.float32)
    for micro_num in range(micro_count):
        normed_cols = normed_buf[micro_num]
        kv_cols = kv_buf[micro_num]
        gout_cols = gout_buf[micro_num]
        stacked = jnp.stack(
            [
                jnp.einsum(
                    "sd,sj->dj", normed_cols, gq_buf[micro_num], preferred_element_type=jnp.float32
                ),
                jnp.einsum(
                    "sd,sj->dj", kv_cols, gk_buf[micro_num], preferred_element_type=jnp.float32
                ),
                jnp.einsum(
                    "sd,sj->dj", kv_cols, gv_buf[micro_num], preferred_element_type=jnp.float32
                ),
                jnp.einsum(
                    "sd,sj->dj",
                    gout_cols,
                    context_buf[micro_num],
                    preferred_element_type=jnp.float32,
                ),
            ],
            axis=1,
        )
        totals = totals + clip_scale[micro_num] * stacked
    summed = lax.psum_scatter(
        totals.astype(jnp.bfloat16), "dp", scatter_dimension=0, tiled=True
    ).astype(jnp.float32)
    examples_total = micro_count * lax.axis_size("dp")
    noisy_grad = (summed + dp_noise[0]) / examples_total
    return (noisy_grad[None], clip_scale)


def solution(mesh):
    placed = (
        P("section", "dp", None, None),
        P("section", None),
        P("section", "dp", None, "mp"),
        P("dp", None, None),
        P(None, "dp"),
        P("section", "dp", None, "mp"),
    )
    return jax.shard_map(
        per_device,
        mesh=mesh,
        in_specs=placed,
        out_specs=(P("section", "dp", None, "mp"), P("dp")),
        check_vma=False,
    )
```

profile of v0, /device:TPU:0, one launch (start us, length us, event | category | flops | bytes accessed | tf_op | source)
XLA Modules:
  0.0 1797.7 jit_solution(10161649349527935221)
XLA Ops:
  7.2 9.6 copy.83
  39.0 542.2 %all-gather.2.cloned.1.call-done = bf16[1,4096,4,1024]{3,1,2,0:T(8,128)(2,1)} async-done(((bf16[1,1024,4,1024]{3,1,2,0:T(8,128)(2,1)}), bf16[1,4096,4,1024]{3,1,2,0:T(8,128)(2,1)}) %all-gather.2.cloned.1.call-update) | async-done | bytes 33554448 | tf_op jit(solution)/shard_map/all_gather | solution.py:94
  630.3 7.8 conditional.3
  630.7 7.3 fusion
  647.3 31.6 %all-reduce.4.cloned.1.call-done = bf16[128,4096]{1,0:T(8,128)(2,1)} async-done(((bf16[128,4096]{1,0:T(8,128)(2,1)}), bf16[128,4096]{1,0:T(8,128)(2,1)}) %all-reduce.4.cloned.1.call-update) | async-done | bytes 1048592 | tf_op jit(solution)/shard_map/psum | solution.py:169
  798.8 24.3 %all-reduce.6.cloned.1.call-done = bf16[128,4096]{1,0:T(8,128)(2,1)} async-done(((bf16[128,4096]{1,0:T(8,128)(2,1)}), bf16[128,4096]{1,0:T(8,128)(2,1)}) %all-reduce.6.cloned.1.call-update) | async-done | bytes 1048592 | tf_op jit(solution)/shard_map/psum | solution.py:169
  827.7 22.3 %collective-permute-done.1 = bf16[128,4096]{1,0:T(8,128)(2,1)S(1)} collective-permute-done((bf16[128,4096]{1,0:T(8,128)(2,1)S(1)}, bf16[128,4096]{1,0:T(8,128)(2,1)S(1)}, u32[]{:S(2)}, u32[]{:S(2)}) %collective-permute-start.1) | collective-permute-done | bytes 1048608 | tf_op jit(solution)/shard_map/ppermute | solution.py:12
  911.1 7.4 conditional.5
  911.1 7.4 fusion.24
  934.5 28.1 %all-reduce.8.cloned.1.call-done = bf16[128,4096]{1,0:T(8,128)(2,1)} async-done(((bf16[128,4096]{1,0:T(8,128)(2,1)}), bf16[128,4096]{1,0:T(8,128)(2,1)}) %all-reduce.8.cloned.1.call-update) | async-done | bytes 1048592 | tf_op jit(solution)/shard_map/psum | solution.py:169
  968.1 21.3 %collective-permute-done.2 = bf16[128,4096]{1,0:T(8,128)(2,1)S(1)} collective-permute-done((bf16[128,4096]{1,0:T(8,128)(2,1)S(1)}, bf16[128,4096]{1,0:T(8,128)(2,1)S(1)}, u32[]{:S(2)}, u32[]{:S(2)}) %collective-permute-start.2) | collective-permute-done | bytes 1048608 | tf_op jit(solution)/shard_map/ppermute | solution.py:12
  1038.7 9.9 convolution_bitcast_fusion.1
  1048.6 9.0 convolution_bitcast_fusion.5
  1057.7 9.1 convolution_bitcast_fusion.2
  1066.8 9.1 convolution_bitcast_fusion.6
  1088.4 8.1 convolution_bitcast_fusion.3
  1096.4 8.3 convolution_bitcast_fusion.7
  1115.9 8.1 convolution_bitcast_fusion
  1126.6 8.5 convolution_bitcast_fusion.4
  1135.1 12.0 psum.31
  1147.7 53.8 %fusion.45 = bf16[4096,4,1024]{2,0,1:T(8,128)(2,1)} fusion(f32[4096,1,1024]{2,0,1:T(8,128)} %convolution_bitcast_fusion.4, f32[4096,1,1024]{2,0,1:T(8,128)} %convolution_bitcast_fusion.5, f32[4096,1,1024]{2,0,1:T(8,128)} %convolution_bitcast_fusion.6, f32[4096,1,1024]{2,0,1:T(8,128)} %convolution_bitcast_fusion.7, ...), kind=kLoop, calls=%fused_computation.40 | loop fusion | flops 167772160 | bytes 167772160 | tf_op jit(solution)/shard_map/convert_element_type | solution.py:202
  1201.5 551.6 %reduce-scatter.2.cloned.1.call-done = bf16[1024,4,1024]{2,0,1:T(8,128)(2,1)} async-done(((bf16[4096,4,1024]{2,0,1:T(8,128)(2,1)}), bf16[1024,4,1024]{2,0,1:T(8,128)(2,1)}) %reduce-scatter.2.cloned.1.call-update) | async-done | bytes 8388624 | tf_op jit(solution)/shard_map/reduce_scatter | solution.py:201
  1753.1 15.9 fusion.47
  1769.1 21.9 %copy.145 = f32[1,1024,4,1024]{3,2,1,0:T(4,128)} copy(f32[1,1024,4,1024]{3,1,2,0:T(8,128)S(1)} %fusion.47) | data formatting | bytes 33554432
  (361 shorter events, 362.6 us)
Async XLA Ops:
  7.2 574.0 %all-gather.2.cloned.1.call-start = ((), (), s32[]{:S(2)}) async-start(), calls=%async_computation.1 | async-start | bytes 41943040 | tf_op jit(solution)/shard_map/all_gather | solution.py:94
  16.9 662.0 %all-reduce.4.cloned.1.call-start = ((), (), s32[]{:S(2)}) async-start(), calls=%async_computation.2 | async-start | bytes 2097152 | tf_op jit(solution)/shard_map/psum | solution.py:169
  29.4 551.7 %copy-start.68 = (bf16[128]{0:T(256)(128)(2,1)}, bf16[128]{0:T(256)(128)(2,1)S(1)}, u32[]{:S(2)}) copy-start(bf16[128]{0:T(256)(128)(2,1)S(1)} %compare_convert_fusion.3) | copy-start | bytes 772
  591.6 21.0 %copy-start.24 = (bf16[2,128,1024]{2,1,0:T(8,128)(2,1)}, bf16[2,128,1024]{2,1,0:T(8,128)(2,1)S(1)}, u32[]{:S(2)}) copy-start(bf16[2,128,1024]{2,1,0:T(8,128)(2,1)S(1)} %get-tuple-element.152) | copy-start | bytes 1572868
  638.1 185.0 %all-reduce.6.cloned.1.call-start = ((), (), s32[]{:S(2)}) async-start(), calls=%async_computation.3 | async-start | bytes 2097152 | tf_op jit(solution)/shard_map/psum | solution.py:169
  683.4 11.9 copy-start.57
  688.3 16.2 copy-start.46
  688.3 28.1 %collective-permute-start = (bf16[128,4096]{1,0:T(8,128)(2,1)}, bf16[128,4096]{1,0:T(8,128)(2,1)}, u32[]{:S(2)}, u32[]{:S(2)}) collective-permute-start(bf16[128,4096]{1,0:T(8,128)(2,1)} %get-tuple-element.111), channel_id=1, source_target_pairs={{0,16},{16,0},{1,17},{17,1},{2,18},{18,2},{3,19},{19,3},{4,20},{20... | collective-permute-start | bytes 3145736 | tf_op jit(solution)/shard_map/ppermute | solution.py:12
  780.9 181.7 %all-reduce.8.cloned.1.call-start = ((), (), s32[]{:S(2)}) async-start(), calls=%async_computation.4 | async-start | bytes 2097152 | tf_op jit(solution)/shard_map/psum | solution.py:169
  797.1 29.7 %copy-start.40 = (bf16[1,128,1024]{2,1,0:T(8,128)(2,1)S(1)}, bf16[1,128,1024]{2,1,0:T(8,128)(2,1)}, u32[]{:S(2)}) copy-start(bf16[1,128,1024]{2,1,0:T(8,128)(2,1)} %copy.132) | copy-start | bytes 786436
  823.1 26.8 %copy-start.21 = (bf16[2,128,4096]{2,1,0:T(8,128)(2,1)S(1)}, bf16[2,128,4096]{2,1,0:T(8,128)(2,1)}, u32[]{:S(2)}) copy-start(bf16[2,128,4096]{2,1,0:T(8,128)(2,1)} %copy.184) | copy-start | bytes 6291460
  825.2 24.7 %collective-permute-start.1 = (bf16[128,4096]{1,0:T(8,128)(2,1)S(1)}, bf16[128,4096]{1,0:T(8,128)(2,1)S(1)}, u32[]{:S(2)}, u32[]{:S(2)}) collective-permute-start(bf16[128,4096]{1,0:T(8,128)(2,1)S(1)} %fusion.79), channel_id=1, source_target_pairs={{0,16},{16,0},{1,17},{17,1},{2,18},{18,2},{3,19},{19,3},{4,20},{20... | collective-permute-start | bytes 3145736 | tf_op jit(solution)/shard_map/ppermute | solution.py:12
  826.9 23.1 %copy-start.2 = (bf16[1,2,128,4096]{3,2,1,0:T(8,128)(2,1)S(1)}, bf16[1,2,128,4096]{3,2,1,0:T(8,128)(2,1)}, u32[]{:S(2)}) copy-start(bf16[1,2,128,4096]{3,2,1,0:T(8,128)(2,1)} %param.12) | copy-start | bytes 6291460
  826.9 23.1 %copy-start.60 = (f32[128]{0:T(128)S(1)}, f32[128]{0:T(128)}, u32[]{:S(2)}) copy-start(f32[128]{0:T(128)} %copy-done.59) | copy-start | bytes 1540
  826.9 23.1 %copy-start.65 = (bf16[128]{0:T(256)(128)(2,1)S(1)}, bf16[128]{0:T(256)(128)(2,1)}, u32[]{:S(2)}) copy-start(bf16[128]{0:T(256)(128)(2,1)} %compare_convert_fusion.1) | copy-start | bytes 772
  918.5 834.6 %reduce-scatter.2.cloned.1.call-start = ((), (), s32[]{:S(2)}) async-start(), calls=%async_computation.5 | async-start | bytes 41943040 | tf_op jit(solution)/shard_map/reduce_scatter | solution.py:201
  964.6 24.7 %collective-permute-start.2 = (bf16[128,4096]{1,0:T(8,128)(2,1)S(1)}, bf16[128,4096]{1,0:T(8,128)(2,1)S(1)}, u32[]{:S(2)}, u32[]{:S(2)}) collective-permute-start(bf16[128,4096]{1,0:T(8,128)(2,1)S(1)} %fusion.89), channel_id=1, source_target_pairs={{0,16},{16,0},{1,17},{17,1},{2,18},{18,2},{3,19},{19,3},{4,20},{20... | collective-permute-start | bytes 3145736 | tf_op jit(solution)/shard_map/ppermute | solution.py:12
  967.8 21.5 %copy-start.3 = (bf16[1,2,128,4096]{3,2,1,0:T(8,128)(2,1)S(1)}, bf16[1,2,128,4096]{3,2,1,0:T(8,128)(2,1)}, u32[]{:S(2)}) copy-start(bf16[1,2,128,4096]{3,2,1,0:T(8,128)(2,1)} %param.12) | copy-start | bytes 6291460
  967.8 21.5 %copy-start.58 = (f32[128]{0:T(128)S(1)}, f32[128]{0:T(128)}, u32[]{:S(2)}) copy-start(f32[128]{0:T(128)} %copy-done.57) | copy-start | bytes 1540
  967.8 21.5 %copy-start.63 = (bf16[128]{0:T(256)(128)(2,1)S(1)}, bf16[128]{0:T(256)(128)(2,1)}, u32[]{:S(2)}) copy-start(bf16[128]{0:T(256)(128)(2,1)} %compare_convert_fusion) | copy-start | bytes 772
  1038.7 9.9 copy-start.10
  1077.8 8.5 copy-start.32
  1115.9 10.7 copy-start.18
  1147.1 54.4 %copy-start.56 = (f32[2]{0:T(128)}, f32[2]{0:T(128)S(1)}, u32[]{:S(2)}) copy-start(f32[2]{0:T(128)S(1)} %add_divide_fusion) | copy-start | bytes 28
  (55 other events, 206.5 us)
Sparse Core Ops, SparseCore 0:
  17.0 564.0 all-gather.1
  638.2 40.6 all-reduce.3
  781.0 42.0 all-reduce.5
  918.6 43.9 all-reduce.7
  1201.6 551.4 reduce-scatter.1
where the time goes:
time: 1800 us
  waiting for transfers between devices  1220 us (68%)
  matrix products  266 us (15%)
  local copies, waits for them, and re-layouts  137 us (8%)
  other arithmetic  132 us (7%)
  between operations  22.5 us (1%)
    reduce_scatter x1, waiting for transfers between devices, per_device(): lax.psum_scatter(totals.astype(jnp.bfloat16), 'dp', scatter_dimension=0,...  552 us
    all_gather x1, waiting for transfers between devices, per_device(): gathered = lax.all_gather(weights, 'dp', axis=1, tiled=True)[0]  542 us
    dot_general x16, matrix products, project(): jnp.dot(left, right, preferred_element_type=jnp.float32)  85.9 us
    psum x3, waiting for transfers between devices, per_device(): lax.psum(relay_term.astype(jnp.bfloat16), 'mp').astype(jnp.float32)  83.9 us
    unnamed x147, local copies, waits for them, and re-layouts  54.9 us
    convert_element_type x1, other arithmetic, per_device(): totals.astype(jnp.bfloat16)  53.8 us
    dynamic_update_slice x25, other arithmetic, put_row(): lax.dynamic_update_index_in_dim(buffer, jnp.where(valid, value, current),...  45.3 us
    ppermute x3, waiting for transfers between devices, from_partner(): lax.ppermute(x, axis, [(i, i ^ 1 << distance) for i in range(lax.axis_siz...  43.6 us
  transfers between devices with their start and end apart: 8, of which 7 were waited for; matrix products, arithmetic and copies ran while one was open for 5% of the time, Pallas kernels for 0%

commit v1 on v0

v1 whole, which is shorter than its diff:
```python
import functools

import jax
import jax.numpy as jnp
from jax import lax
from jax.experimental import pallas as pl
from jax.experimental.pallas import tpu as pltpu
from jax.sharding import PartitionSpec as P

D = 4096
HEADS = 64
HEAD = 64
PAIR = 2 * HEAD
F32 = jnp.float32
BF16 = jnp.bfloat16
NN = (((1,), (0,)), ((), ()))
NT = (((1,), (1,)), ((), ()))
TN = (((0,), (0,)), ((), ()))


def mm(left, right, dims=NN):
    return lax.dot_general(left, right, dims, preferred_element_type=F32)


def dp_shift(x, distance, sections):
    n = lax.axis_size("dp")
    pairs = [(s * n + i, s * n + (i ^ distance)) for s in sections for i in range(n)]
    return lax.ppermute(x, ("section", "dp"), pairs)


def mp_shift(x, distance, sections, flip=False):
    n = lax.axis_size("mp")
    pairs = [
        (s * n + i, (1 - s if flip else s) * n + (i ^ distance)) for s in sections for i in range(n)
    ]
    return lax.ppermute(x, ("section", "mp"), pairs)


def pick(parts, index):
    return lax.dynamic_index_in_dim(parts, index, 0, keepdims=False)


def to_owner(parts, sections):
    n = lax.axis_size("dp")
    me = lax.axis_index("dp")
    got = [dp_shift(pick(parts, me ^ s), s, sections) for s in range(n - 1, 0, -1)]
    return [pick(parts, me)] + got


def in_order(slots):
    me = lax.axis_index("dp")
    stacked = jnp.stack(slots)
    return jnp.stack([pick(stacked, me ^ i) for i in range(len(slots))])


def gather(rows, sections):
    n = lax.axis_size("dp")
    got = {s: dp_shift(rows, s, sections) for s in range(n - 1, 0, -1)}
    return in_order([rows] + [got[s] for s in range(1, n)])


def halves(mine, other, parity):
    return jnp.where(
        parity == 0,
        jnp.concatenate([mine, other], axis=-2),
        jnp.concatenate([other, mine], axis=-2),
    )


def to_columns(rows, parity, sections):
    n = lax.axis_size("dp")
    me = lax.axis_index("dp")
    k, seq, full = rows.shape
    half, width = seq // 2, full // n
    mine = [
        lax.dynamic_slice(rows, (0, parity * half, (me ^ s) * width), (k, half, width))
        for s in range(n)
    ]
    got = {s: dp_shift(mine[s], s, sections) for s in range(n - 1, 0, -1)}
    return in_order([mine[0]] + [got[s] for s in range(1, n)])


def relay(terms, residual, source):
    groups = lax.axis_size("mp") // 2
    index = lax.axis_index("mp")
    parity = index % 2
    half = terms.shape[1] // 2
    low = terms.astype(BF16)
    keep = lax.dynamic_slice_in_dim(low, parity * half, half, 1)
    give = lax.dynamic_slice_in_dim(low, (1 - parity) * half, half, 1)
    total = keep.astype(F32) + mp_shift(give, 1, (source,)).astype(F32)
    if residual is not None:
        total = total + jnp.where(index < 2, residual.astype(F32), 0.0)
    total = total.astype(BF16)
    got = [mp_shift(total, 2 * g, (source,), flip=True).astype(F32) for g in range(groups)]
    mine = functools.reduce(jnp.add, got).astype(BF16)
    other = mp_shift(mine, 1, (1 - source,))
    return halves(mine, other, parity)


def add_up(sources, start):
    terms = [ref[:, offset + start : offset + start + PAIR] for ref, offset in sources]
    if len(terms) == 1:
        return terms[0]
    return functools.reduce(jnp.add, [t.astype(F32) for t in terms]).astype(BF16)


def pair_masks(seq):
    lane = lax.broadcasted_iota(jnp.int32, (seq, PAIR), 1)
    return lane < HEAD


def stack_heads(x, first):
    zero = jnp.zeros_like(x)
    return jnp.concatenate([jnp.where(first, x, zero), jnp.where(first, zero, x)], axis=0)


def softmax_pair(scores, valid):
    seq = scores.shape[0]
    out = []
    for h in range(2):
        s = jnp.where(valid, scores[:, h * seq : (h + 1) * seq] * HEAD**-0.5, -jnp.inf)
        e = jnp.exp(s - jnp.max(s, axis=1, keepdims=True))
        out.append(e / jnp.sum(e, axis=1, keepdims=True))
    return jnp.concatenate(out, axis=1)


def bind(plan, refs):
    return [[(refs[i], offset) for i, offset in sources] for sources in plan]


def fwd_kernel(plan, count, info, *refs):
    qs, ks, vs = bind(plan, refs)
    ctx_ref = refs[count]
    seq, width = ctx_ref.shape

    @pl.when(info[0] == 1)
    def run():
        first = pair_masks(seq)
        valid = lax.broadcasted_iota(jnp.int32, (seq, seq), 1) < info[1]
        for c in range(0, width, PAIR):
            q, k, v = add_up(qs, c), add_up(ks, c), add_up(vs, c)
            probs = softmax_pair(mm(q, stack_heads(k, first), NT), valid)
            ctx = mm(probs.astype(BF16), stack_heads(v, first))
            ctx_ref[:, c : c + PAIR] = ctx.astype(BF16)


def full_kernel(plan, count, decoder, info, *refs):
    qs, ks, vs, gs = bind(plan, refs)
    kv_ref, send_ref, gram_ref = refs[count:]
    seq = kv_ref.shape[0]
    width = kv_ref.shape[1] // 2

    @pl.when(info[0] == 1)
    def run():
        first = pair_masks(seq)
        valid = lax.broadcasted_iota(jnp.int32, (seq, seq), 1) < info[1]
        grams = [jnp.zeros((seq, seq), F32) for _ in range(3)]
        for c in range(0, width, PAIR):
            q, k, v, g = add_up(qs, c), add_up(ks, c), add_up(vs, c), add_up(gs, c)
            k2, v2 = stack_heads(k, first), stack_heads(v, first)
            probs = softmax_pair(mm(q, k2, NT), valid)
            low = probs.astype(BF16)
            ctx = mm(low, v2).astype(BF16)
            gp = mm(g, v2, NT)
            ds = []
            for h in range(2):
                part = slice(h * seq, (h + 1) * seq)
                p, gph = probs[:, part], gp[:, part]
                inner = jnp.sum(gph * p, axis=1, keepdims=True)
                ds.append((p * (gph - inner) * HEAD**-0.5).astype(BF16))
            ds = jnp.concatenate(ds, axis=1)
            gq = mm(ds, k2).astype(BF16)
            gk = mm(ds, q, TN)
            gk = jnp.where(first, gk[:seq], gk[seq:]).astype(BF16)
            gv = mm(low, g, TN)
            gv = jnp.where(first, gv[:seq], gv[seq:]).astype(BF16)
            kv_ref[:, c : c + PAIR] = gk
            kv_ref[:, width + c : width + c + PAIR] = gv
            send_ref[:, c : c + PAIR] = gq
            send_ref[:, width + c : width + c + PAIR] = ctx if decoder else gk
            send_ref[:, 2 * width + c : 2 * width + c + PAIR] = gv
            grams[0] += mm(gq, gq, NT)
            grams[1] += mm(gk, gk, NT) + mm(gv, gv, NT)
            grams[2] += mm(ctx, ctx, NT)
        for i in range(3):
            gram_ref[i] = grams[i]


def call_attention(kernel, info, operands, outs, flops, name):
    arrays, plan = [], []
    for sources in operands:
        plan.append([])
        for array, offset in sources:
            known = [i for i, a in enumerate(arrays) if a is array]
            if not known:
                arrays.append(array)
            plan[-1].append((known[0] if known else len(arrays) - 1, offset))
    vmem = pl.BlockSpec(memory_space=pltpu.VMEM)
    return pl.pallas_call(
        functools.partial(kernel, plan, len(arrays)),
        out_shape=outs,
        in_specs=[pl.BlockSpec(memory_space=pltpu.SMEM)] + [vmem] * len(arrays),
        out_specs=(vmem,) * len(outs),
        compiler_params=pltpu.CompilerParams(vmem_limit_bytes=32 << 20),
        cost_estimate=pl.CostEstimate(
            flops=flops, bytes_accessed=sum(2 * a.size for a in arrays), transcendentals=0
        ),
        name=name,
    )(info, *arrays)


def attend(info, operands, seq, width):
    rows = jax.ShapeDtypeStruct((seq, width), BF16)
    return call_attention(fwd_kernel, info, operands, (rows,), 8 * seq * seq * width, "attend")[0]


def attend_back(info, operands, seq, width, decoder):
    outs = (
        jax.ShapeDtypeStruct((seq, 2 * width), BF16),
        jax.ShapeDtypeStruct((seq, 3 * width), BF16),
        jax.ShapeDtypeStruct((3, seq, seq), F32),
    )

    def kernel(plan, count, *refs):
        full_kernel(plan, count, decoder, *refs)

    return call_attention(kernel, info, operands, outs, 40 * seq * seq * width, "attend_back")


def wgrad_kernel(mb, chunk, scale, clip, info, *refs):
    x1, xa, xb = refs[:mb], refs[mb : 2 * mb], refs[2 * mb : 3 * mb]
    send, swap = refs[3 * mb : 4 * mb], refs[4 * mb : 5 * mb]
    noise, out = refs[5 * mb :]
    width = out.shape[2]
    count = x1[0].shape[0] // chunk
    is_dec = info[0] == 1

    def clipped(group):
        return [
            jnp.concatenate(
                [
                    (ref[i * chunk : (i + 1) * chunk].astype(F32) * clip[b * count + i]).astype(BF16)
                    for i in range(count)
                ],
                axis=0,
            )
            for b, ref in enumerate(group)
        ]

    def put(slot, lefts, rights, first):
        total = functools.reduce(
            jnp.add, [mm(x, y[:, first : first + width], TN) for x, y in zip(lefts, rights)]
        )
        out[:, slot, :] = (total + noise[:, slot, :]) * scale

    l1, la, lb = clipped(x1), clipped(xa), clipped(xb)
    put(0, l1, send, 0)

    @pl.when(is_dec)
    def decoder():
        put(1, lb, swap, 0)
        put(2, lb, send, 2 * width)
        put(3, la, send, width)

    @pl.when(jnp.logical_not(is_dec))
    def encoder():
        put(1, la, send, width)
        put(2, l1, send, 2 * width)
        put(3, lb, swap, 0)


def wgrad(clip, info, x1, xa, xb, send, swap, noise, chunk, examples):
    mb = len(x1)
    tokens, depth = x1[0].shape
    width = noise.shape[2]
    block = 128
    smem = pl.BlockSpec(memory_space=pltpu.SMEM)
    left = pl.BlockSpec((tokens, block), lambda i: (0, i))
    wide = pl.BlockSpec((block, 4, width), lambda i: (i, 0, 0))
    once = [
        pl.BlockSpec(y.shape, lambda i: (0, 0), pipeline_mode=pl.Buffered(1)) for y in send + swap
    ]
    return pl.pallas_call(
        functools.partial(wgrad_kernel, mb, chunk, 1.0 / examples),
        grid=(depth // block,),
        out_shape=jax.ShapeDtypeStruct(noise.shape, F32),
        in_specs=[smem, smem] + [left] * (3 * mb) + once + [wide],
        out_specs=wide,
        compiler_params=pltpu.CompilerParams(vmem_limit_bytes=56 << 20),
        cost_estimate=pl.CostEstimate(
            flops=8 * mb * tokens * depth * width,
            bytes_accessed=depth * 4 * width * 8 + mb * tokens * width * 8,
            transcendentals=0,
        ),
        name="weight_gradient",
    )(clip, info, *x1, *xa, *xb, *send, *swap, noise)


def per_device(inputs, norm_gains, weights, cotangent, lengths, dp_noise):
    section = lax.axis_index("section")
    is_dec = section == 1
    me = lax.axis_index("dp")
    parity = lax.axis_index("mp") % 2
    n = lax.axis_size("dp")
    mb = inputs.shape[1]
    seq = inputs.shape[2]
    depth = weights.shape[1]
    inner = weights.shape[3]
    both, enc, dec = (0, 1), (0,), (1,)
    w = lax.optimization_barrier(jnp.transpose(weights[0], (1, 0, 2)))
    gain = norm_gains[0].astype(F32)
    gain_cols = lax.dynamic_slice_in_dim(gain, me * depth, depth)

    def rows_of(x):
        return x.reshape(n * seq, x.shape[-1])

    def owner_gram(x, sections):
        terms = jnp.einsum("bntd,bnud->nbtu", x, x, preferred_element_type=F32)
        return functools.reduce(jnp.add, to_owner(terms, sections))

    def info(flag, b):
        return jnp.stack([flag.astype(jnp.int32), lengths[0, b]])

    own32 = inputs[0].astype(F32)
    inv = lax.rsqrt(jnp.mean(own32 * own32, axis=-1) + 1e-06)
    inv_all = gather(inv, both)
    raw_half, x = [], []
    for b in range(mb):
        mine = to_columns(inputs[0, b : b + 1], parity, both)[:, 0]
        raw = halves(mine, mp_shift(mine, 1, both), parity)
        raw_half.append(mine)
        x.append(rows_of((raw.astype(F32) * inv_all[:, b, :, None] * gain_cols).astype(BF16)))
    keep = (jnp.arange(seq)[None] < lengths[1][:, None]).astype(BF16)
    cot = cotangent * keep[:, :, None]
    cot_half = to_columns(cot, parity, dec)
    cot_cols = halves(cot_half, mp_shift(cot_half, 1, dec), parity)
    cot_cols = [rows_of(cot_cols[:, b]) for b in range(mb)]
    first = []
    for b in range(mb):
        if b < mb - 1:
            parts = [mm(x[b], w[s]) for s in range(3)]
        else:
            w_k, w_v = jnp.where(is_dec, w[3], w[1]), jnp.where(is_dec, w[3], w[2])
            parts = [
                mm(x[b], w[0]),
                mm(jnp.where(is_dec, cot_cols[0], x[b]), w_k),
                mm(jnp.where(is_dec, cot_cols[1], x[b]), w_v),
            ]
        parts = jnp.concatenate([p.astype(BF16) for p in parts], axis=1)
        first.append(
            lax.psum_scatter(
                parts.reshape(n, seq, 3 * inner), "dp", scatter_dimension=0, tiled=False
            )
        )
    ctx_all, enc_out = [], []
    for b in range(mb):
        qkv = [[(first[b], i * inner)] for i in range(3)]
        ctx = attend(info(section == 0, b), qkv, seq, inner)
        ctx_all.append(rows_of(gather(ctx, enc)))
        terms = mm(ctx_all[b], w[3], NT).reshape(n, seq, depth)
        enc_out.append(relay(terms, raw_half[b], 0))
    gk_all, grad_enc, dec_send, dec_gram = [], [], [], []
    for b in range(mb):
        rows = rows_of(enc_out[b])
        parts = [mm(rows, w[s]).astype(BF16) for s in (1, 2)]
        kv = to_owner(jnp.concatenate(parts, axis=1).reshape(n, seq, 2 * inner), dec)
        operands = [
            [(first[b], 0)],
            [(part, 0) for part in kv],
            [(part, inner) for part in kv],
            [(first[mb - 1], (1 + b) * inner)],
        ]
        gkv, send, gram = attend_back(info(section == 1, b), operands, seq, inner, True)
        gkv_all = rows_of(gather(gkv, dec))
        terms = mm(gkv_all[:, :inner], w[1], NT) + mm(gkv_all[:, inner:], w[2], NT)
        grad_enc.append(relay(terms.reshape(n, seq, depth), None, 1))
        gk_all.append(gkv_all[:, :inner])
        dec_send.append(send)
        dec_gram.append(gram)
    gram_enc_out = owner_gram(jnp.stack(enc_out), dec)
    enc_send, enc_gram = [], []
    for b in range(mb):
        gctx = to_owner(mm(rows_of(grad_enc[b]), w[3]).astype(BF16).reshape(n, seq, inner), enc)
        operands = [[(first[b], i * inner)] for i in range(3)] + [[(part, 0) for part in gctx]]
        unused, send, gram = attend_back(info(section == 0, b), operands, seq, inner, False)
        enc_send.append(send)
        enc_gram.append(gram)
    gram_grad_enc = owner_gram(jnp.stack(grad_enc), enc)
    send_all = [
        lax.all_gather(jnp.where(is_dec, d, e), "dp", axis=0, tiled=True)
        for d, e in zip(dec_send, enc_send)
    ]
    normed = (own32 * inv[..., None] * gain).astype(BF16)
    gram_x = jnp.einsum("btd,bud->btu", normed, normed, preferred_element_type=F32)
    gram_cot = jnp.einsum("btd,bud->btu", cot, cot, preferred_element_type=F32)
    dg, eg = jnp.stack(dec_gram, axis=1), jnp.stack(enc_gram, axis=1)
    dec_sq = jnp.sum(gram_x * dg[0] + gram_enc_out * dg[1] + gram_cot * dg[2], axis=(1, 2))
    enc_sq = jnp.sum(gram_x * (eg[0] + eg[1]) + gram_grad_enc * eg[2], axis=(1, 2))
    sq = jnp.where(is_dec, dec_sq, enc_sq)
    step = 1
    while step < lax.axis_size("mp"):
        sq = sq + mp_shift(sq, step, both)
        step *= 2
    sq = sq + mp_shift(sq, 0, both, flip=True)
    bound = jnp.sqrt(jnp.float32(8.0 * D * HEADS * HEAD))
    clip = bound / (jnp.sqrt(sq) + 0.01 * bound)
    clip_all = gather(clip, both).T.reshape(-1)
    xa = [jnp.where(is_dec, c, r) for c, r in zip(cot_cols, x)]
    xb = [rows_of(jnp.where(is_dec, o, g)) for o, g in zip(enc_out, grad_enc)]
    swap = [jnp.where(is_dec, k, c) for k, c in zip(gk_all, ctx_all)]
    flag = section.astype(jnp.int32)[None]
    out = wgrad(clip_all, flag, x, xa, xb, send_all, swap, dp_noise[0], seq, mb * n)
    return (out[None], clip)


def solution(mesh):
    placed = (
        P("section", "dp", None, None),
        P("section", None),
        P("section", "dp", None, "mp"),
        P("dp", None, None),
        P(None, "dp"),
        P("section", "dp", None, "mp"),
    )
    return jax.shard_map(
        per_device,
        mesh=mesh,
        in_specs=placed,
        out_specs=(P("section", "dp", None, "mp"), P("dp")),
        check_vma=False,
    )
```

time: 1800 us -> 661 us (0.37)
  waiting for transfers between devices: 1220 us -> 361 us
  matrix products: 266 us -> 40 us
  starting transfers between devices: 5.39 us -> 122 us
  local copies, waits for them, and re-layouts: 137 us -> 27.1 us
  other arithmetic: 132 us -> 43.8 us
  Pallas kernels: 0 us -> 42 us
    all_gather x1 -> x2, waiting for transfers between devices: 542 us -> 10.9 us  [per_device(): lax.all_gather(jnp.where(is_dec, d, e), 'dp', axis=0, tiled=True)]
    reduce_scatter x1 -> x2, waiting for transfers between devices: 552 us -> 81.5 us  [per_device(): lax.psum_scatter(parts.reshape(n, seq, 3 * inner), 'dp', scatter_dimensio...]
    ppermute x3 -> x67, waiting for transfers between devices: 43.6 us -> 269 us  [the longest x22 179 us: mp_shift(): return lax.ppermute(x, ('section', 'mp'), pairs)]
    dot_general x79 -> x22, matrix products: 257 us -> 40 us  [the longest x18 36 us: mm(): return lax.dot_general(left, right, dims, preferred_element_type=F32)]
    ppermute x3 -> x67, starting transfers between devices: 4.6 us -> 122 us  [the longest x45 90.6 us: dp_shift(): return lax.ppermute(x, ('section', 'dp'), pairs)]
    psum x3 -> x0, waiting for transfers between devices: 83.9 us -> none  [per_device(): lax.psum(relay_term.astype(jnp.bfloat16), 'mp').astype(jnp.float32)]
    convert_element_type x7 -> x13, other arithmetic: 62.1 us -> 6.63 us  [the longest x2 2.45 us: per_device(): raw.astype(F32) * inv_all[:, b, :, None] * gain_cols]
    dynamic_update_slice x25 -> x0, other arithmetic: 45.3 us -> none  [put_row(): lax.dynamic_update_index_in_dim(buffer, jnp.where(valid, value, current),...]
  transfers between devices with their start and end apart: 8 -> 71, of which waited for: 7 -> 31; matrix products, arithmetic and copies ran while one was open for 5% -> 13% of each run, Pallas kernels for 0% -> 2%
where the time goes in v1:
time: 661 us; the launch traced here: 652 us
  waiting for transfers between devices  361 us (55%)
  starting transfers between devices  122 us (18%)
  other arithmetic  43.8 us (7%)
  Pallas kernels  42 us (6%)
  matrix products  40 us (6%)
  local copies, waits for them, and re-layouts  27.1 us (4%)
  between operations  16.3 us (2%)
    ppermute x22, waiting for transfers between devices, mp_shift(): return lax.ppermute(x, ('section', 'mp'), pairs)  179 us
    ppermute x45, starting transfers between devices, dp_shift(): return lax.ppermute(x, ('section', 'dp'), pairs)  90.6 us
    ppermute x45, waiting for transfers between devices, dp_shift(): return lax.ppermute(x, ('section', 'dp'), pairs)  90 us
    reduce_scatter x2, waiting for transfers between devices, per_device(): lax.psum_scatter(parts.reshape(n, seq, 3 * inner), 'dp', scatter_dimensio...  81.5 us
    dot_general x18, matrix products, mm(): return lax.dot_general(left, right, dims, preferred_element_type=F32)  36 us
    ppermute x22, starting transfers between devices, mp_shift(): return lax.ppermute(x, ('section', 'mp'), pairs)  31 us
    pallas_call x1, Pallas kernels, wgrad(): pl.pallas_call(functools.partial(wgrad_kernel, mb, chunk, 1.0 / examples)...  25.4 us
    pallas_call x6, Pallas kernels, call_attention(): pl.pallas_call(functools.partial(kernel, plan, len(arrays)), out_shape=ou...  16.6 us
  transfers between devices with their start and end apart: 71, of which 31 were waited for; matrix products, arithmetic and copies ran while one was open for 13% of the time, Pallas kernels for 2%

profile of v1, /device:TPU:0, one launch (start us, length us, event | category | flops | bytes accessed | tf_op | source)
XLA Modules:
  0.0 652.4 jit_solution(15945854621410191122)
XLA Ops:
  11.9 5.0 collective-permute-start.19
  22.7 4.9 collective-permute-start
  27.6 9.7 %copy.34 = bf16[1,1024,4,1024]{3,1,2,0:T(8,128)(2,1)} copy(bf16[1,1024,4,1024]{3,2,1,0:T(4,128)(2,1)} %param.8) | data formatting | bytes 16777216 | tf_op args[2]
  76.4 36.8 %reduce-scatter.3.cloned.1.call-done = bf16[1,128,3072]{2,1,0:T(8,128)(2,1)} async-done(((bf16[4,128,3072]{2,1,0:T(8,128)(2,1)}), bf16[1,128,3072]{2,1,0:T(8,128)(2,1)}) %reduce-scatter.3.cloned.1.call-update) | async-done | bytes 786448 | tf_op jit(solution)/shard_map/reduce_scatter | solution.py:352
  129.1 14.7 %collective-permute-done.8 = bf16[128,1024]{1,0:T(8,128)(2,1)S(1)} collective-permute-done((bf16[128,1024]{1,0:T(8,128)(2,1)S(1)}, bf16[128,1024]{1,0:T(8,128)(2,1)S(1)}, u32[]{:S(2)}, u32[]{:S(2)}) %collective-permute-start.8) | collective-permute-done | bytes 262176 | tf_op jit(solution)/shard_map/ppermute | solution.py:28
  150.8 44.6 %reduce-scatter.5.cloned.1.call-done = bf16[1,128,3072]{2,1,0:T(8,128)(2,1)} async-done(((bf16[4,128,3072]{2,1,0:T(8,128)(2,1)}), bf16[1,128,3072]{2,1,0:T(8,128)(2,1)}) %reduce-scatter.5.cloned.1.call-update) | async-done | bytes 786448 | tf_op jit(solution)/shard_map/reduce_scatter | solution.py:352
  211.4 14.1 %collective-permute-done.26 = bf16[128,1024]{1,0:T(8,128)(2,1)} collective-permute-done((bf16[128,1024]{1,0:T(8,128)(2,1)S(1)}, bf16[128,1024]{1,0:T(8,128)(2,1)}, u32[]{:S(2)}, u32[]{:S(2)}) %collective-permute-start.26) | collective-permute-done | bytes 262176 | tf_op jit(solution)/shard_map/ppermute | solution.py:28
  234.4 5.9 collective-permute-start.30
  252.5 10.8 %collective-permute-done.29 = bf16[4,64,1024]{2,1,0:T(8,128)(2,1)S(1)} collective-permute-done((bf16[4,64,1024]{2,1,0:T(8,128)(2,1)S(1)}, bf16[4,64,1024]{2,1,0:T(8,128)(2,1)S(1)}, u32[]{:S(2)}, u32[]{:S(2)}) %collective-permute-start.29) | collective-permute-done | bytes 524320 | tf_op jit(solution)/shard_map/ppermute | solution.py:36
  289.7 84.4 %collective-permute-done.43 = bf16[4,64,1024]{2,1,0:T(8,128)(2,1)S(1)} collective-permute-done((bf16[4,64,1024]{2,1,0:T(8,128)(2,1)S(1)}, bf16[4,64,1024]{2,1,0:T(8,128)(2,1)S(1)}, u32[]{:S(2)}, u32[]{:S(2)}) %collective-permute-start.43) | collective-permute-done | bytes 524320 | tf_op jit(solution)/shard_map/ppermute | solution.py:36
  374.1 9.2 %collective-permute-done.42 = bf16[4,64,1024]{2,1,0:T(8,128)(2,1)S(1)} collective-permute-done((bf16[4,64,1024]{2,1,0:T(8,128)(2,1)S(1)}, bf16[4,64,1024]{2,1,0:T(8,128)(2,1)S(1)}, u32[]{:S(2)}, u32[]{:S(2)}) %collective-permute-start.42) | collective-permute-done | bytes 524320 | tf_op jit(solution)/shard_map/ppermute | solution.py:36
  392.3 4.8 collective-permute-start.46
  404.3 11.2 %collective-permute-done.46.refs_4_ = bf16[128,1024]{1,0:T(8,128)(2,1)S(1)} collective-permute-done((bf16[128,1024]{1,0:T(8,128)(2,1)S(1)}, bf16[128,1024]{1,0:T(8,128)(2,1)S(1)}, u32[]{:S(2)}, u32[]{:S(2)}) %collective-permute-start.46) | collective-permute-done | bytes 262176 | tf_op jit(solution)/shard_map/ppermute | solution.py:28
  415.6 5.6 attend_back.6
  432.3 50.2 %collective-permute-done.53 = bf16[4,64,1024]{2,1,0:T(8,128)(2,1)S(1)} collective-permute-done((bf16[4,64,1024]{2,1,0:T(8,128)(2,1)S(1)}, bf16[4,64,1024]{2,1,0:T(8,128)(2,1)S(1)}, u32[]{:S(2)}, u32[]{:S(2)}) %collective-permute-start.53) | collective-permute-done | bytes 524320 | tf_op jit(solution)/shard_map/ppermute | solution.py:36
  482.5 9.9 %collective-permute-done.52 = bf16[4,64,1024]{2,1,0:T(8,128)(2,1)S(1)} collective-permute-done((bf16[4,64,1024]{2,1,0:T(8,128)(2,1)S(1)}, bf16[4,64,1024]{2,1,0:T(8,128)(2,1)S(1)}, u32[]{:S(2)}, u32[]{:S(2)}) %collective-permute-start.52) | collective-permute-done | bytes 524320 | tf_op jit(solution)/shard_map/ppermute | solution.py:36
  502.9 4.8 collective-permute-start.56
  511.1 15.3 %collective-permute-done.57.refs_5_ = bf16[128,1024]{1,0:T(8,128)(2,1)S(1)} collective-permute-done((bf16[128,1024]{1,0:T(8,128)(2,1)S(1)}, bf16[128,1024]{1,0:T(8,128)(2,1)S(1)}, u32[]{:S(2)}, u32[]{:S(2)}) %collective-permute-start.57) | collective-permute-done | bytes 262176 | tf_op jit(solution)/shard_map/ppermute | solution.py:28
  531.2 4.8 collective-permute-done.55.refs_3_
  536.0 5.9 attend_back.7
  560.3 7.2 %collective-permute-start.60 = (f32[2,128,128]{2,1,0:T(8,128)S(1)}, f32[2,128,128]{2,1,0:T(8,128)S(1)}, u32[]{:S(2)}, u32[]{:S(2)}) collective-permute-start(f32[2,128,128]{2,1,0:T(8,128)S(1)} %get-tuple-element.84), channel_id=1, source_target_pairs={{0,4},{4,0},{8,12},{12,8},{1,5},{5,1},{9,13},{13,9},{2,6},{6,2},{1... | collective-permute-start | bytes 393224 | tf_op jit(solution)/shard_map/ppermute | solution.py:28
  577.5 14.1 %collective-permute-done.59 = f32[2,128,128]{2,1,0:T(8,128)S(1)} collective-permute-done((f32[2,128,128]{2,1,0:T(8,128)S(1)}, f32[2,128,128]{2,1,0:T(8,128)S(1)}, u32[]{:S(2)}, u32[]{:S(2)}) %collective-permute-start.59) | collective-permute-done | bytes 131104 | tf_op jit(solution)/shard_map/ppermute | solution.py:28
  609.1 10.9 %all-gather.5.cloned.1.call-done.refs_7_ = bf16[512,3072]{1,0:T(8,128)(2,1)} async-done(((bf16[128,3072]{1,0:T(8,128)(2,1)}), bf16[512,3072]{1,0:T(8,128)(2,1)}) %all-gather.5.cloned.1.call-update) | async-done | bytes 3145744 | tf_op jit(solution)/shard_map/all_gather | solution.py:391
  620.0 25.4 %weight_gradient.1 = f32[1024,4,1024]{2,1,0:T(4,128)} custom-call(f32[8]{0:T(128)} %reshape.708.clip, s32[1]{0:T(128)} %bitcast.132.info, bf16[512,1024]{1,0:T(8,128)(2,1)} %get-tuple-element.98.refs_0_, bf16[512,1024]{1,0:T(8,128)(2,1)} %get-tuple-element.27.refs_1_, bf16[512,1024]{1,0:T(8,128)(2,1)} %get-tuple-element.97.refs_2_, ...), custom_call_target="tpu_custom_call" | custom-call | flops 8589934592 | bytes 41943040 | tf_op jit(solution)/shard_map/weight_gradient/pallas_call | solution.py:284
  (387 shorter events, 225.7 us)
Async XLA Ops:
  7.2 106.1 %reduce-scatter.3.cloned.1.call-start = ((), (), s32[]{:S(2)}) async-start(), calls=%async_computation.2 | async-start | bytes 3932160 | tf_op jit(solution)/shard_map/reduce_scatter | solution.py:352
  17.0 22.4 %collective-permute-start.17 = (bf16[1,64,1024]{2,1,0:T(8,128)(2,1)}, bf16[1,64,1024]{2,1,0:T(8,128)(2,1)}, u32[]{:S(2)}, u32[]{:S(2)}) collective-permute-start(bf16[1,64,1024]{2,1,0:T(8,128)(2,1)} %get-tuple-element.70), channel_id=1, source_target_pairs={{0,4},{4,0},{8,12},{12,8},{16,20},{20,16},{24,28},{28,24},{1,5},{5... | collective-permute-start | bytes 393224 | tf_op jit(solution)/shard_map/ppermute | solution.py:28
  53.1 142.4 %reduce-scatter.5.cloned.1.call-start = ((), (), s32[]{:S(2)}) async-start(), calls=%async_computation.3 | async-start | bytes 3932160 | tf_op jit(solution)/shard_map/reduce_scatter | solution.py:352
  75.1 534.0 %all-gather.3.cloned.1.call-start = ((), (), s32[]{:S(2)}) async-start(), calls=%async_computation.4 | async-start | bytes 3932160 | tf_op jit(solution)/shard_map/all_gather | solution.py:391
  120.1 23.7 %collective-permute-start.8 = (bf16[128,1024]{1,0:T(8,128)(2,1)S(1)}, bf16[128,1024]{1,0:T(8,128)(2,1)S(1)}, u32[]{:S(2)}, u32[]{:S(2)}) collective-permute-start(bf16[128,1024]{1,0:T(8,128)(2,1)S(1)} %attend.2), channel_id=1, source_target_pairs={{0,8},{4,12},{8,0},{12,4},{1,9},{5,13},{9,1},{13,5},{2,10},{6,14},... | collective-permute-start | bytes 786440 | tf_op jit(solution)/shard_map/ppermute | solution.py:28
  148.2 60.2 %collective-permute-start.10 = (bf16[4,64,1024]{2,1,0:T(8,128)(2,1)}, bf16[4,64,1024]{2,1,0:T(8,128)(2,1)S(1)}, u32[]{:S(2)}, u32[]{:S(2)}) collective-permute-start(bf16[4,64,1024]{2,1,0:T(8,128)(2,1)} %constant_dynamic-slice_fusion.31), channel_id=1, source_target_pairs={{0,1},{1,0},{2,3},{3,2},{4,5},{5,4},{6,7},{7,6},{8,9},{9,8},{10,11... | collective-permute-start | bytes 1572872 | tf_op jit(solution)/shard_map/ppermute | solution.py:36
  202.8 22.6 %collective-permute-start.26 = (bf16[128,1024]{1,0:T(8,128)(2,1)S(1)}, bf16[128,1024]{1,0:T(8,128)(2,1)}, u32[]{:S(2)}, u32[]{:S(2)}) collective-permute-start(bf16[128,1024]{1,0:T(8,128)(2,1)S(1)} %attend.3), channel_id=1, source_target_pairs={{0,8},{4,12},{8,0},{12,4},{1,9},{5,13},{9,1},{13,5},{2,10},{6,14},... | collective-permute-start | bytes 786440 | tf_op jit(solution)/shard_map/ppermute | solution.py:28
  208.7 23.5 %collective-permute-start.12 = (bf16[4,64,1024]{2,1,0:T(8,128)(2,1)S(1)}, bf16[4,64,1024]{2,1,0:T(8,128)(2,1)S(1)}, u32[]{:S(2)}, u32[]{:S(2)}) collective-permute-start(bf16[4,64,1024]{2,1,0:T(8,128)(2,1)S(1)} %add_convert_fusion.9), channel_id=1, source_target_pairs={{0,18},{1,19},{2,16},{3,17},{4,22},{5,23},{6,20},{7,21},{8,26},{9,... | collective-permute-start | bytes 1572872 | tf_op jit(solution)/shard_map/ppermute | solution.py:36
  240.3 23.0 %collective-permute-start.29 = (bf16[4,64,1024]{2,1,0:T(8,128)(2,1)S(1)}, bf16[4,64,1024]{2,1,0:T(8,128)(2,1)S(1)}, u32[]{:S(2)}, u32[]{:S(2)}) collective-permute-start(bf16[4,64,1024]{2,1,0:T(8,128)(2,1)S(1)} %add_convert_fusion.7), channel_id=1, source_target_pairs={{0,16},{1,17},{2,18},{3,19},{4,20},{5,21},{6,22},{7,23},{8,24},{9,... | collective-permute-start | bytes 1572872 | tf_op jit(solution)/shard_map/ppermute | solution.py:36
  283.7 90.4 %collective-permute-start.43 = (bf16[4,64,1024]{2,1,0:T(8,128)(2,1)S(1)}, bf16[4,64,1024]{2,1,0:T(8,128)(2,1)S(1)}, u32[]{:S(2)}, u32[]{:S(2)}) collective-permute-start(bf16[4,64,1024]{2,1,0:T(8,128)(2,1)S(1)} %add_convert_fusion.5), channel_id=1, source_target_pairs={{16,2},{17,3},{18,0},{19,1},{20,6},{21,7},{22,4},{23,5},{24,10},{2... | collective-permute-start | bytes 1572872 | tf_op jit(solution)/shard_map/ppermute | solution.py:36
  285.0 98.3 %collective-permute-start.42 = (bf16[4,64,1024]{2,1,0:T(8,128)(2,1)S(1)}, bf16[4,64,1024]{2,1,0:T(8,128)(2,1)S(1)}, u32[]{:S(2)}, u32[]{:S(2)}) collective-permute-start(bf16[4,64,1024]{2,1,0:T(8,128)(2,1)S(1)} %add_convert_fusion.5), channel_id=1, source_target_pairs={{16,0},{17,1},{18,2},{19,3},{20,4},{21,5},{22,6},{23,7},{24,8},{25... | collective-permute-start | bytes 1572872 | tf_op jit(solution)/shard_map/ppermute | solution.py:36
  287.6 98.1 %collective-permute-start.50 = (bf16[128,2048]{1,0:T(8,128)(2,1)S(1)}, bf16[128,2048]{1,0:T(8,128)(2,1)S(1)}, u32[]{:S(2)}, u32[]{:S(2)}) collective-permute-start(bf16[128,2048]{1,0:T(8,128)(2,1)S(1)} %get-tuple-element.16), channel_id=1, source_target_pairs={{16,28},{20,24},{24,20},{28,16},{17,29},{21,25},{25,21},{29,17},{1... | collective-permute-start | bytes 1572872 | tf_op jit(solution)/shard_map/ppermute | solution.py:28
  288.3 97.4 %collective-permute-start.49 = (bf16[128,2048]{1,0:T(8,128)(2,1)S(1)}, bf16[128,2048]{1,0:T(8,128)(2,1)S(1)}, u32[]{:S(2)}, u32[]{:S(2)}) collective-permute-start(bf16[128,2048]{1,0:T(8,128)(2,1)S(1)} %get-tuple-element.16), channel_id=1, source_target_pairs={{16,24},{20,28},{24,16},{28,20},{17,25},{21,29},{25,17},{29,21},{1... | collective-permute-start | bytes 1572872 | tf_op jit(solution)/shard_map/ppermute | solution.py:28
  289.0 96.7 %collective-permute-start.48 = (bf16[128,2048]{1,0:T(8,128)(2,1)S(1)}, bf16[128,2048]{1,0:T(8,128)(2,1)S(1)}, u32[]{:S(2)}, u32[]{:S(2)}) collective-permute-start(bf16[128,2048]{1,0:T(8,128)(2,1)S(1)} %get-tuple-element.16), channel_id=1, source_target_pairs={{16,20},{20,16},{24,28},{28,24},{17,21},{21,17},{25,29},{29,25},{1... | collective-permute-start | bytes 1572872 | tf_op jit(solution)/shard_map/ppermute | solution.py:28
  392.3 23.2 %collective-permute-start.46 = (bf16[128,1024]{1,0:T(8,128)(2,1)S(1)}, bf16[128,1024]{1,0:T(8,128)(2,1)S(1)}, u32[]{:S(2)}, u32[]{:S(2)}) collective-permute-start(bf16[128,1024]{1,0:T(8,128)(2,1)S(1)} %get-tuple-element.60), channel_id=1, source_target_pairs={{0,8},{4,12},{8,0},{12,4},{1,9},{5,13},{9,1},{13,5},{2,10},{6,14},... | collective-permute-start | bytes 786440 | tf_op jit(solution)/shard_map/ppermute | solution.py:28
  422.2 197.8 %all-gather.5.cloned.1.call-start = ((), (), s32[]{:S(2)}) async-start(), calls=%async_computation.5 | async-start | bytes 3932160 | tf_op jit(solution)/shard_map/all_gather | solution.py:391
  429.7 52.8 %collective-permute-start.53 = (bf16[4,64,1024]{2,1,0:T(8,128)(2,1)S(1)}, bf16[4,64,1024]{2,1,0:T(8,128)(2,1)S(1)}, u32[]{:S(2)}, u32[]{:S(2)}) collective-permute-start(bf16[4,64,1024]{2,1,0:T(8,128)(2,1)S(1)} %add_convert_fusion.3), channel_id=1, source_target_pairs={{16,2},{17,3},{18,0},{19,1},{20,6},{21,7},{22,4},{23,5},{24,10},{2... | collective-permute-start | bytes 1572872 | tf_op jit(solution)/shard_map/ppermute | solution.py:36
  431.0 61.3 %collective-permute-start.52 = (bf16[4,64,1024]{2,1,0:T(8,128)(2,1)S(1)}, bf16[4,64,1024]{2,1,0:T(8,128)(2,1)S(1)}, u32[]{:S(2)}, u32[]{:S(2)}) collective-permute-start(bf16[4,64,1024]{2,1,0:T(8,128)(2,1)S(1)} %add_convert_fusion.3), channel_id=1, source_target_pairs={{16,0},{17,1},{18,2},{19,3},{20,4},{21,5},{22,6},{23,7},{24,8},{25... | collective-permute-start | bytes 1572872 | tf_op jit(solution)/shard_map/ppermute | solution.py:36
  501.0 25.5 %collective-permute-start.57 = (bf16[128,1024]{1,0:T(8,128)(2,1)S(1)}, bf16[128,1024]{1,0:T(8,128)(2,1)S(1)}, u32[]{:S(2)}, u32[]{:S(2)}) collective-permute-start(bf16[128,1024]{1,0:T(8,128)(2,1)S(1)} %get-tuple-element.55), channel_id=1, source_target_pairs={{0,4},{4,0},{8,12},{12,8},{1,5},{5,1},{9,13},{13,9},{2,6},{6,2},{1... | collective-permute-start | bytes 786440 | tf_op jit(solution)/shard_map/ppermute | solution.py:28
  502.9 28.3 %collective-permute-start.56 = (bf16[128,1024]{1,0:T(8,128)(2,1)S(1)}, bf16[128,1024]{1,0:T(8,128)(2,1)S(1)}, u32[]{:S(2)}, u32[]{:S(2)}) collective-permute-start(bf16[128,1024]{1,0:T(8,128)(2,1)S(1)} %get-tuple-element.56), channel_id=1, source_target_pairs={{0,8},{4,12},{8,0},{12,4},{1,9},{5,13},{9,1},{13,5},{2,10},{6,14},... | collective-permute-start | bytes 786440 | tf_op jit(solution)/shard_map/ppermute | solution.py:28
  507.7 28.3 %collective-permute-start.55 = (bf16[128,1024]{1,0:T(8,128)(2,1)S(1)}, bf16[128,1024]{1,0:T(8,128)(2,1)S(1)}, u32[]{:S(2)}, u32[]{:S(2)}) collective-permute-start(bf16[128,1024]{1,0:T(8,128)(2,1)S(1)} %get-tuple-element.57), channel_id=1, source_target_pairs={{0,12},{4,8},{8,4},{12,0},{1,13},{5,9},{9,5},{13,1},{2,14},{6,10},... | collective-permute-start | bytes 786440 | tf_op jit(solution)/shard_map/ppermute | solution.py:28
  554.4 38.6 %collective-permute-start.35 = (f32[2,128,128]{2,1,0:T(8,128)S(1)}, f32[2,128,128]{2,1,0:T(8,128)S(1)}, u32[]{:S(2)}, u32[]{:S(2)}) collective-permute-start(f32[2,128,128]{2,1,0:T(8,128)S(1)} %get-tuple-element.86), channel_id=1, source_target_pairs={{16,28},{20,24},{24,20},{28,16},{17,29},{21,25},{25,21},{29,17},{1... | collective-permute-start | bytes 393224 | tf_op jit(solution)/shard_map/ppermute | solution.py:28
  555.2 37.8 %collective-permute-start.37 = (f32[2,128,128]{2,1,0:T(8,128)S(1)}, f32[2,128,128]{2,1,0:T(8,128)S(1)}, u32[]{:S(2)}, u32[]{:S(2)}) collective-permute-start(f32[2,128,128]{2,1,0:T(8,128)S(1)} %get-tuple-element.87), channel_id=1, source_target_pairs={{16,20},{20,16},{24,28},{28,24},{17,21},{21,17},{25,29},{29,25},{1... | collective-permute-start | bytes 393224 | tf_op jit(solution)/shard_map/ppermute | solution.py:28
  567.5 24.1 %collective-permute-start.59 = (f32[2,128,128]{2,1,0:T(8,128)S(1)}, f32[2,128,128]{2,1,0:T(8,128)S(1)}, u32[]{:S(2)}, u32[]{:S(2)}) collective-permute-start(f32[2,128,128]{2,1,0:T(8,128)S(1)} %get-tuple-element.85), channel_id=1, source_target_pairs={{0,8},{4,12},{8,0},{12,4},{1,9},{5,13},{9,1},{13,5},{2,10},{6,14},... | collective-permute-start | bytes 393224 | tf_op jit(solution)/shard_map/ppermute | solution.py:28
  (118 other events, 1054.2 us)
Sparse Core Ops, SparseCore 0:
  53.2 60.0 reduce-scatter.2
  115.6 79.8 reduce-scatter.4
  422.3 107.5 all-gather.2
  543.0 76.8 all-gather.4

commit v2 on v1

--- a/solution.py
+++ b/solution.py
@@ -80,7 +80,7 @@
     return in_order([mine[0]] + [got[s] for s in range(1, n)])
 
 
-def relay(terms, residual, source):
+def relay(terms, residual, sources, giver, targets):
     groups = lax.axis_size("mp") // 2
     index = lax.axis_index("mp")
     parity = index % 2
@@ -88,13 +88,15 @@
     low = terms.astype(BF16)
     keep = lax.dynamic_slice_in_dim(low, parity * half, half, 1)
     give = lax.dynamic_slice_in_dim(low, (1 - parity) * half, half, 1)
-    total = keep.astype(F32) + mp_shift(give, 1, (source,)).astype(F32)
+    total = keep.astype(F32) + mp_shift(give, 1, sources).astype(F32)
     if residual is not None:
         total = total + jnp.where(index < 2, residual.astype(F32), 0.0)
     total = total.astype(BF16)
-    got = [mp_shift(total, 2 * g, (source,), flip=True).astype(F32) for g in range(groups)]
-    mine = functools.reduce(jnp.add, got).astype(BF16)
-    other = mp_shift(mine, 1, (1 - source,))
+    got = [mp_shift(total, 2 * g, (giver,), flip=True) for g in range(groups - 1, -1, -1)]
+    got += [mp_shift(total, 2 * g, (0,)) for g in range(1, groups)]
+    own = jnp.where(lax.axis_index("section") == 0, total.astype(F32), 0.0)
+    mine = functools.reduce(jnp.add, [g.astype(F32) for g in got], own).astype(BF16)
+    other = mp_shift(mine, 1, targets)
     return halves(mine, other, parity)
 
 
@@ -147,9 +149,8 @@
 
 def full_kernel(plan, count, decoder, info, *refs):
     qs, ks, vs, gs = bind(plan, refs)
-    kv_ref, send_ref, gram_ref = refs[count:]
-    seq = kv_ref.shape[0]
-    width = kv_ref.shape[1] // 2
+    gk_ref, gv_ref, send_ref, gram_ref = refs[count:]
+    seq, width = gk_ref.shape
 
     @pl.when(info[0] == 1)
     def run():
@@ -175,11 +176,10 @@
             gk = jnp.where(first, gk[:seq], gk[seq:]).astype(BF16)
             gv = mm(low, g, TN)
             gv = jnp.where(first, gv[:seq], gv[seq:]).astype(BF16)
-            kv_ref[:, c : c + PAIR] = gk
-            kv_ref[:, width + c : width + c + PAIR] = gv
+            gk_ref[:, c : c + PAIR] = gk
+            gv_ref[:, c : c + PAIR] = gv
             send_ref[:, c : c + PAIR] = gq
             send_ref[:, width + c : width + c + PAIR] = ctx if decoder else gk
-            send_ref[:, 2 * width + c : 2 * width + c + PAIR] = gv
             grams[0] += mm(gq, gq, NT)
             grams[1] += mm(gk, gk, NT) + mm(gv, gv, NT)
             grams[2] += mm(ctx, ctx, NT)
@@ -187,7 +187,7 @@
             gram_ref[i] = grams[i]
 
 
-def call_attention(kernel, info, operands, outs, flops, name):
+def call_attention(kernel, info, operands, outs, flops, name, after=()):
     arrays, plan = [], []
     for sources in operands:
         plan.append([])
@@ -198,40 +198,45 @@
             plan[-1].append((known[0] if known else len(arrays) - 1, offset))
     vmem = pl.BlockSpec(memory_space=pltpu.VMEM)
     return pl.pallas_call(
-        functools.partial(kernel, plan, len(arrays)),
+        functools.partial(kernel, plan, len(arrays) + len(after)),
         out_shape=outs,
-        in_specs=[pl.BlockSpec(memory_space=pltpu.SMEM)] + [vmem] * len(arrays),
+        in_specs=[pl.BlockSpec(memory_space=pltpu.SMEM)]
+        + [vmem] * len(arrays)
+        + [pl.BlockSpec(memory_space=pl.ANY)] * len(after),
         out_specs=(vmem,) * len(outs),
         compiler_params=pltpu.CompilerParams(vmem_limit_bytes=32 << 20),
         cost_estimate=pl.CostEstimate(
             flops=flops, bytes_accessed=sum(2 * a.size for a in arrays), transcendentals=0
         ),
         name=name,
-    )(info, *arrays)
-
-
-def attend(info, operands, seq, width):
+    )(info, *arrays, *after)
+
+
+def attend(info, operands, seq, width, after):
     rows = jax.ShapeDtypeStruct((seq, width), BF16)
-    return call_attention(fwd_kernel, info, operands, (rows,), 8 * seq * seq * width, "attend")[0]
-
-
-def attend_back(info, operands, seq, width, decoder):
+    flops = 8 * seq * seq * width
+    return call_attention(fwd_kernel, info, operands, (rows,), flops, "attend", after)[0]
+
+
+def attend_back(info, operands, seq, width, decoder, after=()):
     outs = (
+        jax.ShapeDtypeStruct((seq, width), BF16),
+        jax.ShapeDtypeStruct((seq, width), BF16),
         jax.ShapeDtypeStruct((seq, 2 * width), BF16),
-        jax.ShapeDtypeStruct((seq, 3 * width), BF16),
         jax.ShapeDtypeStruct((3, seq, seq), F32),
     )
 
     def kernel(plan, count, *refs):
         full_kernel(plan, count, decoder, *refs)
 
-    return call_attention(kernel, info, operands, outs, 40 * seq * seq * width, "attend_back")
+    flops = 40 * seq * seq * width
+    return call_attention(kernel, info, operands, outs, flops, "attend_back", after)
 
 
 def wgrad_kernel(mb, chunk, scale, clip, info, *refs):
     x1, xa, xb = refs[:mb], refs[mb : 2 * mb], refs[2 * mb : 3 * mb]
-    send, swap = refs[3 * mb : 4 * mb], refs[4 * mb : 5 * mb]
-    noise, out = refs[5 * mb :]
+    send, kept, back = (refs[i * mb : (i + 1) * mb] for i in (3, 4, 5))
+    noise, out = refs[6 * mb :]
     width = out.shape[2]
     count = x1[0].shape[0] // chunk
     is_dec = info[0] == 1
@@ -259,27 +264,27 @@
 
     @pl.when(is_dec)
     def decoder():
-        put(1, lb, swap, 0)
-        put(2, lb, send, 2 * width)
+        put(1, lb, back, 0)
+        put(2, lb, kept, 0)
         put(3, la, send, width)
 
     @pl.when(jnp.logical_not(is_dec))
     def encoder():
         put(1, la, send, width)
-        put(2, l1, send, 2 * width)
-        put(3, lb, swap, 0)
-
-
-def wgrad(clip, info, x1, xa, xb, send, swap, noise, chunk, examples):
+        put(2, l1, back, 0)
+        put(3, lb, kept, 0)
+
+
+def wgrad(clip, info, x1, xa, xb, send, kept, back, noise, chunk, examples):
     mb = len(x1)
     tokens, depth = x1[0].shape
     width = noise.shape[2]
-    block = 128
+    block = 256
     smem = pl.BlockSpec(memory_space=pltpu.SMEM)
     left = pl.BlockSpec((tokens, block), lambda i: (0, i))
     wide = pl.BlockSpec((block, 4, width), lambda i: (i, 0, 0))
     once = [
-        pl.BlockSpec(y.shape, lambda i: (0, 0), pipeline_mode=pl.Buffered(1)) for y in send + swap
+        pl.BlockSpec(y.shape, lambda i: (0, 0), pipeline_mode=pl.Buffered(1)) for y in send + kept + back
     ]
     return pl.pallas_call(
         functools.partial(wgrad_kernel, mb, chunk, 1.0 / examples),
@@ -294,7 +299,7 @@
             transcendentals=0,
         ),
         name="weight_gradient",
-    )(clip, info, *x1, *xa, *xb, *send, *swap, noise)
+    )(clip, info, *x1, *xa, *xb, *send, *kept, *back, noise)
 
 
 def per_device(inputs, norm_gains, weights, cotangent, lengths, dp_noise):
@@ -315,9 +320,9 @@
     def rows_of(x):
         return x.reshape(n * seq, x.shape[-1])
 
-    def owner_gram(x, sections):
+    def owner_grams(x, sections):
         terms = jnp.einsum("bntd,bnud->nbtu", x, x, preferred_element_type=F32)
-        return functools.reduce(jnp.add, to_owner(terms, sections))
+        return to_owner(terms, sections)
 
     def info(flag, b):
         return jnp.stack([flag.astype(jnp.int32), lengths[0, b]])
@@ -353,44 +358,50 @@
                 parts.reshape(n, seq, 3 * inner), "dp", scatter_dimension=0, tiled=False
             )
         )
-    ctx_all, enc_out = [], []
+    w_relay = jnp.where(is_dec, w[2], mp_shift(w[1], 0, dec, flip=True))
+    ctx_all, enc_out, kv_parts = [], [], []
     for b in range(mb):
         qkv = [[(first[b], i * inner)] for i in range(3)]
-        ctx = attend(info(section == 0, b), qkv, seq, inner)
+        after = [kv_parts[-1][1]] if b else []
+        ctx = attend(info(section == 0, b), qkv, seq, inner, after)
         ctx_all.append(rows_of(gather(ctx, enc)))
         terms = mm(ctx_all[b], w[3], NT).reshape(n, seq, depth)
-        enc_out.append(relay(terms, raw_half[b], 0))
-    gk_all, grad_enc, dec_send, dec_gram = [], [], [], []
+        enc_out.append(relay(terms, raw_half[b], enc, 0, both))
+        terms = mm(rows_of(enc_out[b]), w_relay).astype(BF16).reshape(n, seq, inner)
+        kv_parts.append(to_owner(terms, both))
+    relay_all, grad_enc, dec_send, dec_gram = [], [], [], []
     for b in range(mb):
-        rows = rows_of(enc_out[b])
-        parts = [mm(rows, w[s]).astype(BF16) for s in (1, 2)]
-        kv = to_owner(jnp.concatenate(parts, axis=1).reshape(n, seq, 2 * inner), dec)
+        parts = kv_parts[b]
+        k = functools.reduce(jnp.add, [part.astype(F32) for part in parts]).astype(BF16)
         operands = [
             [(first[b], 0)],
-            [(part, 0) for part in kv],
-            [(part, inner) for part in kv],
+            [(mp_shift(k, 0, enc, flip=True), 0)],
+            [(part, 0) for part in parts],
             [(first[mb - 1], (1 + b) * inner)],
         ]
-        gkv, send, gram = attend_back(info(section == 1, b), operands, seq, inner, True)
-        gkv_all = rows_of(gather(gkv, dec))
-        terms = mm(gkv_all[:, :inner], w[1], NT) + mm(gkv_all[:, inner:], w[2], NT)
-        grad_enc.append(relay(terms.reshape(n, seq, depth), None, 1))
-        gk_all.append(gkv_all[:, :inner])
+        gk, gv, send, gram = attend_back(info(section == 1, b), operands, seq, inner, True)
+        rows = jnp.where(is_dec, gv, mp_shift(gk, 0, dec, flip=True))
+        relay_all.append(rows_of(gather(rows, both)))
+        terms = mm(relay_all[b], w_relay, NT).reshape(n, seq, depth)
+        grad_enc.append(relay(terms, None, both, 1, enc))
         dec_send.append(send)
         dec_gram.append(gram)
-    gram_enc_out = owner_gram(jnp.stack(enc_out), dec)
-    enc_send, enc_gram = [], []
+    gram_enc_out = functools.reduce(jnp.add, owner_grams(jnp.stack(enc_out), dec))
+    grad_grams = owner_grams(jnp.stack(grad_enc), enc)
+    gram_grad_enc = functools.reduce(jnp.add, grad_grams)
+    send_all, enc_gram, back_all = [], [], []
     for b in range(mb):
         gctx = to_owner(mm(rows_of(grad_enc[b]), w[3]).astype(BF16).reshape(n, seq, inner), enc)
         operands = [[(first[b], i * inner)] for i in range(3)] + [[(part, 0) for part in gctx]]
-        unused, send, gram = attend_back(info(section == 0, b), operands, seq, inner, False)
-        enc_send.append(send)
+        after = grad_grams[1:] if b == mb - 1 else []
+        _, gv, send, gram = attend_back(
+            info(section == 0, b), operands, seq, inner, False, after
+        )
         enc_gram.append(gram)
-    gram_grad_enc = owner_gram(jnp.stack(grad_enc), enc)
-    send_all = [
-        lax.all_gather(jnp.where(is_dec, d, e), "dp", axis=0, tiled=True)
-        for d, e in zip(dec_send, enc_send)
-    ]
+        send = jnp.where(is_dec, dec_send[b], send)
+        send_all.append(lax.all_gather(send, "dp", axis=0, tiled=True))
+        gv_all = rows_of(gather(mp_shift(gv, 0, enc, flip=True), dec))
+        back_all.append(mp_shift(jnp.where(is_dec, gv_all, relay_all[b]), 0, both, flip=True))
     normed = (own32 * inv[..., None] * gain).astype(BF16)
     gram_x = jnp.einsum("btd,bud->btu", normed, normed, preferred_element_type=F32)
     gram_cot = jnp.einsum("btd,bud->btu", cot, cot, preferred_element_type=F32)
@@ -408,9 +419,9 @@
     clip_all = gather(clip, both).T.reshape(-1)
     xa = [jnp.where(is_dec, c, r) for c, r in zip(cot_cols, x)]
     xb = [rows_of(jnp.where(is_dec, o, g)) for o, g in zip(enc_out, grad_enc)]
-    swap = [jnp.where(is_dec, k, c) for k, c in zip(gk_all, ctx_all)]
+    kept = [jnp.where(is_dec, r, c) for r, c in zip(relay_all, ctx_all)]
     flag = section.astype(jnp.int32)[None]
-    out = wgrad(clip_all, flag, x, xa, xb, send_all, swap, dp_noise[0], seq, mb * n)
+    out = wgrad(clip_all, flag, x, xa, xb, send_all, kept, back_all, dp_noise[0], seq, mb * n)
     return (out[None], clip)
 
 

time: 661 us -> 667 us (level)
  waiting for transfers between devices: 361 us -> 255 us
  starting transfers between devices: 122 us -> 226 us
    ppermute x22 -> x35, starting transfers between devices: 31 us -> 95.6 us  [mp_shift(): return lax.ppermute(x, ('section', 'mp'), pairs)]
    ppermute x22 -> x35, waiting for transfers between devices: 179 us -> 117 us  [mp_shift(): return lax.ppermute(x, ('section', 'mp'), pairs)]
    reduce_scatter x2, waiting for transfers between devices: 81.5 us -> 31.6 us  [per_device(): lax.psum_scatter(parts.reshape(n, seq, 3 * inner), 'dp', scatter_dimensio...]
    ppermute x45 -> x51, starting transfers between devices: 90.6 us -> 131 us  [dp_shift(): return lax.ppermute(x, ('section', 'dp'), pairs)]
    ppermute x45 -> x51, waiting for transfers between devices: 90 us -> 106 us  [dp_shift(): return lax.ppermute(x, ('section', 'dp'), pairs)]
    all_gather x2, waiting for transfers between devices: 10.9 us -> 0.02 us  [per_device(): send_all.append(lax.all_gather(send, 'dp', axis=0, tiled=True))]
    dot_general x18 -> x14, matrix products: 36 us -> 31.3 us  [mm(): return lax.dot_general(left, right, dims, preferred_element_type=F32)]
    unnamed x143 -> x173, local copies, waits for them, and re-layouts: 16.3 us -> 19.2 us
  transfers between devices with their start and end apart: 71 -> 90, of which waited for: 31 -> 38; matrix products, arithmetic and copies ran while one was open for 13% -> 15% of each run, Pallas kernels for 2% -> 2%
where the time goes in v2:
time: 667 us; the launch traced here: 658 us
  waiting for transfers between devices  255 us (38%)
  starting transfers between devices  226 us (34%)
  other arithmetic  50 us (7%)
  Pallas kernels  40.1 us (6%)
  matrix products  37.1 us (6%)
  local copies, waits for them, and re-layouts  32.5 us (5%)
  between operations  16.5 us (2%)
    ppermute x51, starting transfers between devices, dp_shift(): return lax.ppermute(x, ('section', 'dp'), pairs)  131 us
    ppermute x35, waiting for transfers between devices, mp_shift(): return lax.ppermute(x, ('section', 'mp'), pairs)  117 us
    ppermute x51, waiting for transfers between devices, dp_shift(): return lax.ppermute(x, ('section', 'dp'), pairs)  106 us
    ppermute x35, starting transfers between devices, mp_shift(): return lax.ppermute(x, ('section', 'mp'), pairs)  95.6 us
    reduce_scatter x2, waiting for transfers between devices, per_device(): lax.psum_scatter(parts.reshape(n, seq, 3 * inner), 'dp', scatter_dimensio...  31.6 us
    dot_general x14, matrix products, mm(): return lax.dot_general(left, right, dims, preferred_element_type=F32)  31.3 us
    pallas_call x1, Pallas kernels, wgrad(): pl.pallas_call(functools.partial(wgrad_kernel, mb, chunk, 1.0 / examples)...  24 us
    unnamed x173, local copies, waits for them, and re-layouts  19.2 us
  transfers between devices with their start and end apart: 90, of which 38 were waited for; matrix products, arithmetic and copies ran while one was open for 15% of the time, Pallas kernels for 2%

profile of v2, /device:TPU:0, one launch (start us, length us, event | category | flops | bytes accessed | tf_op | source)
XLA Modules:
  0.0 657.5 jit_solution(14095530862154416473)
XLA Ops:
  27.6 9.7 %copy.30 = bf16[1,1024,4,1024]{3,1,2,0:T(8,128)(2,1)} copy(bf16[1,1024,4,1024]{3,2,1,0:T(4,128)(2,1)} %param.8) | data formatting | bytes 16777216 | tf_op args[2]
  81.6 31.6 %reduce-scatter.3.cloned.1.call-done = bf16[1,128,3072]{2,1,0:T(8,128)(2,1)} async-done(((bf16[4,128,3072]{2,1,0:T(8,128)(2,1)}), bf16[1,128,3072]{2,1,0:T(8,128)(2,1)}) %reduce-scatter.3.cloned.1.call-update) | async-done | bytes 786448 | tf_op jit(solution)/shard_map/reduce_scatter | solution.py:357
  130.6 13.1 %collective-permute-done.8 = bf16[128,1024]{1,0:T(8,128)(2,1)S(1)} collective-permute-done((bf16[128,1024]{1,0:T(8,128)(2,1)S(1)}, bf16[128,1024]{1,0:T(8,128)(2,1)S(1)}, u32[]{:S(2)}, u32[]{:S(2)}) %collective-permute-start.8) | collective-permute-done | bytes 262176 | tf_op jit(solution)/shard_map/ppermute | solution.py:28
  159.8 9.8 %collective-permute-done.13 = bf16[4,64,1024]{2,1,0:T(8,128)(2,1)S(1)} collective-permute-done((bf16[4,64,1024]{2,1,0:T(8,128)(2,1)S(1)}, bf16[4,64,1024]{2,1,0:T(8,128)(2,1)S(1)}, u32[]{:S(2)}, u32[]{:S(2)}) %collective-permute-start.13) | collective-permute-done | bytes 524320 | tf_op jit(solution)/shard_map/ppermute | solution.py:36
  170.7 10.4 %collective-permute-done.11 = bf16[4,64,1024]{2,1,0:T(8,128)(2,1)S(1)} collective-permute-done((bf16[4,64,1024]{2,1,0:T(8,128)(2,1)S(1)}, bf16[4,64,1024]{2,1,0:T(8,128)(2,1)S(1)}, u32[]{:S(2)}, u32[]{:S(2)}) %collective-permute-start.11) | collective-permute-done | bytes 524320 | tf_op jit(solution)/shard_map/ppermute | solution.py:36
  181.6 7.1 %collective-permute-done.15 = bf16[1024,1024]{1,0:T(8,128)(2,1)} collective-permute-done((bf16[1024,1024]{1,0:T(8,128)(2,1)}, bf16[1024,1024]{1,0:T(8,128)(2,1)}, u32[]{:S(2)}, u32[]{:S(2)}) %collective-permute-start.15) | collective-permute-done | bytes 2097184 | tf_op jit(solution)/shard_map/ppermute | solution.py:36
  198.3 5.9 collective-permute-done.16.refs_4_.refs_1_
  211.2 19.8 %collective-permute-start.29 = (bf16[128,1024]{1,0:T(8,128)(2,1)S(1)}, bf16[128,1024]{1,0:T(8,128)(2,1)S(1)}, u32[]{:S(2)}, u32[]{:S(2)}) collective-permute-start(bf16[128,1024]{1,0:T(8,128)(2,1)S(1)} %attend.3), channel_id=1, source_target_pairs={{0,8},{4,12},{8,0},{12,4},{1,9},{5,13},{9,1},{13,5},{2,10},{6,14},... | collective-permute-start | bytes 786440 | tf_op jit(solution)/shard_map/ppermute | solution.py:28
  249.8 9.3 %collective-permute-done.43 = bf16[128,1024]{1,0:T(8,128)(2,1)S(1)} collective-permute-done((bf16[128,1024]{1,0:T(8,128)(2,1)S(1)}, bf16[128,1024]{1,0:T(8,128)(2,1)S(1)}, u32[]{:S(2)}, u32[]{:S(2)}) %collective-permute-start.43) | collective-permute-done | bytes 262176 | tf_op jit(solution)/shard_map/ppermute | solution.py:36
  269.1 10.2 %collective-permute-start.44 = (bf16[128,1024]{1,0:T(8,128)(2,1)S(1)}, bf16[128,1024]{1,0:T(8,128)(2,1)S(1)}, u32[]{:S(2)}, u32[]{:S(2)}) collective-permute-start(bf16[128,1024]{1,0:T(8,128)(2,1)S(1)} %broadcast_select_fusion.9), channel_id=1, source_target_pairs={{0,4},{4,0},{8,12},{12,8},{16,20},{20,16},{24,28},{28,24},{1,5},{5... | collective-permute-start | bytes 786440 | tf_op jit(solution)/shard_map/ppermute | solution.py:28
  306.4 6.9 %collective-permute-done.38.refs_6_ = bf16[128,1024]{1,0:T(8,128)(2,1)S(1)} collective-permute-done((bf16[128,1024]{1,0:T(8,128)(2,1)S(1)}, bf16[128,1024]{1,0:T(8,128)(2,1)S(1)}, u32[]{:S(2)}, u32[]{:S(2)}) %collective-permute-start.38) | collective-permute-done | bytes 262176 | tf_op jit(solution)/shard_map/ppermute | solution.py:28
  330.7 8.9 %collective-permute-done.55 = bf16[128,1024]{1,0:T(8,128)(2,1)S(1)} collective-permute-done((bf16[128,1024]{1,0:T(8,128)(2,1)S(1)}, bf16[128,1024]{1,0:T(8,128)(2,1)S(1)}, u32[]{:S(2)}, u32[]{:S(2)}) %collective-permute-start.55) | collective-permute-done | bytes 262176 | tf_op jit(solution)/shard_map/ppermute | solution.py:36
  344.6 6.2 collective-permute-done.58
  350.8 11.4 %collective-permute-done.57 = bf16[128,1024]{1,0:T(8,128)(2,1)S(1)} collective-permute-done((bf16[128,1024]{1,0:T(8,128)(2,1)S(1)}, bf16[128,1024]{1,0:T(8,128)(2,1)S(1)}, u32[]{:S(2)}, u32[]{:S(2)}) %collective-permute-start.57) | collective-permute-done | bytes 262176 | tf_op jit(solution)/shard_map/ppermute | solution.py:28
  380.0 12.1 %collective-permute-done.53.refs_4_ = bf16[128,1024]{1,0:T(8,128)(2,1)S(1)} collective-permute-done((bf16[128,1024]{1,0:T(8,128)(2,1)S(1)}, bf16[128,1024]{1,0:T(8,128)(2,1)S(1)}, u32[]{:S(2)}, u32[]{:S(2)}) %collective-permute-start.53) | collective-permute-done | bytes 262176 | tf_op jit(solution)/shard_map/ppermute | solution.py:28
  392.1 5.5 attend_back.6
  405.8 8.2 %collective-permute-done.62 = bf16[4,64,1024]{2,1,0:T(8,128)(2,1)} collective-permute-done((bf16[4,64,1024]{2,1,0:T(8,128)(2,1)}, bf16[4,64,1024]{2,1,0:T(8,128)(2,1)}, u32[]{:S(2)}, u32[]{:S(2)}) %collective-permute-start.62) | collective-permute-done | bytes 524320 | tf_op jit(solution)/shard_map/ppermute | solution.py:36
  417.6 10.7 %collective-permute-done.60 = bf16[4,64,1024]{2,1,0:T(8,128)(2,1)} collective-permute-done((bf16[4,64,1024]{2,1,0:T(8,128)(2,1)}, bf16[4,64,1024]{2,1,0:T(8,128)(2,1)}, u32[]{:S(2)}, u32[]{:S(2)}) %collective-permute-start.60) | collective-permute-done | bytes 524320 | tf_op jit(solution)/shard_map/ppermute | solution.py:36
  445.2 8.1 %collective-permute-start.69 = (f32[2,128,128]{2,1,0:T(8,128)S(1)}, f32[2,128,128]{2,1,0:T(8,128)S(1)}, u32[]{:S(2)}, u32[]{:S(2)}) collective-permute-start(f32[2,128,128]{2,1,0:T(8,128)S(1)} %get-tuple-element.101), channel_id=1, source_target_pairs={{0,4},{4,0},{8,12},{12,8},{1,5},{5,1},{9,13},{13,9},{2,6},{6,2},{1... | collective-permute-start | bytes 393224 | tf_op jit(solution)/shard_map/ppermute | solution.py:28
  470.6 22.0 %collective-permute-done.68.refs_7_ = f32[2,128,128]{2,1,0:T(8,128)S(1)} collective-permute-done((f32[2,128,128]{2,1,0:T(8,128)S(1)}, f32[2,128,128]{2,1,0:T(8,128)S(1)}, u32[]{:S(2)}, u32[]{:S(2)}) %collective-permute-start.68) | collective-permute-done | bytes 131104 | tf_op jit(solution)/shard_map/ppermute | solution.py:28
  498.7 5.5 attend_back.7
  522.1 51.6 %collective-permute-start.80 = (bf16[512,1024]{1,0:T(8,128)(2,1)S(1)}, bf16[512,1024]{1,0:T(8,128)(2,1)}, u32[]{:S(2)}, u32[]{:S(2)}) collective-permute-start(bf16[512,1024]{1,0:T(8,128)(2,1)S(1)} %bitcast.392), channel_id=1, source_target_pairs={{0,16},{1,17},{2,18},{3,19},{16,0},{17,1},{18,2},{19,3},{4,20},{5,... | collective-permute-start | bytes 3145736 | tf_op jit(solution)/shard_map/ppermute | solution.py:36
  585.2 33.6 %collective-permute-done.72 = f32[2]{0:T(128)S(1)} collective-permute-done((f32[2]{0:T(128)S(1)}, f32[2]{0:T(128)S(1)}, u32[]{:S(2)}, u32[]{:S(2)}) %collective-permute-start.72) | collective-permute-done | bytes 40 | tf_op jit(solution)/shard_map/ppermute | solution.py:36
  626.5 24.0 %weight_gradient.1 = f32[1024,4,1024]{2,1,0:T(4,128)} custom-call(f32[8]{0:T(128)} %reshape.678.clip, s32[1]{0:T(128)} %bitcast.129.info, bf16[512,1024]{1,0:T(8,128)(2,1)} %get-tuple-element.116.refs_0_, bf16[512,1024]{1,0:T(8,128)(2,1)} %get-tuple-element.31.refs_1_, bf16[512,1024]{1,0:T(8,128)(2,1)} %get-tuple-element.115.refs_2_, ...), custom_call_target="tpu_custom_call" | custom-call | flops 8589934592 | bytes 41943040 | tf_op jit(solution)/shard_map/weight_gradient/pallas_call | solution.py:289
  (455 shorter events, 299.5 us)
Async XLA Ops:
  7.2 106.1 %reduce-scatter.3.cloned.1.call-start = ((), (), s32[]{:S(2)}) async-start(), calls=%async_computation.2 | async-start | bytes 3932160 | tf_op jit(solution)/shard_map/reduce_scatter | solution.py:357
  53.0 145.2 %reduce-scatter.5.cloned.1.call-start = ((), (), s32[]{:S(2)}) async-start(), calls=%async_computation.3 | async-start | bytes 3932160 | tf_op jit(solution)/shard_map/reduce_scatter | solution.py:357
  80.3 545.3 %all-gather.3.cloned.1.call-start = ((), (), s32[]{:S(2)}) async-start(), calls=%async_computation.4 | async-start | bytes 2621440 | tf_op jit(solution)/shard_map/all_gather | solution.py:402
  129.3 59.4 %collective-permute-start.15 = (bf16[1024,1024]{1,0:T(8,128)(2,1)}, bf16[1024,1024]{1,0:T(8,128)(2,1)}, u32[]{:S(2)}, u32[]{:S(2)}) collective-permute-start(bf16[1024,1024]{1,0:T(8,128)(2,1)} %slice_bitcast_fusion.3), channel_id=1, source_target_pairs={{16,0},{17,1},{18,2},{19,3},{20,4},{21,5},{22,6},{23,7},{24,8},{25... | collective-permute-start | bytes 6291464 | tf_op jit(solution)/shard_map/ppermute | solution.py:36
  195.0 39.1 %collective-permute-start.18 = (bf16[128,1024]{1,0:T(8,128)(2,1)S(1)}, bf16[128,1024]{1,0:T(8,128)(2,1)S(1)}, u32[]{:S(2)}, u32[]{:S(2)}) collective-permute-start(bf16[128,1024]{1,0:T(8,128)(2,1)S(1)} %get-tuple-element.91), channel_id=1, source_target_pairs={{0,4},{4,0},{8,12},{12,8},{16,20},{20,16},{24,28},{28,24},{1,5},{5... | collective-permute-start | bytes 786440 | tf_op jit(solution)/shard_map/ppermute | solution.py:28
  196.0 38.1 %collective-permute-start.17 = (bf16[128,1024]{1,0:T(8,128)(2,1)S(1)}, bf16[128,1024]{1,0:T(8,128)(2,1)S(1)}, u32[]{:S(2)}, u32[]{:S(2)}) collective-permute-start(bf16[128,1024]{1,0:T(8,128)(2,1)S(1)} %get-tuple-element.92), channel_id=1, source_target_pairs={{0,8},{4,12},{8,0},{12,4},{16,24},{20,28},{24,16},{28,20},{1,9},{5... | collective-permute-start | bytes 786440 | tf_op jit(solution)/shard_map/ppermute | solution.py:28
  207.4 29.2 %collective-permute-start.30 = (bf16[128,1024]{1,0:T(8,128)(2,1)S(1)}, bf16[128,1024]{1,0:T(8,128)(2,1)S(1)}, u32[]{:S(2)}, u32[]{:S(2)}) collective-permute-start(bf16[128,1024]{1,0:T(8,128)(2,1)S(1)} %attend.3), channel_id=1, source_target_pairs={{0,12},{4,8},{8,4},{12,0},{1,13},{5,9},{9,5},{13,1},{2,14},{6,10},... | collective-permute-start | bytes 786440 | tf_op jit(solution)/shard_map/ppermute | solution.py:28
  211.2 30.6 %collective-permute-start.29 = (bf16[128,1024]{1,0:T(8,128)(2,1)S(1)}, bf16[128,1024]{1,0:T(8,128)(2,1)S(1)}, u32[]{:S(2)}, u32[]{:S(2)}) collective-permute-start(bf16[128,1024]{1,0:T(8,128)(2,1)S(1)} %attend.3), channel_id=1, source_target_pairs={{0,8},{4,12},{8,0},{12,4},{1,9},{5,13},{9,1},{13,5},{2,10},{6,14},... | collective-permute-start | bytes 786440 | tf_op jit(solution)/shard_map/ppermute | solution.py:28
  298.7 29.5 %collective-permute-start.50 = (bf16[4,64,1024]{2,1,0:T(8,128)(2,1)S(1)}, bf16[4,64,1024]{2,1,0:T(8,128)(2,1)S(1)}, u32[]{:S(2)}, u32[]{:S(2)}) collective-permute-start(bf16[4,64,1024]{2,1,0:T(8,128)(2,1)S(1)} %add_convert_fusion.3), channel_id=1, source_target_pairs={{0,2},{1,3},{2,0},{3,1},{4,6},{5,7},{6,4},{7,5},{8,10},{9,11},{10,... | collective-permute-start | bytes 1572872 | tf_op jit(solution)/shard_map/ppermute | solution.py:36
  300.6 27.6 %collective-permute-start.49 = (bf16[4,64,1024]{2,1,0:T(8,128)(2,1)S(1)}, bf16[4,64,1024]{2,1,0:T(8,128)(2,1)S(1)}, u32[]{:S(2)}, u32[]{:S(2)}) collective-permute-start(bf16[4,64,1024]{2,1,0:T(8,128)(2,1)S(1)} %add_convert_fusion.3), channel_id=1, source_target_pairs={{16,0},{17,1},{18,2},{19,3},{20,4},{21,5},{22,6},{23,7},{24,8},{25... | collective-permute-start | bytes 1572872 | tf_op jit(solution)/shard_map/ppermute | solution.py:36
  363.8 33.8 %collective-permute-start.59 = (bf16[4,64,1024]{2,1,0:T(8,128)(2,1)S(1)}, bf16[4,64,1024]{2,1,0:T(8,128)(2,1)S(1)}, u32[]{:S(2)}, u32[]{:S(2)}) collective-permute-start(bf16[4,64,1024]{2,1,0:T(8,128)(2,1)S(1)} %constant_dynamic-slice_fusion.12), channel_id=1, source_target_pairs={{0,1},{1,0},{2,3},{3,2},{16,17},{17,16},{18,19},{19,18},{4,5},{5,4... | collective-permute-start | bytes 1572872 | tf_op jit(solution)/shard_map/ppermute | solution.py:36
  404.0 221.5 %all-gather.5.cloned.1.call-start = ((), (), s32[]{:S(2)}) async-start(), calls=%async_computation.5 | async-start | bytes 2621440 | tf_op jit(solution)/shard_map/all_gather | solution.py:402
  453.4 41.8 %collective-permute-start.66 = (bf16[128,1024]{1,0:T(8,128)(2,1)S(1)}, bf16[128,1024]{1,0:T(8,128)(2,1)S(1)}, u32[]{:S(2)}, u32[]{:S(2)}) collective-permute-start(bf16[128,1024]{1,0:T(8,128)(2,1)S(1)} %get-tuple-element.59), channel_id=1, source_target_pairs={{0,4},{4,0},{8,12},{12,8},{1,5},{5,1},{9,13},{13,9},{2,6},{6,2},{1... | collective-permute-start | bytes 786440 | tf_op jit(solution)/shard_map/ppermute | solution.py:28
  455.3 40.5 %collective-permute-start.65 = (bf16[128,1024]{1,0:T(8,128)(2,1)S(1)}, bf16[128,1024]{1,0:T(8,128)(2,1)S(1)}, u32[]{:S(2)}, u32[]{:S(2)}) collective-permute-start(bf16[128,1024]{1,0:T(8,128)(2,1)S(1)} %get-tuple-element.60), channel_id=1, source_target_pairs={{0,8},{4,12},{8,0},{12,4},{1,9},{5,13},{9,1},{13,5},{2,10},{6,14},... | collective-permute-start | bytes 786440 | tf_op jit(solution)/shard_map/ppermute | solution.py:28
  459.2 38.1 %collective-permute-start.64 = (bf16[128,1024]{1,0:T(8,128)(2,1)S(1)}, bf16[128,1024]{1,0:T(8,128)(2,1)S(1)}, u32[]{:S(2)}, u32[]{:S(2)}) collective-permute-start(bf16[128,1024]{1,0:T(8,128)(2,1)S(1)} %get-tuple-element.61), channel_id=1, source_target_pairs={{0,12},{4,8},{8,4},{12,0},{1,13},{5,9},{9,5},{13,1},{2,14},{6,10},... | collective-permute-start | bytes 786440 | tf_op jit(solution)/shard_map/ppermute | solution.py:28
  463.5 29.0 %collective-permute-start.68 = (f32[2,128,128]{2,1,0:T(8,128)S(1)}, f32[2,128,128]{2,1,0:T(8,128)S(1)}, u32[]{:S(2)}, u32[]{:S(2)}) collective-permute-start(f32[2,128,128]{2,1,0:T(8,128)S(1)} %get-tuple-element.102), channel_id=1, source_target_pairs={{0,8},{4,12},{8,0},{12,4},{1,9},{5,13},{9,1},{13,5},{2,10},{6,14},... | collective-permute-start | bytes 393224 | tf_op jit(solution)/shard_map/ppermute | solution.py:28
  465.5 28.4 %collective-permute-start.67 = (f32[2,128,128]{2,1,0:T(8,128)S(1)}, f32[2,128,128]{2,1,0:T(8,128)S(1)}, u32[]{:S(2)}, u32[]{:S(2)}) collective-permute-start(f32[2,128,128]{2,1,0:T(8,128)S(1)} %get-tuple-element.103), channel_id=1, source_target_pairs={{0,12},{4,8},{8,4},{12,0},{1,13},{5,9},{9,5},{13,1},{2,14},{6,10},... | collective-permute-start | bytes 393224 | tf_op jit(solution)/shard_map/ppermute | solution.py:28
  492.6 83.9 %collective-permute-start.40 = (f32[2,128,128]{2,1,0:T(8,128)}, f32[2,128,128]{2,1,0:T(8,128)}, u32[]{:S(2)}, u32[]{:S(2)}) collective-permute-start(f32[2,128,128]{2,1,0:T(8,128)} %get-tuple-element.104), channel_id=1, source_target_pairs={{16,28},{20,24},{24,20},{28,16},{17,29},{21,25},{25,21},{29,17},{1... | collective-permute-start | bytes 393224 | tf_op jit(solution)/shard_map/ppermute | solution.py:28
  493.9 82.6 %collective-permute-start.42 = (f32[2,128,128]{2,1,0:T(8,128)}, f32[2,128,128]{2,1,0:T(8,128)}, u32[]{:S(2)}, u32[]{:S(2)}) collective-permute-start(f32[2,128,128]{2,1,0:T(8,128)} %get-tuple-element.105), channel_id=1, source_target_pairs={{16,20},{20,16},{24,28},{28,24},{17,21},{21,17},{25,29},{29,25},{1... | collective-permute-start | bytes 393224 | tf_op jit(solution)/shard_map/ppermute | solution.py:28
  518.3 55.5 %collective-permute-start.82 = (bf16[128,1024]{1,0:T(8,128)(2,1)S(1)}, bf16[128,1024]{1,0:T(8,128)(2,1)S(1)}, u32[]{:S(2)}, u32[]{:S(2)}) collective-permute-start(bf16[128,1024]{1,0:T(8,128)(2,1)S(1)} %collective-permute-done.81), channel_id=1, source_target_pairs={{16,20},{20,16},{24,28},{28,24},{17,21},{21,17},{25,29},{29,25},{1... | collective-permute-start | bytes 786440 | tf_op jit(solution)/shard_map/ppermute | solution.py:28
  521.2 55.4 %collective-permute-start.41 = (f32[2,128,128]{2,1,0:T(8,128)}, f32[2,128,128]{2,1,0:T(8,128)S(1)}, u32[]{:S(2)}, u32[]{:S(2)}) collective-permute-start(f32[2,128,128]{2,1,0:T(8,128)} %get-tuple-element.106), channel_id=1, source_target_pairs={{16,24},{20,28},{24,16},{28,20},{17,25},{21,29},{25,17},{29,21},{1... | collective-permute-start | bytes 393224 | tf_op jit(solution)/shard_map/ppermute | solution.py:28
  522.1 103.4 %collective-permute-start.80 = (bf16[512,1024]{1,0:T(8,128)(2,1)S(1)}, bf16[512,1024]{1,0:T(8,128)(2,1)}, u32[]{:S(2)}, u32[]{:S(2)}) collective-permute-start(bf16[512,1024]{1,0:T(8,128)(2,1)S(1)} %bitcast.392), channel_id=1, source_target_pairs={{0,16},{1,17},{2,18},{3,19},{16,0},{17,1},{18,2},{19,3},{4,20},{5,... | collective-permute-start | bytes 3145736 | tf_op jit(solution)/shard_map/ppermute | solution.py:36
  576.5 49.0 %collective-permute-start.85 = (bf16[512,1024]{1,0:T(8,128)(2,1)S(1)}, bf16[512,1024]{1,0:T(8,128)(2,1)S(1)}, u32[]{:S(2)}, u32[]{:S(2)}) collective-permute-start(bf16[512,1024]{1,0:T(8,128)(2,1)S(1)} %bitcast.393), channel_id=1, source_target_pairs={{0,16},{1,17},{2,18},{3,19},{16,0},{17,1},{18,2},{19,3},{4,20},{5,... | collective-permute-start | bytes 3145736 | tf_op jit(solution)/shard_map/ppermute | solution.py:36
  583.8 35.0 %collective-permute-start.72 = (f32[2]{0:T(128)S(1)}, f32[2]{0:T(128)S(1)}, u32[]{:S(2)}, u32[]{:S(2)}) collective-permute-start(f32[2]{0:T(128)S(1)} %add.323), channel_id=1, source_target_pairs={{0,16},{1,17},{2,18},{3,19},{16,0},{17,1},{18,2},{19,3},{4,20},{5,... | collective-permute-start | bytes 32 | tf_op jit(solution)/shard_map/ppermute | solution.py:36
  (152 other events, 1475.7 us)
Sparse Core Ops, SparseCore 0:
  53.2 60.0 reduce-scatter.2
  115.5 79.9 reduce-scatter.4
  404.2 52.6 all-gather.2
  505.2 43.1 all-gather.4

commit v3 on v2

--- a/solution.py
+++ b/solution.py
@@ -97,7 +97,7 @@
     own = jnp.where(lax.axis_index("section") == 0, total.astype(F32), 0.0)
     mine = functools.reduce(jnp.add, [g.astype(F32) for g in got], own).astype(BF16)
     other = mp_shift(mine, 1, targets)
-    return halves(mine, other, parity)
+    return halves(mine, other, parity), total
 
 
 def add_up(sources, start):
@@ -156,7 +156,7 @@
     def run():
         first = pair_masks(seq)
         valid = lax.broadcasted_iota(jnp.int32, (seq, seq), 1) < info[1]
-        grams = [jnp.zeros((seq, seq), F32) for _ in range(3)]
+        grams = [jnp.zeros((seq, seq), F32) for _ in range(2)]
         for c in range(0, width, PAIR):
             q, k, v, g = add_up(qs, c), add_up(ks, c), add_up(vs, c), add_up(gs, c)
             k2, v2 = stack_heads(k, first), stack_heads(v, first)
@@ -180,10 +180,14 @@
             gv_ref[:, c : c + PAIR] = gv
             send_ref[:, c : c + PAIR] = gq
             send_ref[:, width + c : width + c + PAIR] = ctx if decoder else gk
+            if send_ref.shape[1] > 2 * width:
+                send_ref[:, 2 * width + c : 2 * width + c + PAIR] = gk if decoder else gv
             grams[0] += mm(gq, gq, NT)
-            grams[1] += mm(gk, gk, NT) + mm(gv, gv, NT)
-            grams[2] += mm(ctx, ctx, NT)
-        for i in range(3):
+            if decoder:
+                grams[1] += mm(ctx, ctx, NT)
+            else:
+                grams[1] += mm(gk, gk, NT) + mm(gv, gv, NT)
+        for i in range(2):
             gram_ref[i] = grams[i]
 
 
@@ -218,12 +222,12 @@
     return call_attention(fwd_kernel, info, operands, (rows,), flops, "attend", after)[0]
 
 
-def attend_back(info, operands, seq, width, decoder, after=()):
+def attend_back(info, operands, seq, width, decoder, slots, after=()):
     outs = (
         jax.ShapeDtypeStruct((seq, width), BF16),
         jax.ShapeDtypeStruct((seq, width), BF16),
-        jax.ShapeDtypeStruct((seq, 2 * width), BF16),
-        jax.ShapeDtypeStruct((3, seq, seq), F32),
+        jax.ShapeDtypeStruct((seq, slots * width), BF16),
+        jax.ShapeDtypeStruct((2, seq, seq), F32),
     )
 
     def kernel(plan, count, *refs):
@@ -235,9 +239,13 @@
 
 def wgrad_kernel(mb, chunk, scale, clip, info, *refs):
     x1, xa, xb = refs[:mb], refs[mb : 2 * mb], refs[2 * mb : 3 * mb]
-    send, kept, back = (refs[i * mb : (i + 1) * mb] for i in (3, 4, 5))
-    noise, out = refs[6 * mb :]
+    send, kept = refs[3 * mb : 4 * mb], refs[4 * mb : 5 * mb]
+    noise, out = refs[-2:]
     width = out.shape[2]
+    back = [(ref, 0) for ref in refs[5 * mb : -2]] + [(send[-1], 2 * width)]
+    kept = [(ref, 0) for ref in kept]
+    first = [(ref, 0) for ref in send]
+    second = [(ref, width) for ref in send]
     count = x1[0].shape[0] // chunk
     is_dec = info[0] == 1
 
@@ -253,26 +261,26 @@
             for b, ref in enumerate(group)
         ]
 
-    def put(slot, lefts, rights, first):
+    def put(slot, lefts, rights):
         total = functools.reduce(
-            jnp.add, [mm(x, y[:, first : first + width], TN) for x, y in zip(lefts, rights)]
+            jnp.add, [mm(x, y[:, c : c + width], TN) for x, (y, c) in zip(lefts, rights)]
         )
         out[:, slot, :] = (total + noise[:, slot, :]) * scale
 
     l1, la, lb = clipped(x1), clipped(xa), clipped(xb)
-    put(0, l1, send, 0)
+    put(0, l1, first)
 
     @pl.when(is_dec)
     def decoder():
-        put(1, lb, back, 0)
-        put(2, lb, kept, 0)
-        put(3, la, send, width)
+        put(1, lb, back)
+        put(2, lb, kept)
+        put(3, la, second)
 
     @pl.when(jnp.logical_not(is_dec))
     def encoder():
-        put(1, la, send, width)
-        put(2, l1, back, 0)
-        put(3, lb, kept, 0)
+        put(1, la, second)
+        put(2, l1, back)
+        put(3, lb, kept)
 
 
 def wgrad(clip, info, x1, xa, xb, send, kept, back, noise, chunk, examples):
@@ -320,9 +328,11 @@
     def rows_of(x):
         return x.reshape(n * seq, x.shape[-1])
 
-    def owner_grams(x, sections):
-        terms = jnp.einsum("bntd,bnud->nbtu", x, x, preferred_element_type=F32)
-        return to_owner(terms, sections)
+    def grams(x):
+        return jnp.einsum("itd,iud->itu", x, x, preferred_element_type=F32)
+
+    def gram_terms(left, right):
+        return jnp.sum(grams(left) * grams(right.reshape(n, seq, inner)), axis=(1, 2))
 
     def info(flag, b):
         return jnp.stack([flag.astype(jnp.int32), lengths[0, b]])
@@ -359,64 +369,74 @@
             )
         )
     w_relay = jnp.where(is_dec, w[2], mp_shift(w[1], 0, dec, flip=True))
-    ctx_all, enc_out, kv_parts = [], [], []
+    ctx_all, enc_out, kv_parts, keys = [], [], [], []
     for b in range(mb):
         qkv = [[(first[b], i * inner)] for i in range(3)]
-        after = [kv_parts[-1][1]] if b else []
-        ctx = attend(info(section == 0, b), qkv, seq, inner, after)
+        ctx = attend(info(section == 0, b), qkv, seq, inner, keys[-1:])
         ctx_all.append(rows_of(gather(ctx, enc)))
         terms = mm(ctx_all[b], w[3], NT).reshape(n, seq, depth)
-        enc_out.append(relay(terms, raw_half[b], enc, 0, both))
+        enc_out.append(relay(terms, raw_half[b], enc, 0, both)[0])
         terms = mm(rows_of(enc_out[b]), w_relay).astype(BF16).reshape(n, seq, inner)
         kv_parts.append(to_owner(terms, both))
-    relay_all, grad_enc, dec_send, dec_gram = [], [], [], []
-    for b in range(mb):
-        parts = kv_parts[b]
-        k = functools.reduce(jnp.add, [part.astype(F32) for part in parts]).astype(BF16)
+        keys.append(functools.reduce(jnp.add, [k.astype(F32) for k in kv_parts[b]]).astype(BF16))
+    relay_all, grad_enc, dec_send, dec_gram, dec_gk = [], [], [], [], []
+    slots = [2] * (mb - 1) + [3]
+    for b in range(mb):
         operands = [
             [(first[b], 0)],
-            [(mp_shift(k, 0, enc, flip=True), 0)],
-            [(part, 0) for part in parts],
+            [(mp_shift(keys[b], 0, enc, flip=True), 0)],
+            [(part, 0) for part in kv_parts[b]],
             [(first[mb - 1], (1 + b) * inner)],
         ]
-        gk, gv, send, gram = attend_back(info(section == 1, b), operands, seq, inner, True)
+        gk, gv, send, gram = attend_back(
+            info(section == 1, b), operands, seq, inner, True, slots[b]
+        )
         rows = jnp.where(is_dec, gv, mp_shift(gk, 0, dec, flip=True))
         relay_all.append(rows_of(gather(rows, both)))
         terms = mm(relay_all[b], w_relay, NT).reshape(n, seq, depth)
-        grad_enc.append(relay(terms, None, both, 1, enc))
+        grad, relayed = relay(terms, None, both, 1, enc)
+        grad_enc.append(grad)
         dec_send.append(send)
         dec_gram.append(gram)
-    gram_enc_out = functools.reduce(jnp.add, owner_grams(jnp.stack(enc_out), dec))
-    grad_grams = owner_grams(jnp.stack(grad_enc), enc)
-    gram_grad_enc = functools.reduce(jnp.add, grad_grams)
     send_all, enc_gram, back_all = [], [], []
     for b in range(mb):
         gctx = to_owner(mm(rows_of(grad_enc[b]), w[3]).astype(BF16).reshape(n, seq, inner), enc)
         operands = [[(first[b], i * inner)] for i in range(3)] + [[(part, 0) for part in gctx]]
-        after = grad_grams[1:] if b == mb - 1 else []
+        after = [relayed] if b < mb - 1 else []
         _, gv, send, gram = attend_back(
-            info(section == 0, b), operands, seq, inner, False, after
+            info(section == 0, b), operands, seq, inner, False, slots[b], after
         )
         enc_gram.append(gram)
         send = jnp.where(is_dec, dec_send[b], send)
         send_all.append(lax.all_gather(send, "dp", axis=0, tiled=True))
-        gv_all = rows_of(gather(mp_shift(gv, 0, enc, flip=True), dec))
-        back_all.append(mp_shift(jnp.where(is_dec, gv_all, relay_all[b]), 0, both, flip=True))
+        if b < mb - 1:
+            gv_all = rows_of(gather(mp_shift(gv, 0, enc, flip=True), dec))
+            back_all.append(mp_shift(jnp.where(is_dec, gv_all, relay_all[b]), 0, both, flip=True))
     normed = (own32 * inv[..., None] * gain).astype(BF16)
     gram_x = jnp.einsum("btd,bud->btu", normed, normed, preferred_element_type=F32)
     gram_cot = jnp.einsum("btd,bud->btu", cot, cot, preferred_element_type=F32)
-    dg, eg = jnp.stack(dec_gram, axis=1), jnp.stack(enc_gram, axis=1)
-    dec_sq = jnp.sum(gram_x * dg[0] + gram_enc_out * dg[1] + gram_cot * dg[2], axis=(1, 2))
-    enc_sq = jnp.sum(gram_x * (eg[0] + eg[1]) + gram_grad_enc * eg[2], axis=(1, 2))
-    sq = jnp.where(is_dec, dec_sq, enc_sq)
-    step = 1
-    while step < lax.axis_size("mp"):
-        sq = sq + mp_shift(sq, step, both)
-        step *= 2
+    sq = []
+    for b in range(mb):
+        dg, eg = dec_gram[b], enc_gram[b]
+        own = jnp.where(
+            is_dec,
+            jnp.sum(gram_x[b] * dg[0] + gram_cot[b] * dg[1]),
+            jnp.sum(gram_x[b] * (eg[0] + eg[1])),
+        )
+        terms = jnp.where(is_dec, 0.0, gram_terms(grad_enc[b], ctx_all[b]))
+        terms = terms + gram_terms(enc_out[b], relay_all[b])
+        sq.append(terms + jnp.where(jnp.arange(n) == me, own, 0.0))
+    sq = jnp.stack(sq)
+    for axis, shift in (("mp", mp_shift), ("dp", dp_shift)):
+        step = 1
+        while step < lax.axis_size(axis):
+            sq = sq + shift(sq, step, both)
+            step *= 2
     sq = sq + mp_shift(sq, 0, both, flip=True)
     bound = jnp.sqrt(jnp.float32(8.0 * D * HEADS * HEAD))
-    clip = bound / (jnp.sqrt(sq) + 0.01 * bound)
-    clip_all = gather(clip, both).T.reshape(-1)
+    clip_all = bound / (jnp.sqrt(sq) + 0.01 * bound)
+    clip = lax.dynamic_slice_in_dim(clip_all, me, 1, 1)[:, 0]
+    clip_all = clip_all.reshape(-1)
     xa = [jnp.where(is_dec, c, r) for c, r in zip(cot_cols, x)]
     xb = [rows_of(jnp.where(is_dec, o, g)) for o, g in zip(enc_out, grad_enc)]
     kept = [jnp.where(is_dec, r, c) for r, c in zip(relay_all, ctx_all)]

time: 667 us -> 642 us (0.963)
  starting transfers between devices: 226 us -> 185 us
  waiting for transfers between devices: 255 us -> 274 us
  other arithmetic: 50 us -> 40.5 us
    ppermute x51 -> x41, starting transfers between devices: 131 us -> 85.7 us  [dp_shift(): return lax.ppermute(x, ('section', 'dp'), pairs)]
    ppermute x51 -> x41, waiting for transfers between devices: 106 us -> 135 us  [dp_shift(): return lax.ppermute(x, ('section', 'dp'), pairs)]
    ppermute x35 -> x33, waiting for transfers between devices: 117 us -> 106 us  [mp_shift(): return lax.ppermute(x, ('section', 'mp'), pairs)]
    unnamed x173 -> x161, local copies, waits for them, and re-layouts: 19.2 us -> 23.6 us
    ppermute x35 -> x33, starting transfers between devices: 95.6 us -> 98.7 us  [mp_shift(): return lax.ppermute(x, ('section', 'mp'), pairs)]
  transfers between devices with their start and end apart: 90 -> 78, of which waited for: 38 -> 40; matrix products, arithmetic and copies ran while one was open for 15% -> 13% of each run, Pallas kernels for 2% -> 1%
where the time goes in v3:
time: 642 us; the launch traced here: 633 us
  waiting for transfers between devices  274 us (43%)
  starting transfers between devices  185 us (29%)
  other arithmetic  40.5 us (6%)
  Pallas kernels  39.5 us (6%)
  matrix products  38.6 us (6%)
  local copies, waits for them, and re-layouts  36.8 us (6%)
  between operations  18.7 us (3%)
    ppermute x41, waiting for transfers between devices, dp_shift(): return lax.ppermute(x, ('section', 'dp'), pairs)  135 us
    ppermute x33, waiting for transfers between devices, mp_shift(): return lax.ppermute(x, ('section', 'mp'), pairs)  106 us
    ppermute x33, starting transfers between devices, mp_shift(): return lax.ppermute(x, ('section', 'mp'), pairs)  98.7 us
    ppermute x41, starting transfers between devices, dp_shift(): return lax.ppermute(x, ('section', 'dp'), pairs)  85.7 us
    reduce_scatter x2, waiting for transfers between devices, per_device(): lax.psum_scatter(parts.reshape(n, seq, 3 * inner), 'dp', scatter_dimensio...  32.6 us
    dot_general x14, matrix products, mm(): return lax.dot_general(left, right, dims, preferred_element_type=F32)  31.5 us
    pallas_call x1, Pallas kernels, wgrad(): pl.pallas_call(functools.partial(wgrad_kernel, mb, chunk, 1.0 / examples)...  24 us
    unnamed x161, local copies, waits for them, and re-layouts  23.6 us
  transfers between devices with their start and end apart: 78, of which 40 were waited for; matrix products, arithmetic and copies ran while one was open for 13% of the time, Pallas kernels for 1%

profile of v3, /device:TPU:0, one launch (start us, length us, event | category | flops | bytes accessed | tf_op | source)
XLA Modules:
  0.0 632.5 jit_solution(11339351621143590490)
XLA Ops:
  27.6 9.7 %copy.25 = bf16[1,1024,4,1024]{3,1,2,0:T(8,128)(2,1)} copy(bf16[1,1024,4,1024]{3,2,1,0:T(4,128)(2,1)} %param.8) | data formatting | bytes 16777216 | tf_op args[2]
  80.6 32.6 %reduce-scatter.3.cloned.1.call-done = bf16[1,128,3072]{2,1,0:T(8,128)(2,1)} async-done(((bf16[4,128,3072]{2,1,0:T(8,128)(2,1)}), bf16[1,128,3072]{2,1,0:T(8,128)(2,1)}) %reduce-scatter.3.cloned.1.call-update) | async-done | bytes 786448 | tf_op jit(solution)/shard_map/reduce_scatter | solution.py:367
  130.5 13.3 %collective-permute-done.8 = bf16[128,1024]{1,0:T(8,128)(2,1)} collective-permute-done((bf16[128,1024]{1,0:T(8,128)(2,1)S(1)}, bf16[128,1024]{1,0:T(8,128)(2,1)}, u32[]{:S(2)}, u32[]{:S(2)}) %collective-permute-start.8) | collective-permute-done | bytes 262176 | tf_op jit(solution)/shard_map/ppermute | solution.py:28
  161.3 9.4 %collective-permute-done.13 = bf16[4,64,1024]{2,1,0:T(8,128)(2,1)S(1)} collective-permute-done((bf16[4,64,1024]{2,1,0:T(8,128)(2,1)S(1)}, bf16[4,64,1024]{2,1,0:T(8,128)(2,1)S(1)}, u32[]{:S(2)}, u32[]{:S(2)}) %collective-permute-start.13) | collective-permute-done | bytes 524320 | tf_op jit(solution)/shard_map/ppermute | solution.py:36
  171.9 10.4 %collective-permute-done.11 = bf16[4,64,1024]{2,1,0:T(8,128)(2,1)S(1)} collective-permute-done((bf16[4,64,1024]{2,1,0:T(8,128)(2,1)S(1)}, bf16[4,64,1024]{2,1,0:T(8,128)(2,1)S(1)}, u32[]{:S(2)}, u32[]{:S(2)}) %collective-permute-start.11) | collective-permute-done | bytes 524320 | tf_op jit(solution)/shard_map/ppermute | solution.py:36
  182.7 5.9 collective-permute-done.15
  197.6 5.8 collective-permute-done.16.refs_4_
  207.4 11.8 %collective-permute-done.17.refs_5_ = bf16[128,1024]{1,0:T(8,128)(2,1)S(1)} collective-permute-done((bf16[128,1024]{1,0:T(8,128)(2,1)S(1)}, bf16[128,1024]{1,0:T(8,128)(2,1)S(1)}, u32[]{:S(2)}, u32[]{:S(2)}) %collective-permute-start.17) | collective-permute-done | bytes 262176 | tf_op jit(solution)/shard_map/ppermute | solution.py:28
  235.2 12.2 %collective-permute-done.41 = bf16[128,1024]{1,0:T(8,128)(2,1)S(1)} collective-permute-done((bf16[128,1024]{1,0:T(8,128)(2,1)S(1)}, bf16[128,1024]{1,0:T(8,128)(2,1)S(1)}, u32[]{:S(2)}, u32[]{:S(2)}) %collective-permute-start.41) | collective-permute-done | bytes 262176 | tf_op jit(solution)/shard_map/ppermute | solution.py:28
  266.6 12.7 %collective-permute-done.28 = bf16[128,1024]{1,0:T(8,128)(2,1)S(1)} collective-permute-done((bf16[128,1024]{1,0:T(8,128)(2,1)S(1)}, bf16[128,1024]{1,0:T(8,128)(2,1)S(1)}, u32[]{:S(2)}, u32[]{:S(2)}) %collective-permute-start.28) | collective-permute-done | bytes 262176 | tf_op jit(solution)/shard_map/ppermute | solution.py:36
  290.5 12.1 %collective-permute-done.30 = bf16[128,1024]{1,0:T(8,128)(2,1)S(1)} collective-permute-done((bf16[128,1024]{1,0:T(8,128)(2,1)S(1)}, bf16[128,1024]{1,0:T(8,128)(2,1)S(1)}, u32[]{:S(2)}, u32[]{:S(2)}) %collective-permute-start.30) | collective-permute-done | bytes 262176 | tf_op jit(solution)/shard_map/ppermute | solution.py:28
  312.3 6.5 %collective-permute-done.48.refs_4_ = bf16[128,1024]{1,0:T(8,128)(2,1)S(1)} collective-permute-done((bf16[128,1024]{1,0:T(8,128)(2,1)S(1)}, bf16[128,1024]{1,0:T(8,128)(2,1)S(1)}, u32[]{:S(2)}, u32[]{:S(2)}) %collective-permute-start.48) | collective-permute-done | bytes 262176 | tf_op jit(solution)/shard_map/ppermute | solution.py:28
  318.9 6.3 collective-permute-done.50.refs_6_
  339.8 26.2 %collective-permute-done.52 = bf16[128,1024]{1,0:T(8,128)(2,1)S(1)} collective-permute-done((bf16[128,1024]{1,0:T(8,128)(2,1)S(1)}, bf16[128,1024]{1,0:T(8,128)(2,1)S(1)}, u32[]{:S(2)}, u32[]{:S(2)}) %collective-permute-start.52) | collective-permute-done | bytes 262176 | tf_op jit(solution)/shard_map/ppermute | solution.py:36
  377.2 9.6 %collective-permute-done.54 = bf16[128,1024]{1,0:T(8,128)(2,1)S(1)} collective-permute-done((bf16[128,1024]{1,0:T(8,128)(2,1)S(1)}, bf16[128,1024]{1,0:T(8,128)(2,1)S(1)}, u32[]{:S(2)}, u32[]{:S(2)}) %collective-permute-start.54) | collective-permute-done | bytes 262176 | tf_op jit(solution)/shard_map/ppermute | solution.py:28
  405.2 12.3 %collective-permute-done.38.refs_4_ = bf16[128,1024]{1,0:T(8,128)(2,1)S(1)} collective-permute-done((bf16[128,1024]{1,0:T(8,128)(2,1)S(1)}, bf16[128,1024]{1,0:T(8,128)(2,1)S(1)}, u32[]{:S(2)}, u32[]{:S(2)}) %collective-permute-start.38) | collective-permute-done | bytes 262176 | tf_op jit(solution)/shard_map/ppermute | solution.py:28
  417.4 5.3 attend_back.6
  428.4 10.5 %collective-permute-done.59 = bf16[4,64,1024]{2,1,0:T(8,128)(2,1)S(1)} collective-permute-done((bf16[4,64,1024]{2,1,0:T(8,128)(2,1)S(1)}, bf16[4,64,1024]{2,1,0:T(8,128)(2,1)S(1)}, u32[]{:S(2)}, u32[]{:S(2)}) %collective-permute-start.59) | collective-permute-done | bytes 524320 | tf_op jit(solution)/shard_map/ppermute | solution.py:36
  442.5 10.6 %collective-permute-done.57 = bf16[4,64,1024]{2,1,0:T(8,128)(2,1)S(1)} collective-permute-done((bf16[4,64,1024]{2,1,0:T(8,128)(2,1)S(1)}, bf16[4,64,1024]{2,1,0:T(8,128)(2,1)S(1)}, u32[]{:S(2)}, u32[]{:S(2)}) %collective-permute-start.57) | collective-permute-done | bytes 524320 | tf_op jit(solution)/shard_map/ppermute | solution.py:36
  461.2 8.2 %collective-permute-start.63 = (bf16[128,1024]{1,0:T(8,128)(2,1)S(1)}, bf16[128,1024]{1,0:T(8,128)(2,1)S(1)}, u32[]{:S(2)}, u32[]{:S(2)}) collective-permute-start(bf16[128,1024]{1,0:T(8,128)(2,1)S(1)} %get-tuple-element.57), channel_id=1, source_target_pairs={{0,4},{4,0},{8,12},{12,8},{1,5},{5,1},{9,13},{13,9},{2,6},{6,2},{1... | collective-permute-start | bytes 786440 | tf_op jit(solution)/shard_map/ppermute | solution.py:28
  479.0 13.6 %collective-permute-done.62.refs_4_ = bf16[128,1024]{1,0:T(8,128)(2,1)S(1)} collective-permute-done((bf16[128,1024]{1,0:T(8,128)(2,1)S(1)}, bf16[128,1024]{1,0:T(8,128)(2,1)S(1)}, u32[]{:S(2)}, u32[]{:S(2)}) %collective-permute-start.62) | collective-permute-done | bytes 262176 | tf_op jit(solution)/shard_map/ppermute | solution.py:28
  492.7 5.6 attend_back.7
  521.3 57.1 %collective-permute-start.73 = (bf16[512,1024]{1,0:T(8,128)(2,1)S(1)}, bf16[512,1024]{1,0:T(8,128)(2,1)}, u32[]{:S(2)}, u32[]{:S(2)}) collective-permute-start(bf16[512,1024]{1,0:T(8,128)(2,1)S(1)} %bitcast.303), channel_id=1, source_target_pairs={{0,16},{1,17},{2,18},{3,19},{16,0},{17,1},{18,2},{19,3},{4,20},{5,... | collective-permute-start | bytes 3145736 | tf_op jit(solution)/shard_map/ppermute | solution.py:36
  601.4 24.0 %weight_gradient.1 = f32[1024,4,1024]{2,1,0:T(4,128)} custom-call(f32[8]{0:T(128)} %reshape.520.clip, s32[1]{0:T(128)} %bitcast.101.info, bf16[512,1024]{1,0:T(8,128)(2,1)} %get-tuple-element.108.refs_0_, bf16[512,1024]{1,0:T(8,128)(2,1)} %get-tuple-element.35.refs_1_, bf16[512,1024]{1,0:T(8,128)(2,1)} %get-tuple-element.107.refs_2_, ...), custom_call_target="tpu_custom_call" | custom-call | flops 8589934592 | bytes 41943040 | tf_op jit(solution)/shard_map/weight_gradient/pallas_call | solution.py:297
  (418 shorter events, 282.2 us)
Async XLA Ops:
  7.2 106.0 %reduce-scatter.3.cloned.1.call-start = ((), (), s32[]{:S(2)}) async-start(), calls=%async_computation.2 | async-start | bytes 3932160 | tf_op jit(solution)/shard_map/reduce_scatter | solution.py:367
  17.0 22.4 %collective-permute-start = (bf16[1,64,1024]{2,1,0:T(8,128)(2,1)}, bf16[1,64,1024]{2,1,0:T(8,128)(2,1)}, u32[]{:S(2)}, u32[]{:S(2)}) collective-permute-start(bf16[1,64,1024]{2,1,0:T(8,128)(2,1)} %get-tuple-element.90), channel_id=1, source_target_pairs={{0,4},{4,0},{8,12},{12,8},{16,20},{20,16},{24,28},{28,24},{1,5},{5... | collective-permute-start | bytes 393224 | tf_op jit(solution)/shard_map/ppermute | solution.py:28
  18.3 22.2 %collective-permute-start.22 = (bf16[1,64,1024]{2,1,0:T(8,128)(2,1)}, bf16[1,64,1024]{2,1,0:T(8,128)(2,1)S(1)}, u32[]{:S(2)}, u32[]{:S(2)}) collective-permute-start(bf16[1,64,1024]{2,1,0:T(8,128)(2,1)} %get-tuple-element.92), channel_id=1, source_target_pairs={{0,12},{4,8},{8,4},{12,0},{16,28},{20,24},{24,20},{28,16},{1,13},{... | collective-permute-start | bytes 393224 | tf_op jit(solution)/shard_map/ppermute | solution.py:28
  53.0 166.4 %reduce-scatter.5.cloned.1.call-start = ((), (), s32[]{:S(2)}) async-start(), calls=%async_computation.3 | async-start | bytes 3932160 | tf_op jit(solution)/shard_map/reduce_scatter | solution.py:367
  79.2 522.3 %all-gather.3.cloned.1.call-start = ((), (), s32[]{:S(2)}) async-start(), calls=%async_computation.4 | async-start | bytes 2621440 | tf_op jit(solution)/shard_map/all_gather | solution.py:411
  120.0 23.8 %collective-permute-start.8 = (bf16[128,1024]{1,0:T(8,128)(2,1)S(1)}, bf16[128,1024]{1,0:T(8,128)(2,1)}, u32[]{:S(2)}, u32[]{:S(2)}) collective-permute-start(bf16[128,1024]{1,0:T(8,128)(2,1)S(1)} %attend.2), channel_id=1, source_target_pairs={{0,8},{4,12},{8,0},{12,4},{1,9},{5,13},{9,1},{13,5},{2,10},{6,14},... | collective-permute-start | bytes 786440 | tf_op jit(solution)/shard_map/ppermute | solution.py:28
  122.3 21.5 %collective-permute-start.7 = (bf16[128,1024]{1,0:T(8,128)(2,1)S(1)}, bf16[128,1024]{1,0:T(8,128)(2,1)}, u32[]{:S(2)}, u32[]{:S(2)}) collective-permute-start(bf16[128,1024]{1,0:T(8,128)(2,1)S(1)} %attend.2), channel_id=1, source_target_pairs={{0,4},{4,0},{8,12},{12,8},{1,5},{5,1},{9,13},{13,9},{2,6},{6,2},{1... | collective-permute-start | bytes 786440 | tf_op jit(solution)/shard_map/ppermute | solution.py:28
  129.2 59.4 %collective-permute-start.15 = (bf16[1024,1024]{1,0:T(8,128)(2,1)}, bf16[1024,1024]{1,0:T(8,128)(2,1)S(1)}, u32[]{:S(2)}, u32[]{:S(2)}) collective-permute-start(bf16[1024,1024]{1,0:T(8,128)(2,1)} %slice_bitcast_fusion.3), channel_id=1, source_target_pairs={{16,0},{17,1},{18,2},{19,3},{20,4},{21,5},{22,6},{23,7},{24,8},{25... | collective-permute-start | bytes 6291464 | tf_op jit(solution)/shard_map/ppermute | solution.py:36
  159.6 22.7 %collective-permute-start.11 = (bf16[4,64,1024]{2,1,0:T(8,128)(2,1)S(1)}, bf16[4,64,1024]{2,1,0:T(8,128)(2,1)S(1)}, u32[]{:S(2)}, u32[]{:S(2)}) collective-permute-start(bf16[4,64,1024]{2,1,0:T(8,128)(2,1)S(1)} %add_convert_fusion.7), channel_id=1, source_target_pairs={{0,18},{1,19},{2,16},{3,17},{4,22},{5,23},{6,20},{7,21},{8,26},{9,... | collective-permute-start | bytes 1572872 | tf_op jit(solution)/shard_map/ppermute | solution.py:36
  195.9 23.3 %collective-permute-start.17 = (bf16[128,1024]{1,0:T(8,128)(2,1)S(1)}, bf16[128,1024]{1,0:T(8,128)(2,1)S(1)}, u32[]{:S(2)}, u32[]{:S(2)}) collective-permute-start(bf16[128,1024]{1,0:T(8,128)(2,1)S(1)} %get-tuple-element.82), channel_id=1, source_target_pairs={{0,8},{4,12},{8,0},{12,4},{16,24},{20,28},{24,16},{28,20},{1,9},{5... | collective-permute-start | bytes 786440 | tf_op jit(solution)/shard_map/ppermute | solution.py:28
  225.7 21.7 %collective-permute-start.41 = (bf16[128,1024]{1,0:T(8,128)(2,1)S(1)}, bf16[128,1024]{1,0:T(8,128)(2,1)S(1)}, u32[]{:S(2)}, u32[]{:S(2)}) collective-permute-start(bf16[128,1024]{1,0:T(8,128)(2,1)S(1)} %attend.3), channel_id=1, source_target_pairs={{0,8},{4,12},{8,0},{12,4},{1,9},{5,13},{9,1},{13,5},{2,10},{6,14},... | collective-permute-start | bytes 786440 | tf_op jit(solution)/shard_map/ppermute | solution.py:28
  258.8 22.7 %collective-permute-start.46 = (bf16[4,64,1024]{2,1,0:T(8,128)(2,1)S(1)}, bf16[4,64,1024]{2,1,0:T(8,128)(2,1)S(1)}, u32[]{:S(2)}, u32[]{:S(2)}) collective-permute-start(bf16[4,64,1024]{2,1,0:T(8,128)(2,1)S(1)} %add_convert_fusion.3), channel_id=1, source_target_pairs={{0,2},{1,3},{2,0},{3,1},{4,6},{5,7},{6,4},{7,5},{8,10},{9,11},{10,... | collective-permute-start | bytes 1572872 | tf_op jit(solution)/shard_map/ppermute | solution.py:36
  261.9 21.9 %collective-permute-start.45 = (bf16[4,64,1024]{2,1,0:T(8,128)(2,1)S(1)}, bf16[4,64,1024]{2,1,0:T(8,128)(2,1)S(1)}, u32[]{:S(2)}, u32[]{:S(2)}) collective-permute-start(bf16[4,64,1024]{2,1,0:T(8,128)(2,1)S(1)} %add_convert_fusion.3), channel_id=1, source_target_pairs={{0,16},{1,17},{2,18},{3,19},{4,20},{5,21},{6,22},{7,23},{8,24},{9,... | collective-permute-start | bytes 1572872 | tf_op jit(solution)/shard_map/ppermute | solution.py:36
  263.2 22.9 %collective-permute-start.44 = (bf16[4,64,1024]{2,1,0:T(8,128)(2,1)S(1)}, bf16[4,64,1024]{2,1,0:T(8,128)(2,1)S(1)}, u32[]{:S(2)}, u32[]{:S(2)}) collective-permute-start(bf16[4,64,1024]{2,1,0:T(8,128)(2,1)S(1)} %add_convert_fusion.3), channel_id=1, source_target_pairs={{0,18},{1,19},{2,16},{3,17},{4,22},{5,23},{6,20},{7,21},{8,26},{9,... | collective-permute-start | bytes 1572872 | tf_op jit(solution)/shard_map/ppermute | solution.py:36
  332.2 35.4 %collective-permute-start.35 = (bf16[4,64,1024]{2,1,0:T(8,128)(2,1)S(1)}, bf16[4,64,1024]{2,1,0:T(8,128)(2,1)S(1)}, u32[]{:S(2)}, u32[]{:S(2)}) collective-permute-start(bf16[4,64,1024]{2,1,0:T(8,128)(2,1)S(1)} %add_convert_fusion.5), channel_id=1, source_target_pairs={{0,2},{1,3},{2,0},{3,1},{4,6},{5,7},{6,4},{7,5},{8,10},{9,11},{10,... | collective-permute-start | bytes 1572872 | tf_op jit(solution)/shard_map/ppermute | solution.py:36
  335.4 35.1 %collective-permute-start.34 = (bf16[4,64,1024]{2,1,0:T(8,128)(2,1)S(1)}, bf16[4,64,1024]{2,1,0:T(8,128)(2,1)S(1)}, u32[]{:S(2)}, u32[]{:S(2)}) collective-permute-start(bf16[4,64,1024]{2,1,0:T(8,128)(2,1)S(1)} %add_convert_fusion.5), channel_id=1, source_target_pairs={{16,0},{17,1},{18,2},{19,3},{20,4},{21,5},{22,6},{23,7},{24,8},{25... | collective-permute-start | bytes 1572872 | tf_op jit(solution)/shard_map/ppermute | solution.py:36
  336.7 33.8 %collective-permute-start.33 = (bf16[4,64,1024]{2,1,0:T(8,128)(2,1)S(1)}, bf16[4,64,1024]{2,1,0:T(8,128)(2,1)S(1)}, u32[]{:S(2)}, u32[]{:S(2)}) collective-permute-start(bf16[4,64,1024]{2,1,0:T(8,128)(2,1)S(1)} %add_convert_fusion.5), channel_id=1, source_target_pairs={{16,2},{17,3},{18,0},{19,1},{20,6},{21,7},{22,4},{23,5},{24,10},{2... | collective-permute-start | bytes 1572872 | tf_op jit(solution)/shard_map/ppermute | solution.py:36
  338.5 27.5 %collective-permute-start.52 = (bf16[128,1024]{1,0:T(8,128)(2,1)S(1)}, bf16[128,1024]{1,0:T(8,128)(2,1)S(1)}, u32[]{:S(2)}, u32[]{:S(2)}) collective-permute-start(bf16[128,1024]{1,0:T(8,128)(2,1)S(1)} %get-tuple-element.19), channel_id=1, source_target_pairs={{16,0},{17,1},{18,2},{19,3},{20,4},{21,5},{22,6},{23,7},{24,8},{25... | collective-permute-start | bytes 786440 | tf_op jit(solution)/shard_map/ppermute | solution.py:36
  394.2 23.2 %collective-permute-start.38 = (bf16[128,1024]{1,0:T(8,128)(2,1)S(1)}, bf16[128,1024]{1,0:T(8,128)(2,1)S(1)}, u32[]{:S(2)}, u32[]{:S(2)}) collective-permute-start(bf16[128,1024]{1,0:T(8,128)(2,1)S(1)} %get-tuple-element.62), channel_id=1, source_target_pairs={{0,8},{4,12},{8,0},{12,4},{1,9},{5,13},{9,1},{13,5},{2,10},{6,14},... | collective-permute-start | bytes 786440 | tf_op jit(solution)/shard_map/ppermute | solution.py:28
  423.6 177.8 %all-gather.5.cloned.1.call-start = ((), (), s32[]{:S(2)}) async-start(), calls=%async_computation.5 | async-start | bytes 3932160 | tf_op jit(solution)/shard_map/all_gather | solution.py:411
  427.1 26.1 %collective-permute-start.57 = (bf16[4,64,1024]{2,1,0:T(8,128)(2,1)S(1)}, bf16[4,64,1024]{2,1,0:T(8,128)(2,1)S(1)}, u32[]{:S(2)}, u32[]{:S(2)}) collective-permute-start(bf16[4,64,1024]{2,1,0:T(8,128)(2,1)S(1)} %add_convert_fusion.1.refs_6_), channel_id=1, source_target_pairs={{16,2},{17,3},{18,0},{19,1},{20,6},{21,7},{22,4},{23,5},{24,10},{2... | collective-permute-start | bytes 1572872 | tf_op jit(solution)/shard_map/ppermute | solution.py:36
  469.4 23.2 %collective-permute-start.62 = (bf16[128,1024]{1,0:T(8,128)(2,1)S(1)}, bf16[128,1024]{1,0:T(8,128)(2,1)S(1)}, u32[]{:S(2)}, u32[]{:S(2)}) collective-permute-start(bf16[128,1024]{1,0:T(8,128)(2,1)S(1)} %get-tuple-element.58), channel_id=1, source_target_pairs={{0,8},{4,12},{8,0},{12,4},{1,9},{5,13},{9,1},{13,5},{2,10},{6,14},... | collective-permute-start | bytes 786440 | tf_op jit(solution)/shard_map/ppermute | solution.py:28
  471.4 21.3 %collective-permute-start.61 = (bf16[128,1024]{1,0:T(8,128)(2,1)S(1)}, bf16[128,1024]{1,0:T(8,128)(2,1)S(1)}, u32[]{:S(2)}, u32[]{:S(2)}) collective-permute-start(bf16[128,1024]{1,0:T(8,128)(2,1)S(1)} %get-tuple-element.59), channel_id=1, source_target_pairs={{0,12},{4,8},{8,4},{12,0},{1,13},{5,9},{9,5},{13,1},{2,14},{6,10},... | collective-permute-start | bytes 786440 | tf_op jit(solution)/shard_map/ppermute | solution.py:28
  521.3 80.2 %collective-permute-start.73 = (bf16[512,1024]{1,0:T(8,128)(2,1)S(1)}, bf16[512,1024]{1,0:T(8,128)(2,1)}, u32[]{:S(2)}, u32[]{:S(2)}) collective-permute-start(bf16[512,1024]{1,0:T(8,128)(2,1)S(1)} %bitcast.303), channel_id=1, source_target_pairs={{0,16},{1,17},{2,18},{3,19},{16,0},{17,1},{18,2},{19,3},{4,20},{5,... | collective-permute-start | bytes 3145736 | tf_op jit(solution)/shard_map/ppermute | solution.py:36
  (134 other events, 1016.5 us)
Sparse Core Ops, SparseCore 0:
  53.1 60.0 reduce-scatter.2
  115.5 79.8 reduce-scatter.4
  423.7 47.4 all-gather.2
  499.4 64.3 all-gather.4

commit v4 on v3

--- a/solution.py
+++ b/solution.py
@@ -67,15 +67,30 @@
     )
 
 
-def to_columns(rows, parity, sections):
+def gate(x, *after):
+    anywhere = pl.BlockSpec(memory_space=pl.ANY)
+
+    def kernel(*refs):
+        pass
+
+    return pl.pallas_call(
+        kernel,
+        out_shape=jax.ShapeDtypeStruct(x.shape, x.dtype),
+        in_specs=[anywhere] * (1 + len(after)),
+        out_specs=anywhere,
+        input_output_aliases={0: 0},
+        name="gate",
+    )(x, *after)
+
+
+def to_columns(rows, parity, sections, after=()):
     n = lax.axis_size("dp")
     me = lax.axis_index("dp")
-    k, seq, full = rows.shape
-    half, width = seq // 2, full // n
-    mine = [
-        lax.dynamic_slice(rows, (0, parity * half, (me ^ s) * width), (k, half, width))
-        for s in range(n)
-    ]
+    half, width = rows.shape[1] // 2, rows.shape[2] // n
+    rows = lax.dynamic_slice_in_dim(rows, parity * half, half, 1)
+    if after:
+        rows = gate(rows, *after)
+    mine = [lax.dynamic_slice_in_dim(rows, (me ^ s) * width, width, 2) for s in range(n)]
     got = {s: dp_shift(mine[s], s, sections) for s in range(n - 1, 0, -1)}
     return in_order([mine[0]] + [got[s] for s in range(1, n)])
 
@@ -97,7 +112,7 @@
     own = jnp.where(lax.axis_index("section") == 0, total.astype(F32), 0.0)
     mine = functools.reduce(jnp.add, [g.astype(F32) for g in got], own).astype(BF16)
     other = mp_shift(mine, 1, targets)
-    return halves(mine, other, parity), total
+    return halves(mine, other, parity)
 
 
 def add_up(sources, start):
@@ -180,8 +195,7 @@
             gv_ref[:, c : c + PAIR] = gv
             send_ref[:, c : c + PAIR] = gq
             send_ref[:, width + c : width + c + PAIR] = ctx if decoder else gk
-            if send_ref.shape[1] > 2 * width:
-                send_ref[:, 2 * width + c : 2 * width + c + PAIR] = gk if decoder else gv
+            send_ref[:, 2 * width + c : 2 * width + c + PAIR] = gk if decoder else gv
             grams[0] += mm(gq, gq, NT)
             if decoder:
                 grams[1] += mm(ctx, ctx, NT)
@@ -222,11 +236,11 @@
     return call_attention(fwd_kernel, info, operands, (rows,), flops, "attend", after)[0]
 
 
-def attend_back(info, operands, seq, width, decoder, slots, after=()):
+def attend_back(info, operands, seq, width, decoder, after=()):
     outs = (
         jax.ShapeDtypeStruct((seq, width), BF16),
         jax.ShapeDtypeStruct((seq, width), BF16),
-        jax.ShapeDtypeStruct((seq, slots * width), BF16),
+        jax.ShapeDtypeStruct((seq, 3 * width), BF16),
         jax.ShapeDtypeStruct((2, seq, seq), F32),
     )
 
@@ -237,77 +251,64 @@
     return call_attention(kernel, info, operands, outs, flops, "attend_back", after)
 
 
-def wgrad_kernel(mb, chunk, scale, clip, info, *refs):
-    x1, xa, xb = refs[:mb], refs[mb : 2 * mb], refs[2 * mb : 3 * mb]
-    send, kept = refs[3 * mb : 4 * mb], refs[4 * mb : 5 * mb]
-    noise, out = refs[-2:]
+def wgrad_kernel(count, chunk, scale, start, clip, info, x1, xa, xb, send, kept, base, out):
     width = out.shape[2]
-    back = [(ref, 0) for ref in refs[5 * mb : -2]] + [(send[-1], 2 * width)]
-    kept = [(ref, 0) for ref in kept]
-    first = [(ref, 0) for ref in send]
-    second = [(ref, width) for ref in send]
-    count = x1[0].shape[0] // chunk
     is_dec = info[0] == 1
 
-    def clipped(group):
-        return [
-            jnp.concatenate(
-                [
-                    (ref[i * chunk : (i + 1) * chunk].astype(F32) * clip[b * count + i]).astype(BF16)
-                    for i in range(count)
-                ],
-                axis=0,
-            )
-            for b, ref in enumerate(group)
+    def clipped(ref):
+        parts = [
+            (ref[i * chunk : (i + 1) * chunk].astype(F32) * clip[i]).astype(BF16)
+            for i in range(count)
         ]
-
-    def put(slot, lefts, rights):
-        total = functools.reduce(
-            jnp.add, [mm(x, y[:, c : c + width], TN) for x, (y, c) in zip(lefts, rights)]
-        )
-        out[:, slot, :] = (total + noise[:, slot, :]) * scale
+        return jnp.concatenate(parts, axis=0)
+
+    def put(slot, left, right, first):
+        total = mm(left, right[:, first : first + width], TN)
+        if start:
+            out[:, slot, :] = (total + base[:, slot, :]) * scale
+        else:
+            out[:, slot, :] = total * scale + base[:, slot, :]
 
     l1, la, lb = clipped(x1), clipped(xa), clipped(xb)
-    put(0, l1, first)
+    put(0, l1, send, 0)
 
     @pl.when(is_dec)
     def decoder():
-        put(1, lb, back)
-        put(2, lb, kept)
-        put(3, la, second)
+        put(1, lb, send, 2 * width)
+        put(2, lb, kept, 0)
+        put(3, la, send, width)
 
     @pl.when(jnp.logical_not(is_dec))
     def encoder():
-        put(1, la, second)
-        put(2, l1, back)
-        put(3, lb, kept)
-
-
-def wgrad(clip, info, x1, xa, xb, send, kept, back, noise, chunk, examples):
-    mb = len(x1)
-    tokens, depth = x1[0].shape
-    width = noise.shape[2]
+        put(1, la, send, width)
+        put(2, l1, send, 2 * width)
+        put(3, lb, kept, 0)
+
+
+def wgrad(clip, info, x1, xa, xb, send, kept, base, chunk, examples, start):
+    tokens, depth = x1.shape
+    width = base.shape[2]
     block = 256
     smem = pl.BlockSpec(memory_space=pltpu.SMEM)
     left = pl.BlockSpec((tokens, block), lambda i: (0, i))
     wide = pl.BlockSpec((block, 4, width), lambda i: (i, 0, 0))
     once = [
-        pl.BlockSpec(y.shape, lambda i: (0, 0), pipeline_mode=pl.Buffered(1)) for y in send + kept + back
+        pl.BlockSpec(y.shape, lambda i: (0, 0), pipeline_mode=pl.Buffered(1)) for y in (send, kept)
     ]
     return pl.pallas_call(
-        functools.partial(wgrad_kernel, mb, chunk, 1.0 / examples),
+        functools.partial(wgrad_kernel, tokens // chunk, chunk, 1.0 / examples, start),
         grid=(depth // block,),
-        out_shape=jax.ShapeDtypeStruct(noise.shape, F32),
-        in_specs=[smem, smem] + [left] * (3 * mb) + once + [wide],
+        out_shape=jax.ShapeDtypeStruct(base.shape, F32),
+        in_specs=[smem, smem, left, left, left] + once + [wide],
         out_specs=wide,
         compiler_params=pltpu.CompilerParams(vmem_limit_bytes=56 << 20),
         cost_estimate=pl.CostEstimate(
-            flops=8 * mb * tokens * depth * width,
-            bytes_accessed=depth * 4 * width * 8 + mb * tokens * width * 8,
+            flops=8 * tokens * depth * width,
+            bytes_accessed=depth * 4 * width * 8 + tokens * width * 8,
             transcendentals=0,
         ),
         name="weight_gradient",
-    )(clip, info, *x1, *xa, *xb, *send, *kept, *back, noise)
+    )(clip, info, x1, xa, xb, send, kept, base)
 
 
 def per_device(inputs, norm_gains, weights, cotangent, lengths, dp_noise):
@@ -342,7 +343,7 @@
     inv_all = gather(inv, both)
     raw_half, x = [], []
     for b in range(mb):
-        mine = to_columns(inputs[0, b : b + 1], parity, both)[:, 0]
+        mine = to_columns(inputs[0, b : b + 1], parity, both, raw_half[-1:])[:, 0]
         raw = halves(mine, mp_shift(mine, 1, both), parity)
         raw_half.append(mine)
         x.append(rows_of((raw.astype(F32) * inv_all[:, b, :, None] * gain_cols).astype(BF16)))
@@ -369,49 +370,45 @@
             )
         )
     w_relay = jnp.where(is_dec, w[2], mp_shift(w[1], 0, dec, flip=True))
-    ctx_all, enc_out, kv_parts, keys = [], [], [], []
+    ctx_all, enc_out, kv_terms, kv_parts, keys = [], [], [], [], []
     for b in range(mb):
         qkv = [[(first[b], i * inner)] for i in range(3)]
-        ctx = attend(info(section == 0, b), qkv, seq, inner, keys[-1:])
-        ctx_all.append(rows_of(gather(ctx, enc)))
+        ctx = attend(info(section == 0, b), qkv, seq, inner, kv_terms[-1:])
+        ctx = rows_of(gather(ctx, enc))
+        ctx_all.append(gate(ctx, keys[-1]) if keys else ctx)
         terms = mm(ctx_all[b], w[3], NT).reshape(n, seq, depth)
-        enc_out.append(relay(terms, raw_half[b], enc, 0, both)[0])
+        enc_out.append(relay(terms, raw_half[b], enc, 0, both))
         terms = mm(rows_of(enc_out[b]), w_relay).astype(BF16).reshape(n, seq, inner)
+        kv_terms.append(terms)
         kv_parts.append(to_owner(terms, both))
-        keys.append(functools.reduce(jnp.add, [k.astype(F32) for k in kv_parts[b]]).astype(BF16))
-    relay_all, grad_enc, dec_send, dec_gram, dec_gk = [], [], [], [], []
-    slots = [2] * (mb - 1) + [3]
+        key = functools.reduce(jnp.add, [k.astype(F32) for k in kv_parts[b]]).astype(BF16)
+        keys.append(mp_shift(key, 0, enc, flip=True))
+    relay_all, grad_enc, dec_send, dec_gram, ctx_terms = [], [], [], [], []
     for b in range(mb):
         operands = [
             [(first[b], 0)],
-            [(mp_shift(keys[b], 0, enc, flip=True), 0)],
+            [(keys[b], 0)],
             [(part, 0) for part in kv_parts[b]],
             [(first[mb - 1], (1 + b) * inner)],
         ]
-        gk, gv, send, gram = attend_back(
-            info(section == 1, b), operands, seq, inner, True, slots[b]
-        )
+        gk, gv, send, gram = attend_back(info(section == 1, b), operands, seq, inner, True)
         rows = jnp.where(is_dec, gv, mp_shift(gk, 0, dec, flip=True))
-        relay_all.append(rows_of(gather(rows, both)))
+        rows = rows_of(gather(rows, both))
+        relay_all.append(gate(rows, ctx_terms[-1]) if ctx_terms else rows)
         terms = mm(relay_all[b], w_relay, NT).reshape(n, seq, depth)
-        grad, relayed = relay(terms, None, both, 1, enc)
-        grad_enc.append(grad)
+        grad_enc.append(relay(terms, None, both, 1, enc))
+        terms = mm(rows_of(grad_enc[b]), w[3]).astype(BF16)
+        ctx_terms.append(terms.reshape(n, seq, inner))
         dec_send.append(send)
         dec_gram.append(gram)
-    send_all, enc_gram, back_all = [], [], []
-    for b in range(mb):
-        gctx = to_owner(mm(rows_of(grad_enc[b]), w[3]).astype(BF16).reshape(n, seq, inner), enc)
+    send_all, enc_gram = [], []
+    for b in range(mb):
+        gctx = to_owner(ctx_terms[b], enc)
         operands = [[(first[b], i * inner)] for i in range(3)] + [[(part, 0) for part in gctx]]
-        after = [relayed] if b < mb - 1 else []
-        _, gv, send, gram = attend_back(
-            info(section == 0, b), operands, seq, inner, False, slots[b], after
-        )
+        _, _, send, gram = attend_back(info(section == 0, b), operands, seq, inner, False)
         enc_gram.append(gram)
         send = jnp.where(is_dec, dec_send[b], send)
         send_all.append(lax.all_gather(send, "dp", axis=0, tiled=True))
-        if b < mb - 1:
-            gv_all = rows_of(gather(mp_shift(gv, 0, enc, flip=True), dec))
-            back_all.append(mp_shift(jnp.where(is_dec, gv_all, relay_all[b]), 0, both, flip=True))
     normed = (own32 * inv[..., None] * gain).astype(BF16)
     gram_x = jnp.einsum("btd,bud->btu", normed, normed, preferred_element_type=F32)
     gram_cot = jnp.einsum("btd,bud->btu", cot, cot, preferred_element_type=F32)
@@ -436,12 +433,15 @@
     bound = jnp.sqrt(jnp.float32(8.0 * D * HEADS * HEAD))
     clip_all = bound / (jnp.sqrt(sq) + 0.01 * bound)
     clip = lax.dynamic_slice_in_dim(clip_all, me, 1, 1)[:, 0]
-    clip_all = clip_all.reshape(-1)
-    xa = [jnp.where(is_dec, c, r) for c, r in zip(cot_cols, x)]
-    xb = [rows_of(jnp.where(is_dec, o, g)) for o, g in zip(enc_out, grad_enc)]
-    kept = [jnp.where(is_dec, r, c) for r, c in zip(relay_all, ctx_all)]
     flag = section.astype(jnp.int32)[None]
-    out = wgrad(clip_all, flag, x, xa, xb, send_all, kept, back_all, dp_noise[0], seq, mb * n)
+    out = dp_noise[0]
+    for b in range(mb):
+        xa = jnp.where(is_dec, cot_cols[b], x[b])
+        xb = rows_of(jnp.where(is_dec, enc_out[b], grad_enc[b]))
+        kept = jnp.where(is_dec, relay_all[b], ctx_all[b])
+        out = wgrad(
+            clip_all[b], flag, x[b], xa, xb, send_all[b], kept, out, seq, mb * n, b == 0
+        )
     return (out[None], clip)
 
 

time: 642 us -> 579 us (0.902)
  starting transfers between devices: 185 us -> 128 us
  waiting for transfers between devices: 274 us -> 249 us
  Pallas kernels: 39.5 us -> 53.5 us
    ppermute x33 -> x31, starting transfers between devices: 98.7 us -> 45.3 us  [mp_shift(): return lax.ppermute(x, ('section', 'mp'), pairs)]
    ppermute x41 -> x38, waiting for transfers between devices: 135 us -> 111 us  [dp_shift(): return lax.ppermute(x, ('section', 'dp'), pairs)]
    pallas_call x1 -> x5, Pallas kernels: 24 us -> 37.6 us  [the longest x2 37.6 us: wgrad(): pl.pallas_call(functools.partial(wgrad_kernel, tokens // chunk, chunk, 1....]
    unnamed x161 -> x135, local copies, waits for them, and re-layouts: 23.6 us -> 19.3 us
    ppermute x33 -> x31, waiting for transfers between devices: 106 us -> 102 us  [mp_shift(): return lax.ppermute(x, ('section', 'mp'), pairs)]
    ppermute x41 -> x38, starting transfers between devices: 85.7 us -> 81.9 us  [dp_shift(): return lax.ppermute(x, ('section', 'dp'), pairs)]
  transfers between devices with their start and end apart: 78 -> 73, of which waited for: 40 -> 35; matrix products, arithmetic and copies ran while one was open for 13% -> 17% of each run, Pallas kernels for 1% -> 6%
where the time goes in v4:
time: 579 us; the launch traced here: 569 us
  waiting for transfers between devices  249 us (43%)
  starting transfers between devices  128 us (22%)
  Pallas kernels  53.5 us (9%)
  other arithmetic  46.9 us (8%)
  matrix products  42.8 us (7%)
  local copies, waits for them, and re-layouts  31.3 us (5%)
  between operations  18.5 us (3%)
    ppermute x38, waiting for transfers between devices, dp_shift(): return lax.ppermute(x, ('section', 'dp'), pairs)  111 us
    ppermute x31, waiting for transfers between devices, mp_shift(): return lax.ppermute(x, ('section', 'mp'), pairs)  102 us
    ppermute x38, starting transfers between devices, dp_shift(): return lax.ppermute(x, ('section', 'dp'), pairs)  81.9 us
    ppermute x31, starting transfers between devices, mp_shift(): return lax.ppermute(x, ('section', 'mp'), pairs)  45.3 us
    pallas_call x2, Pallas kernels, wgrad(): pl.pallas_call(functools.partial(wgrad_kernel, tokens // chunk, chunk, 1....  37.6 us
    dot_general x14, matrix products, mm(): return lax.dot_general(left, right, dims, preferred_element_type=F32)  35.7 us
    reduce_scatter x2, waiting for transfers between devices, per_device(): lax.psum_scatter(parts.reshape(n, seq, 3 * inner), 'dp', scatter_dimensio...  32.5 us
    unnamed x135, local copies, waits for them, and re-layouts  19.3 us
  transfers between devices with their start and end apart: 73, of which 35 were waited for; matrix products, arithmetic and copies ran while one was open for 17% of the time, Pallas kernels for 6%

profile of v4, /device:TPU:0, one launch (start us, length us, event | category | flops | bytes accessed | tf_op | source)
XLA Modules:
  0.0 569.4 jit_solution(13052709584909645101)
XLA Ops:
  18.6 6.6 %collective-permute-done.1 = bf16[1,64,1024]{2,1,0:T(8,128)(2,1)S(1)} collective-permute-done((bf16[1,64,1024]{2,1,0:T(8,128)(2,1)S(1)}, bf16[1,64,1024]{2,1,0:T(8,128)(2,1)S(1)}, u32[]{:S(2)}, u32[]{:S(2)}) %collective-permute-start.1) | collective-permute-done | bytes 131104 | tf_op jit(solution)/shard_map/ppermute | solution.py:28
  35.0 9.7 %copy.26 = bf16[1,1024,4,1024]{3,1,2,0:T(8,128)(2,1)} copy(bf16[1,1024,4,1024]{3,2,1,0:T(4,128)(2,1)} %param.8) | data formatting | bytes 16777216 | tf_op args[2]
  86.5 32.5 %reduce-scatter.3.cloned.1.call-done = bf16[1,128,3072]{2,1,0:T(8,128)(2,1)} async-done(((bf16[4,128,3072]{2,1,0:T(8,128)(2,1)}), bf16[1,128,3072]{2,1,0:T(8,128)(2,1)}) %reduce-scatter.3.cloned.1.call-update) | async-done | bytes 786448 | tf_op jit(solution)/shard_map/reduce_scatter | solution.py:368
  136.4 13.1 %collective-permute-done.8 = bf16[128,1024]{1,0:T(8,128)(2,1)S(1)} collective-permute-done((bf16[128,1024]{1,0:T(8,128)(2,1)S(1)}, bf16[128,1024]{1,0:T(8,128)(2,1)S(1)}, u32[]{:S(2)}, u32[]{:S(2)}) %collective-permute-start.8) | collective-permute-done | bytes 262176 | tf_op jit(solution)/shard_map/ppermute | solution.py:28
  164.2 9.8 %collective-permute-done.13 = bf16[4,64,1024]{2,1,0:T(8,128)(2,1)S(1)} collective-permute-done((bf16[4,64,1024]{2,1,0:T(8,128)(2,1)S(1)}, bf16[4,64,1024]{2,1,0:T(8,128)(2,1)S(1)}, u32[]{:S(2)}, u32[]{:S(2)}) %collective-permute-start.13) | collective-permute-done | bytes 524320 | tf_op jit(solution)/shard_map/ppermute | solution.py:36
  175.1 10.4 %collective-permute-done.11 = bf16[4,64,1024]{2,1,0:T(8,128)(2,1)S(1)} collective-permute-done((bf16[4,64,1024]{2,1,0:T(8,128)(2,1)S(1)}, bf16[4,64,1024]{2,1,0:T(8,128)(2,1)S(1)}, u32[]{:S(2)}, u32[]{:S(2)}) %collective-permute-start.11) | collective-permute-done | bytes 524320 | tf_op jit(solution)/shard_map/ppermute | solution.py:36
  186.0 7.4 %collective-permute-done.15 = bf16[1024,1024]{1,0:T(8,128)(2,1)} collective-permute-done((bf16[1024,1024]{1,0:T(8,128)(2,1)}, bf16[1024,1024]{1,0:T(8,128)(2,1)}, u32[]{:S(2)}, u32[]{:S(2)}) %collective-permute-start.15) | collective-permute-done | bytes 2097184 | tf_op jit(solution)/shard_map/ppermute | solution.py:36
  217.8 18.2 %collective-permute-done.17.refs_5_ = bf16[128,1024]{1,0:T(8,128)(2,1)S(1)} collective-permute-done((bf16[128,1024]{1,0:T(8,128)(2,1)S(1)}, bf16[128,1024]{1,0:T(8,128)(2,1)S(1)}, u32[]{:S(2)}, u32[]{:S(2)}) %collective-permute-start.17) | collective-permute-done | bytes 262176 | tf_op jit(solution)/shard_map/ppermute | solution.py:28
  237.5 9.3 %collective-permute-done.41 = bf16[128,1024]{1,0:T(8,128)(2,1)S(1)} collective-permute-done((bf16[128,1024]{1,0:T(8,128)(2,1)S(1)}, bf16[128,1024]{1,0:T(8,128)(2,1)S(1)}, u32[]{:S(2)}, u32[]{:S(2)}) %collective-permute-start.41) | collective-permute-done | bytes 262176 | tf_op jit(solution)/shard_map/ppermute | solution.py:28
  256.2 9.3 %collective-permute-done.28 = bf16[128,1024]{1,0:T(8,128)(2,1)S(1)} collective-permute-done((bf16[128,1024]{1,0:T(8,128)(2,1)S(1)}, bf16[128,1024]{1,0:T(8,128)(2,1)S(1)}, u32[]{:S(2)}, u32[]{:S(2)}) %collective-permute-start.28) | collective-permute-done | bytes 262176 | tf_op jit(solution)/shard_map/ppermute | solution.py:36
  279.2 10.3 %collective-permute-done.30 = bf16[128,1024]{1,0:T(8,128)(2,1)S(1)} collective-permute-done((bf16[128,1024]{1,0:T(8,128)(2,1)S(1)}, bf16[128,1024]{1,0:T(8,128)(2,1)S(1)}, u32[]{:S(2)}, u32[]{:S(2)}) %collective-permute-start.30) | collective-permute-done | bytes 262176 | tf_op jit(solution)/shard_map/ppermute | solution.py:28
  306.7 6.7 %collective-permute-done.35 = bf16[4,64,1024]{2,1,0:T(8,128)(2,1)S(1)} collective-permute-done((bf16[4,64,1024]{2,1,0:T(8,128)(2,1)S(1)}, bf16[4,64,1024]{2,1,0:T(8,128)(2,1)S(1)}, u32[]{:S(2)}, u32[]{:S(2)}) %collective-permute-start.35) | collective-permute-done | bytes 524320 | tf_op jit(solution)/shard_map/ppermute | solution.py:36
  316.3 11.5 %collective-permute-done.33 = bf16[4,64,1024]{2,1,0:T(8,128)(2,1)S(1)} collective-permute-done((bf16[4,64,1024]{2,1,0:T(8,128)(2,1)S(1)}, bf16[4,64,1024]{2,1,0:T(8,128)(2,1)S(1)}, u32[]{:S(2)}, u32[]{:S(2)}) %collective-permute-start.33) | collective-permute-done | bytes 524320 | tf_op jit(solution)/shard_map/ppermute | solution.py:36
  360.7 20.4 %collective-permute-done.38.refs_4_ = bf16[128,1024]{1,0:T(8,128)(2,1)S(1)} collective-permute-done((bf16[128,1024]{1,0:T(8,128)(2,1)S(1)}, bf16[128,1024]{1,0:T(8,128)(2,1)S(1)}, u32[]{:S(2)}, u32[]{:S(2)}) %collective-permute-start.38) | collective-permute-done | bytes 262176 | tf_op jit(solution)/shard_map/ppermute | solution.py:28
  381.0 5.4 attend_back.5
  387.7 8.2 %collective-permute-done.54 = bf16[128,1024]{1,0:T(8,128)(2,1)} collective-permute-done((bf16[128,1024]{1,0:T(8,128)(2,1)}, bf16[128,1024]{1,0:T(8,128)(2,1)}, u32[]{:S(2)}, u32[]{:S(2)}) %collective-permute-start.54) | collective-permute-done | bytes 262176 | tf_op jit(solution)/shard_map/ppermute | solution.py:28
  409.4 10.7 %collective-permute-done.59 = bf16[4,64,1024]{2,1,0:T(8,128)(2,1)S(1)} collective-permute-done((bf16[4,64,1024]{2,1,0:T(8,128)(2,1)S(1)}, bf16[4,64,1024]{2,1,0:T(8,128)(2,1)S(1)}, u32[]{:S(2)}, u32[]{:S(2)}) %collective-permute-start.59) | collective-permute-done | bytes 524320 | tf_op jit(solution)/shard_map/ppermute | solution.py:36
  423.5 11.0 %collective-permute-done.57 = bf16[4,64,1024]{2,1,0:T(8,128)(2,1)S(1)} collective-permute-done((bf16[4,64,1024]{2,1,0:T(8,128)(2,1)S(1)}, bf16[4,64,1024]{2,1,0:T(8,128)(2,1)S(1)}, u32[]{:S(2)}, u32[]{:S(2)}) %collective-permute-start.57) | collective-permute-done | bytes 524320 | tf_op jit(solution)/shard_map/ppermute | solution.py:36
  462.9 8.1 %collective-permute-done.61.refs_3_ = bf16[128,1024]{1,0:T(8,128)(2,1)S(1)} collective-permute-done((bf16[128,1024]{1,0:T(8,128)(2,1)S(1)}, bf16[128,1024]{1,0:T(8,128)(2,1)S(1)}, u32[]{:S(2)}, u32[]{:S(2)}) %collective-permute-start.61) | collective-permute-done | bytes 262176 | tf_op jit(solution)/shard_map/ppermute | solution.py:28
  471.0 5.7 attend_back.7
  477.7 5.6 bitcast_select_fusion.1
  502.8 5.5 collective-permute-start.66
  520.9 18.8 %weight_gradient.2.base = f32[1024,4,1024]{2,1,0:T(4,128)} custom-call(f32[4]{0:T(128)} %get-tuple-element.109.clip, s32[1]{0:T(128)} %bitcast.105.info, bf16[512,1024]{1,0:T(8,128)(2,1)} %get-tuple-element.33.x1, bf16[512,1024]{1,0:T(8,128)(2,1)} %get-tuple-element.32.xa, bf16[512,1024]{1,0:T(8,128)(2,1)} %broadcast_select_fusion.1.xb, ...), custom_call_target="tpu_custom_call" | custom-call | flops 4294967296 | bytes 37748736 | tf_op jit(solution)/shard_map/weight_gradient/pallas_call | solution.py:298
  543.7 18.7 %weight_gradient.3 = f32[1024,4,1024]{2,1,0:T(4,128)} custom-call(f32[4]{0:T(128)} %get-tuple-element.110.clip, s32[1]{0:T(128)} %bitcast.105.info, bf16[512,1024]{1,0:T(8,128)(2,1)} %get-tuple-element.98.x1, bf16[512,1024]{1,0:T(8,128)(2,1)} %get-tuple-element.97.xa, bf16[512,1024]{1,0:T(8,128)(2,1)} %broadcast_select_fusion.3.xb, ...), custom_call_target="tpu_custom_call" | custom-call | flops 4294967296 | bytes 37748736 | tf_op jit(solution)/shard_map/weight_gradient/pallas_call | solution.py:298
  (389 shorter events, 277.9 us)
Async XLA Ops:
  7.2 111.8 %reduce-scatter.3.cloned.1.call-start = ((), (), s32[]{:S(2)}) async-start(), calls=%async_computation.2 | async-start | bytes 3932160 | tf_op jit(solution)/shard_map/reduce_scatter | solution.py:368
  58.3 144.6 %reduce-scatter.5.cloned.1.call-start = ((), (), s32[]{:S(2)}) async-start(), calls=%async_computation.3 | async-start | bytes 3932160 | tf_op jit(solution)/shard_map/reduce_scatter | solution.py:368
  85.1 435.8 %all-gather.5.cloned.1.call-start = ((), (), s32[]{:S(2)}) async-start(), calls=%async_computation.5 | async-start | bytes 3932160 | tf_op jit(solution)/shard_map/all_gather | solution.py:411
  125.9 23.6 %collective-permute-start.8 = (bf16[128,1024]{1,0:T(8,128)(2,1)S(1)}, bf16[128,1024]{1,0:T(8,128)(2,1)S(1)}, u32[]{:S(2)}, u32[]{:S(2)}) collective-permute-start(bf16[128,1024]{1,0:T(8,128)(2,1)S(1)} %attend.2), channel_id=1, source_target_pairs={{0,8},{4,12},{8,0},{12,4},{1,9},{5,13},{9,1},{13,5},{2,10},{6,14},... | collective-permute-start | bytes 786440 | tf_op jit(solution)/shard_map/ppermute | solution.py:28
  128.1 21.3 %collective-permute-start.7 = (bf16[128,1024]{1,0:T(8,128)(2,1)S(1)}, bf16[128,1024]{1,0:T(8,128)(2,1)S(1)}, u32[]{:S(2)}, u32[]{:S(2)}) collective-permute-start(bf16[128,1024]{1,0:T(8,128)(2,1)S(1)} %attend.2), channel_id=1, source_target_pairs={{0,4},{4,0},{8,12},{12,8},{1,5},{5,1},{9,13},{13,9},{2,6},{6,2},{1... | collective-permute-start | bytes 786440 | tf_op jit(solution)/shard_map/ppermute | solution.py:28
  135.1 58.4 %collective-permute-start.15 = (bf16[1024,1024]{1,0:T(8,128)(2,1)}, bf16[1024,1024]{1,0:T(8,128)(2,1)}, u32[]{:S(2)}, u32[]{:S(2)}) collective-permute-start(bf16[1024,1024]{1,0:T(8,128)(2,1)} %slice_bitcast_fusion.3), channel_id=1, source_target_pairs={{16,0},{17,1},{18,2},{19,3},{20,4},{21,5},{22,6},{23,7},{24,8},{25... | collective-permute-start | bytes 6291464 | tf_op jit(solution)/shard_map/ppermute | solution.py:36
  162.9 22.7 %collective-permute-start.11 = (bf16[4,64,1024]{2,1,0:T(8,128)(2,1)S(1)}, bf16[4,64,1024]{2,1,0:T(8,128)(2,1)S(1)}, u32[]{:S(2)}, u32[]{:S(2)}) collective-permute-start(bf16[4,64,1024]{2,1,0:T(8,128)(2,1)S(1)} %add_convert_fusion.7), channel_id=1, source_target_pairs={{0,18},{1,19},{2,16},{3,17},{4,22},{5,23},{6,20},{7,21},{8,26},{9,... | collective-permute-start | bytes 1572872 | tf_op jit(solution)/shard_map/ppermute | solution.py:36
  201.7 34.3 %collective-permute-start.17 = (bf16[128,1024]{1,0:T(8,128)(2,1)S(1)}, bf16[128,1024]{1,0:T(8,128)(2,1)S(1)}, u32[]{:S(2)}, u32[]{:S(2)}) collective-permute-start(bf16[128,1024]{1,0:T(8,128)(2,1)S(1)} %get-tuple-element.68), channel_id=1, source_target_pairs={{0,8},{4,12},{8,0},{12,4},{16,24},{20,28},{24,16},{28,20},{1,9},{5... | collective-permute-start | bytes 786440 | tf_op jit(solution)/shard_map/ppermute | solution.py:28
  206.2 31.3 %collective-permute-start.42 = (bf16[128,1024]{1,0:T(8,128)(2,1)S(1)}, bf16[128,1024]{1,0:T(8,128)(2,1)S(1)}, u32[]{:S(2)}, u32[]{:S(2)}) collective-permute-start(bf16[128,1024]{1,0:T(8,128)(2,1)S(1)} %attend.3), channel_id=1, source_target_pairs={{0,12},{4,8},{8,4},{12,0},{1,13},{5,9},{9,5},{13,1},{2,14},{6,10},... | collective-permute-start | bytes 786440 | tf_op jit(solution)/shard_map/ppermute | solution.py:28
  210.7 36.1 %collective-permute-start.41 = (bf16[128,1024]{1,0:T(8,128)(2,1)S(1)}, bf16[128,1024]{1,0:T(8,128)(2,1)S(1)}, u32[]{:S(2)}, u32[]{:S(2)}) collective-permute-start(bf16[128,1024]{1,0:T(8,128)(2,1)S(1)} %attend.3), channel_id=1, source_target_pairs={{0,8},{4,12},{8,0},{12,4},{1,9},{5,13},{9,1},{13,5},{2,10},{6,14},... | collective-permute-start | bytes 786440 | tf_op jit(solution)/shard_map/ppermute | solution.py:28
  212.9 33.9 %collective-permute-start.40 = (bf16[128,1024]{1,0:T(8,128)(2,1)S(1)}, bf16[128,1024]{1,0:T(8,128)(2,1)S(1)}, u32[]{:S(2)}, u32[]{:S(2)}) collective-permute-start(bf16[128,1024]{1,0:T(8,128)(2,1)S(1)} %attend.3), channel_id=1, source_target_pairs={{0,4},{4,0},{8,12},{12,8},{1,5},{5,1},{9,13},{13,9},{2,6},{6,2},{1... | collective-permute-start | bytes 786440 | tf_op jit(solution)/shard_map/ppermute | solution.py:28
  268.1 21.4 %collective-permute-start.30 = (bf16[128,1024]{1,0:T(8,128)(2,1)S(1)}, bf16[128,1024]{1,0:T(8,128)(2,1)S(1)}, u32[]{:S(2)}, u32[]{:S(2)}) collective-permute-start(bf16[128,1024]{1,0:T(8,128)(2,1)S(1)} %broadcast_select_fusion.9), channel_id=1, source_target_pairs={{0,8},{4,12},{8,0},{12,4},{16,24},{20,28},{24,16},{28,20},{1,9},{5... | collective-permute-start | bytes 786440 | tf_op jit(solution)/shard_map/ppermute | solution.py:28
  268.1 21.4 %collective-permute-start.29 = (bf16[128,1024]{1,0:T(8,128)(2,1)S(1)}, bf16[128,1024]{1,0:T(8,128)(2,1)S(1)}, u32[]{:S(2)}, u32[]{:S(2)}) collective-permute-start(bf16[128,1024]{1,0:T(8,128)(2,1)S(1)} %broadcast_select_fusion.9), channel_id=1, source_target_pairs={{0,4},{4,0},{8,12},{12,8},{16,20},{20,16},{24,28},{28,24},{1,5},{5... | collective-permute-start | bytes 786440 | tf_op jit(solution)/shard_map/ppermute | solution.py:28
  270.3 22.6 %collective-permute-start.46 = (bf16[4,64,1024]{2,1,0:T(8,128)(2,1)S(1)}, bf16[4,64,1024]{2,1,0:T(8,128)(2,1)S(1)}, u32[]{:S(2)}, u32[]{:S(2)}) collective-permute-start(bf16[4,64,1024]{2,1,0:T(8,128)(2,1)S(1)} %add_convert_fusion.3), channel_id=1, source_target_pairs={{0,2},{1,3},{2,0},{3,1},{4,6},{5,7},{6,4},{7,5},{8,10},{9,11},{10,... | collective-permute-start | bytes 1572872 | tf_op jit(solution)/shard_map/ppermute | solution.py:36
  300.9 26.8 %collective-permute-start.33 = (bf16[4,64,1024]{2,1,0:T(8,128)(2,1)S(1)}, bf16[4,64,1024]{2,1,0:T(8,128)(2,1)S(1)}, u32[]{:S(2)}, u32[]{:S(2)}) collective-permute-start(bf16[4,64,1024]{2,1,0:T(8,128)(2,1)S(1)} %add_convert_fusion.5), channel_id=1, source_target_pairs={{16,2},{17,3},{18,0},{19,1},{20,6},{21,7},{22,4},{23,5},{24,10},{2... | collective-permute-start | bytes 1572872 | tf_op jit(solution)/shard_map/ppermute | solution.py:36
  304.2 25.8 %collective-permute-start.48 = (bf16[128,1024]{1,0:T(8,128)(2,1)S(1)}, bf16[128,1024]{1,0:T(8,128)(2,1)S(1)}, u32[]{:S(2)}, u32[]{:S(2)}) collective-permute-start(bf16[128,1024]{1,0:T(8,128)(2,1)S(1)} %get-tuple-element.63), channel_id=1, source_target_pairs={{0,12},{4,8},{8,4},{12,0},{16,28},{20,24},{24,20},{28,16},{1,13},{... | collective-permute-start | bytes 786440 | tf_op jit(solution)/shard_map/ppermute | solution.py:28
  306.7 23.3 %collective-permute-start.50 = (bf16[128,1024]{1,0:T(8,128)(2,1)S(1)}, bf16[128,1024]{1,0:T(8,128)(2,1)S(1)}, u32[]{:S(2)}, u32[]{:S(2)}) collective-permute-start(bf16[128,1024]{1,0:T(8,128)(2,1)S(1)} %get-tuple-element.64), channel_id=1, source_target_pairs={{0,4},{4,0},{8,12},{12,8},{16,20},{20,16},{24,28},{28,24},{1,5},{5... | collective-permute-start | bytes 786440 | tf_op jit(solution)/shard_map/ppermute | solution.py:28
  347.3 33.7 %collective-permute-start.38 = (bf16[128,1024]{1,0:T(8,128)(2,1)S(1)}, bf16[128,1024]{1,0:T(8,128)(2,1)S(1)}, u32[]{:S(2)}, u32[]{:S(2)}) collective-permute-start(bf16[128,1024]{1,0:T(8,128)(2,1)S(1)} %get-tuple-element.52), channel_id=1, source_target_pairs={{0,8},{4,12},{8,0},{12,4},{1,9},{5,13},{9,1},{13,5},{2,10},{6,14},... | collective-permute-start | bytes 786440 | tf_op jit(solution)/shard_map/ppermute | solution.py:28
  352.0 29.0 %collective-permute-start.37 = (bf16[128,1024]{1,0:T(8,128)(2,1)S(1)}, bf16[128,1024]{1,0:T(8,128)(2,1)S(1)}, u32[]{:S(2)}, u32[]{:S(2)}) collective-permute-start(bf16[128,1024]{1,0:T(8,128)(2,1)S(1)} %get-tuple-element.53), channel_id=1, source_target_pairs={{0,12},{4,8},{8,4},{12,0},{1,13},{5,9},{9,5},{13,1},{2,14},{6,10},... | collective-permute-start | bytes 786440 | tf_op jit(solution)/shard_map/ppermute | solution.py:28
  356.3 31.4 %collective-permute-start.55 = (bf16[128,1024]{1,0:T(8,128)(2,1)}, bf16[128,1024]{1,0:T(8,128)(2,1)}, u32[]{:S(2)}, u32[]{:S(2)}) collective-permute-start(bf16[128,1024]{1,0:T(8,128)(2,1)} %broadcast_select_fusion.8), channel_id=1, source_target_pairs={{0,12},{4,8},{8,4},{12,0},{16,28},{20,24},{24,20},{28,16},{1,13},{... | collective-permute-start | bytes 786440 | tf_op jit(solution)/shard_map/ppermute | solution.py:28
  358.5 37.4 %collective-permute-start.54 = (bf16[128,1024]{1,0:T(8,128)(2,1)}, bf16[128,1024]{1,0:T(8,128)(2,1)}, u32[]{:S(2)}, u32[]{:S(2)}) collective-permute-start(bf16[128,1024]{1,0:T(8,128)(2,1)} %broadcast_select_fusion.8), channel_id=1, source_target_pairs={{0,8},{4,12},{8,0},{12,4},{16,24},{20,28},{24,16},{28,20},{1,9},{5... | collective-permute-start | bytes 786440 | tf_op jit(solution)/shard_map/ppermute | solution.py:28
  358.5 37.4 %collective-permute-start.53 = (bf16[128,1024]{1,0:T(8,128)(2,1)}, bf16[128,1024]{1,0:T(8,128)(2,1)}, u32[]{:S(2)}, u32[]{:S(2)}) collective-permute-start(bf16[128,1024]{1,0:T(8,128)(2,1)} %broadcast_select_fusion.8), channel_id=1, source_target_pairs={{0,4},{4,0},{8,12},{12,8},{16,20},{20,16},{24,28},{28,24},{1,5},{5... | collective-permute-start | bytes 786440 | tf_op jit(solution)/shard_map/ppermute | solution.py:28
  387.5 156.2 %all-gather.3.cloned.1.call-start = ((), (), s32[]{:S(2)}) async-start(), calls=%async_computation.4 | async-start | bytes 3932160 | tf_op jit(solution)/shard_map/all_gather | solution.py:411
  408.1 26.4 %collective-permute-start.57 = (bf16[4,64,1024]{2,1,0:T(8,128)(2,1)S(1)}, bf16[4,64,1024]{2,1,0:T(8,128)(2,1)S(1)}, u32[]{:S(2)}, u32[]{:S(2)}) collective-permute-start(bf16[4,64,1024]{2,1,0:T(8,128)(2,1)S(1)} %add_convert_fusion.1), channel_id=1, source_target_pairs={{16,2},{17,3},{18,0},{19,1},{20,6},{21,7},{22,4},{23,5},{24,10},{2... | collective-permute-start | bytes 1572872 | tf_op jit(solution)/shard_map/ppermute | solution.py:36
  (116 other events, 1082.9 us)
Sparse Core Ops, SparseCore 0:
  58.4 60.5 reduce-scatter.2
  121.3 80.0 reduce-scatter.4
  387.6 66.7 all-gather.4
  477.8 65.8 all-gather.2

commit v5 on v4

--- a/solution.py
+++ b/solution.py
@@ -107,12 +107,19 @@
     if residual is not None:
         total = total + jnp.where(index < 2, residual.astype(F32), 0.0)
     total = total.astype(BF16)
-    got = [mp_shift(total, 2 * g, (giver,), flip=True) for g in range(groups - 1, -1, -1)]
-    got += [mp_shift(total, 2 * g, (0,)) for g in range(1, groups)]
-    own = jnp.where(lax.axis_index("section") == 0, total.astype(F32), 0.0)
-    mine = functools.reduce(jnp.add, [g.astype(F32) for g in got], own).astype(BF16)
+    sums = total
+    if giver == 1:
+        sums = (sums.astype(F32) + mp_shift(sums, 0, (1,), flip=True).astype(F32)).astype(BF16)
+    step = 2
+    while step < 2 * groups:
+        sums = (sums.astype(F32) + mp_shift(sums, step, (0,)).astype(F32)).astype(BF16)
+        step *= 2
+    mine = sums
+    if giver == 0:
+        here = lax.axis_index("section") == 0
+        mine = jnp.where(here, sums, mp_shift(sums, 0, (0,), flip=True))
     other = mp_shift(mine, 1, targets)
-    return halves(mine, other, parity)
+    return halves(mine, other, parity), sums
 
 
 def add_up(sources, start):
@@ -140,6 +147,10 @@
         e = jnp.exp(s - jnp.max(s, axis=1, keepdims=True))
         out.append(e / jnp.sum(e, axis=1, keepdims=True))
     return jnp.concatenate(out, axis=1)
+
+
+def plan_size(plan):
+    return 1 + max(i for sources in plan for i, _ in sources)
 
 
 def bind(plan, refs):
@@ -166,6 +177,11 @@
     qs, ks, vs, gs = bind(plan, refs)
     gk_ref, gv_ref, send_ref, gram_ref = refs[count:]
     seq, width = gk_ref.shape
+
+    if not decoder:
+        @pl.when(info[0] == 0)
+        def hand_on():
+            send_ref[...] = refs[plan_size(plan)][...]
 
     @pl.when(info[0] == 1)
     def run():
@@ -205,7 +221,7 @@
             gram_ref[i] = grams[i]
 
 
-def call_attention(kernel, info, operands, outs, flops, name, after=()):
+def call_attention(kernel, info, operands, outs, flops, name, extra=(), after=()):
     arrays, plan = [], []
     for sources in operands:
         plan.append([])
@@ -214,6 +230,7 @@
             if not known:
                 arrays.append(array)
             plan[-1].append((known[0] if known else len(arrays) - 1, offset))
+    arrays.extend(extra)
     vmem = pl.BlockSpec(memory_space=pltpu.VMEM)
     return pl.pallas_call(
         functools.partial(kernel, plan, len(arrays) + len(after)),
@@ -233,10 +250,10 @@
 def attend(info, operands, seq, width, after):
     rows = jax.ShapeDtypeStruct((seq, width), BF16)
     flops = 8 * seq * seq * width
-    return call_attention(fwd_kernel, info, operands, (rows,), flops, "attend", after)[0]
-
-
-def attend_back(info, operands, seq, width, decoder, after=()):
+    return call_attention(fwd_kernel, info, operands, (rows,), flops, "attend", (), after)[0]
+
+
+def attend_back(info, operands, seq, width, decoder, extra=(), after=()):
     outs = (
         jax.ShapeDtypeStruct((seq, width), BF16),
         jax.ShapeDtypeStruct((seq, width), BF16),
@@ -248,7 +265,7 @@
         full_kernel(plan, count, decoder, *refs)
 
     flops = 40 * seq * seq * width
-    return call_attention(kernel, info, operands, outs, flops, "attend_back", after)
+    return call_attention(kernel, info, operands, outs, flops, "attend_back", extra, after)
 
 
 def wgrad_kernel(count, chunk, scale, start, clip, info, x1, xa, xb, send, kept, base, out):
@@ -341,22 +358,23 @@
     own32 = inputs[0].astype(F32)
     inv = lax.rsqrt(jnp.mean(own32 * own32, axis=-1) + 1e-06)
     inv_all = gather(inv, both)
-    raw_half, x = [], []
-    for b in range(mb):
-        mine = to_columns(inputs[0, b : b + 1], parity, both, raw_half[-1:])[:, 0]
+    raw_half, x, first, payloads = [], [], [], []
+    keep = (jnp.arange(seq)[None] < lengths[1][:, None]).astype(BF16)
+    cot = cotangent * keep[:, :, None]
+    cot_cols = []
+    for b in range(mb):
+        mine = to_columns(inputs[0, b : b + 1], parity, both, payloads[-1:])[:, 0]
+        if b == 0:
+            mine = gate(mine, w)
         raw = halves(mine, mp_shift(mine, 1, both), parity)
         raw_half.append(mine)
         x.append(rows_of((raw.astype(F32) * inv_all[:, b, :, None] * gain_cols).astype(BF16)))
-    keep = (jnp.arange(seq)[None] < lengths[1][:, None]).astype(BF16)
-    cot = cotangent * keep[:, :, None]
-    cot_half = to_columns(cot, parity, dec)
-    cot_cols = halves(cot_half, mp_shift(cot_half, 1, dec), parity)
-    cot_cols = [rows_of(cot_cols[:, b]) for b in range(mb)]
-    first = []
-    for b in range(mb):
         if b < mb - 1:
             parts = [mm(x[b], w[s]) for s in range(3)]
         else:
+            cot_half = to_columns(cot, parity, dec, payloads[-1:])
+            cot_cols = halves(cot_half, mp_shift(cot_half, 1, dec), parity)
+            cot_cols = [rows_of(cot_cols[:, i]) for i in range(mb)]
             w_k, w_v = jnp.where(is_dec, w[3], w[1]), jnp.where(is_dec, w[3], w[2])
             parts = [
                 mm(x[b], w[0]),
@@ -364,11 +382,8 @@
                 mm(jnp.where(is_dec, cot_cols[1], x[b]), w_v),
             ]
         parts = jnp.concatenate([p.astype(BF16) for p in parts], axis=1)
-        first.append(
-            lax.psum_scatter(
-                parts.reshape(n, seq, 3 * inner), "dp", scatter_dimension=0, tiled=False
-            )
-        )
+        payloads.append(parts.reshape(n, seq, 3 * inner))
+        first.append(lax.psum_scatter(payloads[b], "dp", scatter_dimension=0, tiled=False))
     w_relay = jnp.where(is_dec, w[2], mp_shift(w[1], 0, dec, flip=True))
     ctx_all, enc_out, kv_terms, kv_parts, keys = [], [], [], [], []
     for b in range(mb):
@@ -377,8 +392,9 @@
         ctx = rows_of(gather(ctx, enc))
         ctx_all.append(gate(ctx, keys[-1]) if keys else ctx)
         terms = mm(ctx_all[b], w[3], NT).reshape(n, seq, depth)
-        enc_out.append(relay(terms, raw_half[b], enc, 0, both))
-        terms = mm(rows_of(enc_out[b]), w_relay).astype(BF16).reshape(n, seq, inner)
+        out, relayed = relay(terms, raw_half[b], enc, 0, both)
+        enc_out.append(out)
+        terms = mm(rows_of(out), w_relay).astype(BF16).reshape(n, seq, inner)
         kv_terms.append(terms)
         kv_parts.append(to_owner(terms, both))
         key = functools.reduce(jnp.add, [k.astype(F32) for k in kv_parts[b]]).astype(BF16)
@@ -391,12 +407,18 @@
             [(part, 0) for part in kv_parts[b]],
             [(first[mb - 1], (1 + b) * inner)],
         ]
-        gk, gv, send, gram = attend_back(info(section == 1, b), operands, seq, inner, True)
+        after = (relayed,) if b == 0 else ()
+        gk, gv, send, gram = attend_back(
+            info(section == 1, b), operands, seq, inner, True, (), after
+        )
         rows = jnp.where(is_dec, gv, mp_shift(gk, 0, dec, flip=True))
+        if b == 0:
+            rows = gate(rows, kv_terms[-1])
         rows = rows_of(gather(rows, both))
-        relay_all.append(gate(rows, ctx_terms[-1]) if ctx_terms else rows)
+        relay_all.append(gate(rows, keys[-1]) if b == 0 else rows)
         terms = mm(relay_all[b], w_relay, NT).reshape(n, seq, depth)
-        grad_enc.append(relay(terms, None, both, 1, enc))
+        grad, met = relay(terms, None, both, 1, enc)
+        grad_enc.append(grad)
         terms = mm(rows_of(grad_enc[b]), w[3]).astype(BF16)
         ctx_terms.append(terms.reshape(n, seq, inner))
         dec_send.append(send)
@@ -405,9 +427,11 @@
     for b in range(mb):
         gctx = to_owner(ctx_terms[b], enc)
         operands = [[(first[b], i * inner)] for i in range(3)] + [[(part, 0) for part in gctx]]
-        _, _, send, gram = attend_back(info(section == 0, b), operands, seq, inner, False)
+        after = (met,) if b < mb - 1 else ()
+        _, _, send, gram = attend_back(
+            info(section == 0, b), operands, seq, inner, False, (dec_send[b],), after
+        )
         enc_gram.append(gram)
-        send = jnp.where(is_dec, dec_send[b], send)
         send_all.append(lax.all_gather(send, "dp", axis=0, tiled=True))
     normed = (own32 * inv[..., None] * gain).astype(BF16)
     gram_x = jnp.einsum("btd,bud->btu", normed, normed, preferred_element_type=F32)

time: 579 us -> 653 us (1.13)
  waiting for transfers between devices: 249 us -> 304 us
  starting transfers between devices: 128 us -> 146 us
    ppermute x38, waiting for transfers between devices: 111 us -> 152 us  [dp_shift(): return lax.ppermute(x, ('section', 'dp'), pairs)]
    ppermute x31 -> x27, waiting for transfers between devices: 102 us -> 123 us  [mp_shift(): return lax.ppermute(x, ('section', 'mp'), pairs)]
    ppermute x38, starting transfers between devices: 81.9 us -> 102 us  [dp_shift(): return lax.ppermute(x, ('section', 'dp'), pairs)]
    reduce_scatter x2, waiting for transfers between devices: 32.5 us -> 15.9 us  [per_device(): lax.psum_scatter(payloads[b], 'dp', scatter_dimension=0, tiled=False)]
    all_gather x2, waiting for transfers between devices: 3.92 us -> 12.4 us  [per_device(): send_all.append(lax.all_gather(send, 'dp', axis=0, tiled=True))]
    unnamed x135 -> x111, local copies, waits for them, and re-layouts: 19.3 us -> 15.8 us
    ppermute x31 -> x27, starting transfers between devices: 45.3 us -> 44.4 us  [mp_shift(): return lax.ppermute(x, ('section', 'mp'), pairs)]
  transfers between devices with their start and end apart: 73 -> 69, of which waited for: 35 -> 35; matrix products, arithmetic and copies ran while one was open for 17% -> 15% of each run, Pallas kernels for 6% -> 4%
where the time goes in v5:
time: 653 us; the launch traced here: 644 us
  waiting for transfers between devices  304 us (47%)
  starting transfers between devices  146 us (22%)
  Pallas kernels  54.7 us (8%)
  other arithmetic  47.9 us (7%)
  matrix products  44.2 us (7%)
  local copies, waits for them, and re-layouts  28 us (4%)
  between operations  18.3 us (3%)
    ppermute x38, waiting for transfers between devices, dp_shift(): return lax.ppermute(x, ('section', 'dp'), pairs)  152 us
    ppermute x27, waiting for transfers between devices, mp_shift(): return lax.ppermute(x, ('section', 'mp'), pairs)  123 us
    ppermute x38, starting transfers between devices, dp_shift(): return lax.ppermute(x, ('section', 'dp'), pairs)  102 us
    ppermute x27, starting transfers between devices, mp_shift(): return lax.ppermute(x, ('section', 'mp'), pairs)  44.4 us
    pallas_call x2, Pallas kernels, wgrad(): pl.pallas_call(functools.partial(wgrad_kernel, tokens // chunk, chunk, 1....  37.6 us
    dot_general x14, matrix products, mm(): return lax.dot_general(left, right, dims, preferred_element_type=F32)  34.4 us
    pallas_call x6, Pallas kernels, call_attention(): pl.pallas_call(functools.partial(kernel, plan, len(arrays) + len(after)),...  17.1 us
    reduce_scatter x2, waiting for transfers between devices, per_device(): lax.psum_scatter(payloads[b], 'dp', scatter_dimension=0, tiled=False)  15.9 us
  transfers between devices with their start and end apart: 69, of which 35 were waited for; matrix products, arithmetic and copies ran while one was open for 15% of the time, Pallas kernels for 4%

profile of v5, /device:TPU:0, one launch (start us, length us, event | category | flops | bytes accessed | tf_op | source)
XLA Modules:
  0.0 643.6 jit_solution(11514787062139335010)
XLA Ops:
  20.5 9.6 %copy.25 = bf16[1,1024,4,1024]{3,1,2,0:T(8,128)(2,1)} copy(bf16[1,1024,4,1024]{3,2,1,0:T(4,128)(2,1)} %param.8) | data formatting | bytes 16777216 | tf_op args[2]
  61.2 17.3 %collective-permute-done.20 = bf16[1,64,1024]{2,1,0:T(8,128)(2,1)S(1)} collective-permute-done((bf16[1,64,1024]{2,1,0:T(8,128)(2,1)S(1)}, bf16[1,64,1024]{2,1,0:T(8,128)(2,1)S(1)}, u32[]{:S(2)}, u32[]{:S(2)}) %collective-permute-start.20) | collective-permute-done | bytes 131104 | tf_op jit(solution)/shard_map/ppermute | solution.py:28
  98.9 15.9 %reduce-scatter.3.cloned.1.call-done = bf16[1,128,3072]{2,1,0:T(8,128)(2,1)} async-done(((bf16[4,128,3072]{2,1,0:T(8,128)(2,1)}), bf16[1,128,3072]{2,1,0:T(8,128)(2,1)}) %reduce-scatter.3.cloned.1.call-update) | async-done | bytes 786448 | tf_op jit(solution)/shard_map/reduce_scatter | solution.py:386
  130.6 15.9 %collective-permute-done.8 = bf16[128,1024]{1,0:T(8,128)(2,1)S(1)} collective-permute-done((bf16[128,1024]{1,0:T(8,128)(2,1)S(1)}, bf16[128,1024]{1,0:T(8,128)(2,1)S(1)}, u32[]{:S(2)}, u32[]{:S(2)}) %collective-permute-start.8) | collective-permute-done | bytes 262176 | tf_op jit(solution)/shard_map/ppermute | solution.py:28
  161.8 12.6 %collective-permute-done.11 = bf16[4,64,1024]{2,1,0:T(8,128)(2,1)S(1)} collective-permute-done((bf16[4,64,1024]{2,1,0:T(8,128)(2,1)S(1)}, bf16[4,64,1024]{2,1,0:T(8,128)(2,1)S(1)}, u32[]{:S(2)}, u32[]{:S(2)}) %collective-permute-start.11) | collective-permute-done | bytes 524320 | tf_op jit(solution)/shard_map/ppermute | solution.py:36
  176.3 10.9 %collective-permute-done.12 = bf16[4,64,1024]{2,1,0:T(8,128)(2,1)S(1)} collective-permute-done((bf16[4,64,1024]{2,1,0:T(8,128)(2,1)S(1)}, bf16[4,64,1024]{2,1,0:T(8,128)(2,1)S(1)}, u32[]{:S(2)}, u32[]{:S(2)}) %collective-permute-start.12) | collective-permute-done | bytes 524320 | tf_op jit(solution)/shard_map/ppermute | solution.py:36
  187.4 22.9 %collective-permute-done.14 = bf16[1024,1024]{1,0:T(8,128)(2,1)} collective-permute-done((bf16[1024,1024]{1,0:T(8,128)(2,1)}, bf16[1024,1024]{1,0:T(8,128)(2,1)}, u32[]{:S(2)}, u32[]{:S(2)}) %collective-permute-start.14) | collective-permute-done | bytes 2097184 | tf_op jit(solution)/shard_map/ppermute | solution.py:36
  242.7 15.6 %collective-permute-done.28 = bf16[128,1024]{1,0:T(8,128)(2,1)S(1)} collective-permute-done((bf16[128,1024]{1,0:T(8,128)(2,1)S(1)}, bf16[128,1024]{1,0:T(8,128)(2,1)S(1)}, u32[]{:S(2)}, u32[]{:S(2)}) %collective-permute-start.28) | collective-permute-done | bytes 262176 | tf_op jit(solution)/shard_map/ppermute | solution.py:28
  271.4 12.4 %collective-permute-done.31 = bf16[4,64,1024]{2,1,0:T(8,128)(2,1)S(1)} collective-permute-done((bf16[4,64,1024]{2,1,0:T(8,128)(2,1)S(1)}, bf16[4,64,1024]{2,1,0:T(8,128)(2,1)S(1)}, u32[]{:S(2)}, u32[]{:S(2)}) %collective-permute-start.31) | collective-permute-done | bytes 524320 | tf_op jit(solution)/shard_map/ppermute | solution.py:36
  285.3 10.9 %collective-permute-done.33 = bf16[4,64,1024]{2,1,0:T(8,128)(2,1)S(1)} collective-permute-done((bf16[4,64,1024]{2,1,0:T(8,128)(2,1)S(1)}, bf16[4,64,1024]{2,1,0:T(8,128)(2,1)S(1)}, u32[]{:S(2)}, u32[]{:S(2)}) %collective-permute-start.33) | collective-permute-done | bytes 524320 | tf_op jit(solution)/shard_map/ppermute | solution.py:36
  323.0 16.0 %collective-permute-done.39.refs_5_ = bf16[128,1024]{1,0:T(8,128)(2,1)S(1)} collective-permute-done((bf16[128,1024]{1,0:T(8,128)(2,1)S(1)}, bf16[128,1024]{1,0:T(8,128)(2,1)S(1)}, u32[]{:S(2)}, u32[]{:S(2)}) %collective-permute-start.39) | collective-permute-done | bytes 262176 | tf_op jit(solution)/shard_map/ppermute | solution.py:28
  340.2 10.1 %collective-permute-start.41 = (bf16[128,1024]{1,0:T(8,128)(2,1)S(1)}, bf16[128,1024]{1,0:T(8,128)(2,1)S(1)}, u32[]{:S(2)}, u32[]{:S(2)}) collective-permute-start(bf16[128,1024]{1,0:T(8,128)(2,1)S(1)} %get-tuple-element.36), channel_id=1, source_target_pairs={{0,16},{1,17},{2,18},{3,19},{4,20},{5,21},{6,22},{7,23},{8,24},{9,... | collective-permute-start | bytes 786440 | tf_op jit(solution)/shard_map/ppermute | solution.py:36
  362.3 13.9 %collective-permute-done.49 = bf16[128,1024]{1,0:T(8,128)(2,1)S(1)} collective-permute-done((bf16[128,1024]{1,0:T(8,128)(2,1)}, bf16[128,1024]{1,0:T(8,128)(2,1)S(1)}, u32[]{:S(2)}, u32[]{:S(2)}) %collective-permute-start.49) | collective-permute-done | bytes 262176 | tf_op jit(solution)/shard_map/ppermute | solution.py:36
  387.4 11.8 %collective-permute-done.51 = bf16[128,1024]{1,0:T(8,128)(2,1)S(1)} collective-permute-done((bf16[128,1024]{1,0:T(8,128)(2,1)S(1)}, bf16[128,1024]{1,0:T(8,128)(2,1)S(1)}, u32[]{:S(2)}, u32[]{:S(2)}) %collective-permute-start.51) | collective-permute-done | bytes 262176 | tf_op jit(solution)/shard_map/ppermute | solution.py:28
  402.7 11.1 %collective-permute-done.43 = bf16[4,64,1024]{2,1,0:T(8,128)(2,1)S(1)} collective-permute-done((bf16[4,64,1024]{2,1,0:T(8,128)(2,1)S(1)}, bf16[4,64,1024]{2,1,0:T(8,128)(2,1)S(1)}, u32[]{:S(2)}, u32[]{:S(2)}) %collective-permute-start.43) | collective-permute-done | bytes 524320 | tf_op jit(solution)/shard_map/ppermute | solution.py:36
  418.9 8.1 %collective-permute-done.44 = bf16[4,64,1024]{2,1,0:T(8,128)(2,1)S(1)} collective-permute-done((bf16[4,64,1024]{2,1,0:T(8,128)(2,1)S(1)}, bf16[4,64,1024]{2,1,0:T(8,128)(2,1)S(1)}, u32[]{:S(2)}, u32[]{:S(2)}) %collective-permute-start.44) | collective-permute-done | bytes 524320 | tf_op jit(solution)/shard_map/ppermute | solution.py:36
  450.0 12.1 %collective-permute-done.47.refs_4_ = bf16[128,1024]{1,0:T(8,128)(2,1)S(1)} collective-permute-done((bf16[128,1024]{1,0:T(8,128)(2,1)S(1)}, bf16[128,1024]{1,0:T(8,128)(2,1)S(1)}, u32[]{:S(2)}, u32[]{:S(2)}) %collective-permute-start.47) | collective-permute-done | bytes 262176 | tf_op jit(solution)/shard_map/ppermute | solution.py:28
  482.6 7.3 %collective-permute-start.59 = (bf16[128,1024]{1,0:T(8,128)(2,1)S(1)}, bf16[128,1024]{1,0:T(8,128)(2,1)S(1)}, u32[]{:S(2)}, u32[]{:S(2)}) collective-permute-start(bf16[128,1024]{1,0:T(8,128)(2,1)S(1)} %get-tuple-element.43), channel_id=1, source_target_pairs={{0,4},{4,0},{8,12},{12,8},{1,5},{5,1},{9,13},{13,9},{2,6},{6,2},{1... | collective-permute-start | bytes 786440 | tf_op jit(solution)/shard_map/ppermute | solution.py:28
  496.6 17.9 %collective-permute-done.59.refs_5_ = bf16[128,1024]{1,0:T(8,128)(2,1)S(1)} collective-permute-done((bf16[128,1024]{1,0:T(8,128)(2,1)S(1)}, bf16[128,1024]{1,0:T(8,128)(2,1)S(1)}, u32[]{:S(2)}, u32[]{:S(2)}) %collective-permute-start.59) | collective-permute-done | bytes 262176 | tf_op jit(solution)/shard_map/ppermute | solution.py:28
  514.5 12.7 %collective-permute-done.58.refs_4_ = bf16[128,1024]{1,0:T(8,128)(2,1)S(1)} collective-permute-done((bf16[128,1024]{1,0:T(8,128)(2,1)S(1)}, bf16[128,1024]{1,0:T(8,128)(2,1)S(1)}, u32[]{:S(2)}, u32[]{:S(2)}) %collective-permute-start.58) | collective-permute-done | bytes 262176 | tf_op jit(solution)/shard_map/ppermute | solution.py:28
  552.4 22.4 %collective-permute-start.62 = (f32[2,4]{1,0:T(2,128)S(1)}, f32[2,4]{1,0:T(2,128)S(1)}, u32[]{:S(2)}, u32[]{:S(2)}) collective-permute-start(f32[2,4]{1,0:T(2,128)S(1)} %fusion.131), channel_id=1, source_target_pairs={{0,4},{4,0},{8,12},{12,8},{16,20},{20,16},{24,28},{28,24},{1,5},{5... | collective-permute-start | bytes 104 | tf_op jit(solution)/shard_map/ppermute | solution.py:28
  586.5 18.9 %weight_gradient.2.base = f32[1024,4,1024]{2,1,0:T(4,128)} custom-call(f32[4]{0:T(128)} %get-tuple-element.107.clip, s32[1]{0:T(128)} %bitcast.103.info, bf16[512,1024]{1,0:T(8,128)(2,1)} %get-tuple-element.33.x1, bf16[512,1024]{1,0:T(8,128)(2,1)} %get-tuple-element.32.xa, bf16[512,1024]{1,0:T(8,128)(2,1)} %broadcast_select_fusion.xb, ...), custom_call_target="tpu_custom_call" | custom-call | flops 4294967296 | bytes 37748736 | tf_op jit(solution)/shard_map/weight_gradient/pallas_call | solution.py:315
  605.4 12.4 %all-gather.3.cloned.1.call-done.send = bf16[512,3072]{1,0:T(8,128)(2,1)} async-done(((bf16[128,3072]{1,0:T(8,128)(2,1)}), bf16[512,3072]{1,0:T(8,128)(2,1)}) %all-gather.3.cloned.1.call-update) | async-done | bytes 3145744 | tf_op jit(solution)/shard_map/all_gather | solution.py:435
  617.8 18.7 %weight_gradient.3 = f32[1024,4,1024]{2,1,0:T(4,128)} custom-call(f32[4]{0:T(128)} %get-tuple-element.108.clip, s32[1]{0:T(128)} %bitcast.103.info, bf16[512,1024]{1,0:T(8,128)(2,1)} %get-tuple-element.98.x1, bf16[512,1024]{1,0:T(8,128)(2,1)} %get-tuple-element.97.xa, bf16[512,1024]{1,0:T(8,128)(2,1)} %broadcast_select_fusion.1.xb, ...), custom_call_target="tpu_custom_call" | custom-call | flops 4294967296 | bytes 37748736 | tf_op jit(solution)/shard_map/weight_gradient/pallas_call | solution.py:315
  (366 shorter events, 287.9 us)
Async XLA Ops:
  7.2 107.6 %reduce-scatter.3.cloned.1.call-start = ((), (), s32[]{:S(2)}) async-start(), calls=%async_computation.2 | async-start | bytes 3932160 | tf_op jit(solution)/shard_map/reduce_scatter | solution.py:386
  9.5 22.5 %collective-permute-start.6 = (f32[2,128]{1,0:T(2,128)S(1)}, f32[2,128]{1,0:T(2,128)S(1)}, u32[]{:S(2)}, u32[]{:S(2)}) collective-permute-start(f32[2,128]{1,0:T(2,128)S(1)} %add_rsqrt_fusion), channel_id=1, source_target_pairs={{0,12},{4,8},{8,4},{12,0},{16,28},{20,24},{24,20},{28,16},{1,13},{... | collective-permute-start | bytes 3080 | tf_op jit(solution)/shard_map/ppermute | solution.py:28
  46.7 173.1 %reduce-scatter.5.cloned.1.call-start = ((), (), s32[]{:S(2)}) async-start(), calls=%async_computation.3 | async-start | bytes 3932160 | tf_op jit(solution)/shard_map/reduce_scatter | solution.py:386
  52.8 25.7 %collective-permute-start.20 = (bf16[1,64,1024]{2,1,0:T(8,128)(2,1)S(1)}, bf16[1,64,1024]{2,1,0:T(8,128)(2,1)S(1)}, u32[]{:S(2)}, u32[]{:S(2)}) collective-permute-start(bf16[1,64,1024]{2,1,0:T(8,128)(2,1)S(1)} %get-tuple-element.91), channel_id=1, source_target_pairs={{0,8},{4,12},{8,0},{12,4},{16,24},{20,28},{24,16},{28,20},{1,9},{5... | collective-permute-start | bytes 393224 | tf_op jit(solution)/shard_map/ppermute | solution.py:28
  52.8 25.7 %collective-permute-start.19 = (bf16[1,64,1024]{2,1,0:T(8,128)(2,1)S(1)}, bf16[1,64,1024]{2,1,0:T(8,128)(2,1)S(1)}, u32[]{:S(2)}, u32[]{:S(2)}) collective-permute-start(bf16[1,64,1024]{2,1,0:T(8,128)(2,1)S(1)} %get-tuple-element.92), channel_id=1, source_target_pairs={{0,4},{4,0},{8,12},{12,8},{16,20},{20,16},{24,28},{28,24},{1,5},{5... | collective-permute-start | bytes 393224 | tf_op jit(solution)/shard_map/ppermute | solution.py:28
  57.1 21.7 %collective-permute-start.25 = (bf16[2,64,1024]{2,1,0:T(8,128)(2,1)S(1)}, bf16[2,64,1024]{2,1,0:T(8,128)(2,1)S(1)}, u32[]{:S(2)}, u32[]{:S(2)}) collective-permute-start(bf16[2,64,1024]{2,1,0:T(8,128)(2,1)S(1)} %get-tuple-element.78), channel_id=1, source_target_pairs={{16,28},{20,24},{24,20},{28,16},{17,29},{21,25},{25,21},{29,17},{1... | collective-permute-start | bytes 786440 | tf_op jit(solution)/shard_map/ppermute | solution.py:28
  97.5 489.0 %all-gather.5.cloned.1.call-start = ((), (), s32[]{:S(2)}) async-start(), calls=%async_computation.5 | async-start | bytes 3932160 | tf_op jit(solution)/shard_map/all_gather | solution.py:435
  122.4 24.0 %collective-permute-start.8 = (bf16[128,1024]{1,0:T(8,128)(2,1)S(1)}, bf16[128,1024]{1,0:T(8,128)(2,1)S(1)}, u32[]{:S(2)}, u32[]{:S(2)}) collective-permute-start(bf16[128,1024]{1,0:T(8,128)(2,1)S(1)} %attend.2), channel_id=1, source_target_pairs={{0,8},{4,12},{8,0},{12,4},{1,9},{5,13},{9,1},{13,5},{2,10},{6,14},... | collective-permute-start | bytes 786440 | tf_op jit(solution)/shard_map/ppermute | solution.py:28
  125.2 21.2 %collective-permute-start.7 = (bf16[128,1024]{1,0:T(8,128)(2,1)S(1)}, bf16[128,1024]{1,0:T(8,128)(2,1)S(1)}, u32[]{:S(2)}, u32[]{:S(2)}) collective-permute-start(bf16[128,1024]{1,0:T(8,128)(2,1)S(1)} %attend.2), channel_id=1, source_target_pairs={{0,4},{4,0},{8,12},{12,8},{1,5},{5,1},{9,13},{13,9},{2,6},{6,2},{1... | collective-permute-start | bytes 786440 | tf_op jit(solution)/shard_map/ppermute | solution.py:28
  155.5 54.7 %collective-permute-start.14 = (bf16[1024,1024]{1,0:T(8,128)(2,1)}, bf16[1024,1024]{1,0:T(8,128)(2,1)}, u32[]{:S(2)}, u32[]{:S(2)}) collective-permute-start(bf16[1024,1024]{1,0:T(8,128)(2,1)} %slice_bitcast_fusion.3), channel_id=1, source_target_pairs={{16,0},{17,1},{18,2},{19,3},{20,4},{21,5},{22,6},{23,7},{24,8},{25... | collective-permute-start | bytes 6291464 | tf_op jit(solution)/shard_map/ppermute | solution.py:36
  187.3 25.4 %collective-permute-start.13 = (bf16[4,64,1024]{2,1,0:T(8,128)(2,1)S(1)}, bf16[4,64,1024]{2,1,0:T(8,128)(2,1)S(1)}, u32[]{:S(2)}, u32[]{:S(2)}) collective-permute-start(bf16[4,64,1024]{2,1,0:T(8,128)(2,1)S(1)} %broadcast_select_fusion.5), channel_id=1, source_target_pairs={{0,1},{1,0},{2,3},{3,2},{16,17},{17,16},{18,19},{19,18},{4,5},{5,4... | collective-permute-start | bytes 1572872 | tf_op jit(solution)/shard_map/ppermute | solution.py:36
  224.6 33.7 %collective-permute-start.28 = (bf16[128,1024]{1,0:T(8,128)(2,1)S(1)}, bf16[128,1024]{1,0:T(8,128)(2,1)S(1)}, u32[]{:S(2)}, u32[]{:S(2)}) collective-permute-start(bf16[128,1024]{1,0:T(8,128)(2,1)S(1)} %attend.3), channel_id=1, source_target_pairs={{0,8},{4,12},{8,0},{12,4},{1,9},{5,13},{9,1},{13,5},{2,10},{6,14},... | collective-permute-start | bytes 786440 | tf_op jit(solution)/shard_map/ppermute | solution.py:28
  227.9 30.4 %collective-permute-start.27 = (bf16[128,1024]{1,0:T(8,128)(2,1)S(1)}, bf16[128,1024]{1,0:T(8,128)(2,1)S(1)}, u32[]{:S(2)}, u32[]{:S(2)}) collective-permute-start(bf16[128,1024]{1,0:T(8,128)(2,1)S(1)} %attend.3), channel_id=1, source_target_pairs={{0,4},{4,0},{8,12},{12,8},{1,5},{5,1},{9,13},{13,9},{2,6},{6,2},{1... | collective-permute-start | bytes 786440 | tf_op jit(solution)/shard_map/ppermute | solution.py:28
  235.4 24.2 %collective-permute-start.18 = (bf16[128,1024]{1,0:T(8,128)(2,1)S(1)}, bf16[128,1024]{1,0:T(8,128)(2,1)S(1)}, u32[]{:S(2)}, u32[]{:S(2)}) collective-permute-start(bf16[128,1024]{1,0:T(8,128)(2,1)S(1)} %get-tuple-element.38), channel_id=1, source_target_pairs={{0,16},{1,17},{2,18},{3,19},{4,20},{5,21},{6,22},{7,23},{8,24},{9,... | collective-permute-start | bytes 786440 | tf_op jit(solution)/shard_map/ppermute | solution.py:36
  305.2 33.9 %collective-permute-start.39 = (bf16[128,1024]{1,0:T(8,128)(2,1)S(1)}, bf16[128,1024]{1,0:T(8,128)(2,1)S(1)}, u32[]{:S(2)}, u32[]{:S(2)}) collective-permute-start(bf16[128,1024]{1,0:T(8,128)(2,1)S(1)} %get-tuple-element.61), channel_id=1, source_target_pairs={{0,8},{4,12},{8,0},{12,4},{16,24},{20,28},{24,16},{28,20},{1,9},{5... | collective-permute-start | bytes 786440 | tf_op jit(solution)/shard_map/ppermute | solution.py:28
  315.5 34.8 %collective-permute-start.37 = (bf16[128,1024]{1,0:T(8,128)(2,1)}, bf16[128,1024]{1,0:T(8,128)(2,1)S(1)}, u32[]{:S(2)}, u32[]{:S(2)}) collective-permute-start(bf16[128,1024]{1,0:T(8,128)(2,1)} %gate.10), channel_id=1, source_target_pairs={{0,12},{4,8},{8,4},{12,0},{16,28},{20,24},{24,20},{28,16},{1,13},{... | collective-permute-start | bytes 786440 | tf_op jit(solution)/shard_map/ppermute | solution.py:28
  317.3 33.0 %collective-permute-start.36 = (bf16[128,1024]{1,0:T(8,128)(2,1)}, bf16[128,1024]{1,0:T(8,128)(2,1)S(1)}, u32[]{:S(2)}, u32[]{:S(2)}) collective-permute-start(bf16[128,1024]{1,0:T(8,128)(2,1)} %gate.10), channel_id=1, source_target_pairs={{0,8},{4,12},{8,0},{12,4},{16,24},{20,28},{24,16},{28,20},{1,9},{5... | collective-permute-start | bytes 786440 | tf_op jit(solution)/shard_map/ppermute | solution.py:28
  317.3 33.0 %collective-permute-start.35 = (bf16[128,1024]{1,0:T(8,128)(2,1)}, bf16[128,1024]{1,0:T(8,128)(2,1)S(1)}, u32[]{:S(2)}, u32[]{:S(2)}) collective-permute-start(bf16[128,1024]{1,0:T(8,128)(2,1)} %gate.10), channel_id=1, source_target_pairs={{0,4},{4,0},{8,12},{12,8},{16,20},{20,16},{24,28},{28,24},{1,5},{5... | collective-permute-start | bytes 786440 | tf_op jit(solution)/shard_map/ppermute | solution.py:28
  438.9 23.2 %collective-permute-start.47 = (bf16[128,1024]{1,0:T(8,128)(2,1)S(1)}, bf16[128,1024]{1,0:T(8,128)(2,1)S(1)}, u32[]{:S(2)}, u32[]{:S(2)}) collective-permute-start(bf16[128,1024]{1,0:T(8,128)(2,1)S(1)} %get-tuple-element.48), channel_id=1, source_target_pairs={{0,8},{4,12},{8,0},{12,4},{1,9},{5,13},{9,1},{13,5},{2,10},{6,14},... | collective-permute-start | bytes 786440 | tf_op jit(solution)/shard_map/ppermute | solution.py:28
  468.1 149.7 %all-gather.3.cloned.1.call-start = ((), (), s32[]{:S(2)}) async-start(), calls=%async_computation.4 | async-start | bytes 3932160 | tf_op jit(solution)/shard_map/all_gather | solution.py:435
  482.6 31.8 %collective-permute-start.59 = (bf16[128,1024]{1,0:T(8,128)(2,1)S(1)}, bf16[128,1024]{1,0:T(8,128)(2,1)S(1)}, u32[]{:S(2)}, u32[]{:S(2)}) collective-permute-start(bf16[128,1024]{1,0:T(8,128)(2,1)S(1)} %get-tuple-element.43), channel_id=1, source_target_pairs={{0,4},{4,0},{8,12},{12,8},{1,5},{5,1},{9,13},{13,9},{2,6},{6,2},{1... | collective-permute-start | bytes 786440 | tf_op jit(solution)/shard_map/ppermute | solution.py:28
  489.9 37.2 %collective-permute-start.58 = (bf16[128,1024]{1,0:T(8,128)(2,1)S(1)}, bf16[128,1024]{1,0:T(8,128)(2,1)S(1)}, u32[]{:S(2)}, u32[]{:S(2)}) collective-permute-start(bf16[128,1024]{1,0:T(8,128)(2,1)S(1)} %get-tuple-element.44), channel_id=1, source_target_pairs={{0,8},{4,12},{8,0},{12,4},{1,9},{5,13},{9,1},{13,5},{2,10},{6,14},... | collective-permute-start | bytes 786440 | tf_op jit(solution)/shard_map/ppermute | solution.py:28
  492.3 34.9 %collective-permute-start.57 = (bf16[128,1024]{1,0:T(8,128)(2,1)S(1)}, bf16[128,1024]{1,0:T(8,128)(2,1)S(1)}, u32[]{:S(2)}, u32[]{:S(2)}) collective-permute-start(bf16[128,1024]{1,0:T(8,128)(2,1)S(1)} %get-tuple-element.45), channel_id=1, source_target_pairs={{0,12},{4,8},{8,4},{12,0},{1,13},{5,9},{9,5},{13,1},{2,14},{6,10},... | collective-permute-start | bytes 786440 | tf_op jit(solution)/shard_map/ppermute | solution.py:28
  552.4 23.9 %collective-permute-start.62 = (f32[2,4]{1,0:T(2,128)S(1)}, f32[2,4]{1,0:T(2,128)S(1)}, u32[]{:S(2)}, u32[]{:S(2)}) collective-permute-start(f32[2,4]{1,0:T(2,128)S(1)} %fusion.131), channel_id=1, source_target_pairs={{0,4},{4,0},{8,12},{12,8},{16,20},{20,16},{24,28},{28,24},{1,5},{5... | collective-permute-start | bytes 104 | tf_op jit(solution)/shard_map/ppermute | solution.py:28
  (100 other events, 934.0 us)
Sparse Core Ops, SparseCore 0:
  46.8 67.9 reduce-scatter.2
  117.1 89.6 reduce-scatter.4
  468.2 86.8 all-gather.4
  556.6 61.1 all-gather.2

commit v6 on v5

--- a/solution.py
+++ b/solution.py
@@ -53,10 +53,14 @@
     return jnp.stack([pick(stacked, me ^ i) for i in range(len(slots))])
 
 
-def gather(rows, sections):
+def exchange(rows, sections):
     n = lax.axis_size("dp")
     got = {s: dp_shift(rows, s, sections) for s in range(n - 1, 0, -1)}
-    return in_order([rows] + [got[s] for s in range(1, n)])
+    return [rows] + [got[s] for s in range(1, n)]
+
+
+def gather(rows, sections):
+    return in_order(exchange(rows, sections))
 
 
 def halves(mine, other, parity):
@@ -95,7 +99,7 @@
     return in_order([mine[0]] + [got[s] for s in range(1, n)])
 
 
-def relay(terms, residual, sources, giver, targets):
+def relay(terms, residual, sources, giver, targets, after=()):
     groups = lax.axis_size("mp") // 2
     index = lax.axis_index("mp")
     parity = index % 2
@@ -107,19 +111,14 @@
     if residual is not None:
         total = total + jnp.where(index < 2, residual.astype(F32), 0.0)
     total = total.astype(BF16)
-    sums = total
-    if giver == 1:
-        sums = (sums.astype(F32) + mp_shift(sums, 0, (1,), flip=True).astype(F32)).astype(BF16)
-    step = 2
-    while step < 2 * groups:
-        sums = (sums.astype(F32) + mp_shift(sums, step, (0,)).astype(F32)).astype(BF16)
-        step *= 2
-    mine = sums
-    if giver == 0:
-        here = lax.axis_index("section") == 0
-        mine = jnp.where(here, sums, mp_shift(sums, 0, (0,), flip=True))
+    got = [mp_shift(total, 2 * g, (giver,), flip=True) for g in range(groups - 1, -1, -1)]
+    got += [mp_shift(total, 2 * g, (0,)) for g in range(1, groups)]
+    if after:
+        got[-1] = gate(got[-1], *after)
+    own = jnp.where(lax.axis_index("section") == 0, total.astype(F32), 0.0)
+    mine = functools.reduce(jnp.add, [g.astype(F32) for g in got], own).astype(BF16)
     other = mp_shift(mine, 1, targets)
-    return halves(mine, other, parity), sums
+    return halves(mine, other, parity), total, got[-1]
 
 
 def add_up(sources, start):
@@ -388,13 +387,13 @@
     ctx_all, enc_out, kv_terms, kv_parts, keys = [], [], [], [], []
     for b in range(mb):
         qkv = [[(first[b], i * inner)] for i in range(3)]
-        ctx = attend(info(section == 0, b), qkv, seq, inner, kv_terms[-1:])
+        ctx = attend(info(section == 0, b), qkv, seq, inner, kv_terms[-1:] or [w_relay])
         ctx = rows_of(gather(ctx, enc))
         ctx_all.append(gate(ctx, keys[-1]) if keys else ctx)
         terms = mm(ctx_all[b], w[3], NT).reshape(n, seq, depth)
-        out, relayed = relay(terms, raw_half[b], enc, 0, both)
+        out, total, posted = relay(terms, raw_half[b], enc, 0, both)
         enc_out.append(out)
-        terms = mm(rows_of(out), w_relay).astype(BF16).reshape(n, seq, inner)
+        terms = mm(rows_of(enc_out[b]), w_relay).astype(BF16).reshape(n, seq, inner)
         kv_terms.append(terms)
         kv_parts.append(to_owner(terms, both))
         key = functools.reduce(jnp.add, [k.astype(F32) for k in kv_parts[b]]).astype(BF16)
@@ -407,18 +406,19 @@
             [(part, 0) for part in kv_parts[b]],
             [(first[mb - 1], (1 + b) * inner)],
         ]
-        after = (relayed,) if b == 0 else ()
+        after = (total,) if b == 0 else ()
         gk, gv, send, gram = attend_back(
             info(section == 1, b), operands, seq, inner, True, (), after
         )
         rows = jnp.where(is_dec, gv, mp_shift(gk, 0, dec, flip=True))
         if b == 0:
-            rows = gate(rows, kv_terms[-1])
-        rows = rows_of(gather(rows, both))
-        relay_all.append(gate(rows, keys[-1]) if b == 0 else rows)
+            rows = gate(rows, posted)
+        slots = exchange(rows, both)
+        rows = rows_of(in_order(slots))
+        relay_all.append(gate(rows, ctx_terms[-1]) if ctx_terms else rows)
         terms = mm(relay_all[b], w_relay, NT).reshape(n, seq, depth)
-        grad, met = relay(terms, None, both, 1, enc)
-        grad_enc.append(grad)
+        after = kv_terms[b + 1 : b + 2]
+        grad_enc.append(relay(terms, None, both, 1, enc, after)[0])
         terms = mm(rows_of(grad_enc[b]), w[3]).astype(BF16)
         ctx_terms.append(terms.reshape(n, seq, inner))
         dec_send.append(send)
@@ -427,9 +427,14 @@
     for b in range(mb):
         gctx = to_owner(ctx_terms[b], enc)
         operands = [[(first[b], i * inner)] for i in range(3)] + [[(part, 0) for part in gctx]]
-        after = (met,) if b < mb - 1 else ()
         _, _, send, gram = attend_back(
-            info(section == 0, b), operands, seq, inner, False, (dec_send[b],), after
+            info(section == 0, b),
+            operands,
+            seq,
+            inner,
+            False,
+            (dec_send[b],),
+            slots[1:] if b < mb - 1 else (),
         )
         enc_gram.append(gram)
         send_all.append(lax.all_gather(send, "dp", axis=0, tiled=True))

time: 653 us -> 671 us (1.028)
  waiting for transfers between devices: 304 us -> 321 us
  starting transfers between devices: 146 us -> 133 us
  other arithmetic: 47.9 us -> 57.6 us
  local copies, waits for them, and re-layouts: 28 us -> 37.6 us
    ppermute x27 -> x31, waiting for transfers between devices: 123 us -> 161 us  [mp_shift(): return lax.ppermute(x, ('section', 'mp'), pairs)]
    reduce_scatter x2, waiting for transfers between devices: 15.9 us -> 0.02 us  [per_device(): lax.psum_scatter(payloads[b], 'dp', scatter_dimension=0, tiled=False)]
    ppermute x38, starting transfers between devices: 102 us -> 86.3 us  [dp_shift(): return lax.ppermute(x, ('section', 'dp'), pairs)]
    unnamed x111 -> x165, local copies, waits for them, and re-layouts: 15.8 us -> 24.7 us
    all_gather x2, waiting for transfers between devices: 12.4 us -> 3.9 us  [per_device(): send_all.append(lax.all_gather(send, 'dp', axis=0, tiled=True))]
    ppermute x27 -> x31, starting transfers between devices: 44.4 us -> 46.2 us  [mp_shift(): return lax.ppermute(x, ('section', 'mp'), pairs)]
  transfers between devices with their start and end apart: 69 -> 73, of which waited for: 35 -> 37; matrix products, arithmetic and copies ran while one was open for 15% -> 15% of each run, Pallas kernels for 4% -> 5%
where the time goes in v6:
time: 671 us; the launch traced here: 661 us
  waiting for transfers between devices  321 us (48%)
  starting transfers between devices  133 us (20%)
  other arithmetic  57.6 us (9%)
  Pallas kernels  54.8 us (8%)
  matrix products  39 us (6%)
  local copies, waits for them, and re-layouts  37.6 us (6%)
  between operations  18.5 us (3%)
    ppermute x31, waiting for transfers between devices, mp_shift(): return lax.ppermute(x, ('section', 'mp'), pairs)  161 us
    ppermute x38, waiting for transfers between devices, dp_shift(): return lax.ppermute(x, ('section', 'dp'), pairs)  156 us
    ppermute x38, starting transfers between devices, dp_shift(): return lax.ppermute(x, ('section', 'dp'), pairs)  86.3 us
    ppermute x31, starting transfers between devices, mp_shift(): return lax.ppermute(x, ('section', 'mp'), pairs)  46.2 us
    pallas_call x2, Pallas kernels, wgrad(): pl.pallas_call(functools.partial(wgrad_kernel, tokens // chunk, chunk, 1....  37.8 us
    dot_general x14, matrix products, mm(): return lax.dot_general(left, right, dims, preferred_element_type=F32)  33.3 us
    unnamed x165, local copies, waits for them, and re-layouts  24.7 us
    pallas_call x6, Pallas kernels, call_attention(): pl.pallas_call(functools.partial(kernel, plan, len(arrays) + len(after)),...  17 us
  transfers between devices with their start and end apart: 73, of which 37 were waited for; matrix products, arithmetic and copies ran while one was open for 15% of the time, Pallas kernels for 5%

profile of v6, /device:TPU:0, one launch (start us, length us, event | category | flops | bytes accessed | tf_op | source)
XLA Modules:
  0.0 660.8 jit_solution(13092322707414998364)
XLA Ops:
  20.5 9.6 %copy.26 = bf16[1,1024,4,1024]{3,1,2,0:T(8,128)(2,1)} copy(bf16[1,1024,4,1024]{3,2,1,0:T(4,128)(2,1)} %param.8) | data formatting | bytes 16777216 | tf_op args[2]
  61.3 17.2 %collective-permute-done.21 = bf16[1,64,1024]{2,1,0:T(8,128)(2,1)S(1)} collective-permute-done((bf16[1,64,1024]{2,1,0:T(8,128)(2,1)S(1)}, bf16[1,64,1024]{2,1,0:T(8,128)(2,1)S(1)}, u32[]{:S(2)}, u32[]{:S(2)}) %collective-permute-start.21) | collective-permute-done | bytes 131104 | tf_op jit(solution)/shard_map/ppermute | solution.py:28
  103.3 81.5 %collective-permute-done.7 = bf16[1024,1024]{1,0:T(8,128)(2,1)} collective-permute-done((bf16[1024,1024]{1,0:T(8,128)(2,1)}, bf16[1024,1024]{1,0:T(8,128)(2,1)}, u32[]{:S(2)}, u32[]{:S(2)}) %collective-permute-start.7) | collective-permute-done | bytes 2097184 | tf_op jit(solution)/shard_map/ppermute | solution.py:36
  194.0 6.3 collective-permute-start.8
  200.3 8.3 %collective-permute-done.10 = bf16[128,1024]{1,0:T(8,128)(2,1)S(1)} collective-permute-done((bf16[128,1024]{1,0:T(8,128)(2,1)S(1)}, bf16[128,1024]{1,0:T(8,128)(2,1)S(1)}, u32[]{:S(2)}, u32[]{:S(2)}) %collective-permute-start.10) | collective-permute-done | bytes 262176 | tf_op jit(solution)/shard_map/ppermute | solution.py:28
  208.7 25.5 %collective-permute-done.9 = bf16[128,1024]{1,0:T(8,128)(2,1)S(1)} collective-permute-done((bf16[128,1024]{1,0:T(8,128)(2,1)S(1)}, bf16[128,1024]{1,0:T(8,128)(2,1)S(1)}, u32[]{:S(2)}, u32[]{:S(2)}) %collective-permute-start.9) | collective-permute-done | bytes 262176 | tf_op jit(solution)/shard_map/ppermute | solution.py:28
  250.2 9.8 %collective-permute-done.14 = bf16[4,64,1024]{2,1,0:T(8,128)(2,1)S(1)} collective-permute-done((bf16[4,64,1024]{2,1,0:T(8,128)(2,1)S(1)}, bf16[4,64,1024]{2,1,0:T(8,128)(2,1)S(1)}, u32[]{:S(2)}, u32[]{:S(2)}) %collective-permute-start.14) | collective-permute-done | bytes 524320 | tf_op jit(solution)/shard_map/ppermute | solution.py:36
  261.1 10.4 %collective-permute-done.12 = bf16[4,64,1024]{2,1,0:T(8,128)(2,1)S(1)} collective-permute-done((bf16[4,64,1024]{2,1,0:T(8,128)(2,1)S(1)}, bf16[4,64,1024]{2,1,0:T(8,128)(2,1)S(1)}, u32[]{:S(2)}, u32[]{:S(2)}) %collective-permute-start.12) | collective-permute-done | bytes 524320 | tf_op jit(solution)/shard_map/ppermute | solution.py:36
  296.7 15.5 %collective-permute-done.17.refs_5_ = bf16[128,1024]{1,0:T(8,128)(2,1)} collective-permute-done((bf16[128,1024]{1,0:T(8,128)(2,1)}, bf16[128,1024]{1,0:T(8,128)(2,1)}, u32[]{:S(2)}, u32[]{:S(2)}) %collective-permute-start.17) | collective-permute-done | bytes 262176 | tf_op jit(solution)/shard_map/ppermute | solution.py:28
  315.5 7.1 %collective-permute-done.29 = bf16[128,1024]{1,0:T(8,128)(2,1)S(1)} collective-permute-done((bf16[128,1024]{1,0:T(8,128)(2,1)S(1)}, bf16[128,1024]{1,0:T(8,128)(2,1)S(1)}, u32[]{:S(2)}, u32[]{:S(2)}) %collective-permute-start.29) | collective-permute-done | bytes 262176 | tf_op jit(solution)/shard_map/ppermute | solution.py:28
  347.3 8.7 %collective-permute-done.32 = bf16[128,1024]{1,0:T(8,128)(2,1)S(1)} collective-permute-done((bf16[128,1024]{1,0:T(8,128)(2,1)S(1)}, bf16[128,1024]{1,0:T(8,128)(2,1)S(1)}, u32[]{:S(2)}, u32[]{:S(2)}) %collective-permute-start.32) | collective-permute-done | bytes 262176 | tf_op jit(solution)/shard_map/ppermute | solution.py:36
  368.0 12.0 %collective-permute-done.35 = bf16[128,1024]{1,0:T(8,128)(2,1)S(1)} collective-permute-done((bf16[128,1024]{1,0:T(8,128)(2,1)}, bf16[128,1024]{1,0:T(8,128)(2,1)S(1)}, u32[]{:S(2)}, u32[]{:S(2)}) %collective-permute-start.35) | collective-permute-done | bytes 262176 | tf_op jit(solution)/shard_map/ppermute | solution.py:28
  403.0 6.6 %collective-permute-done.49.refs_5_ = bf16[128,1024]{1,0:T(8,128)(2,1)S(1)} collective-permute-done((bf16[128,1024]{1,0:T(8,128)(2,1)S(1)}, bf16[128,1024]{1,0:T(8,128)(2,1)S(1)}, u32[]{:S(2)}, u32[]{:S(2)}) %collective-permute-start.49) | collective-permute-done | bytes 262176 | tf_op jit(solution)/shard_map/ppermute | solution.py:28
  422.8 10.5 %collective-permute-done.52 = bf16[128,1024]{1,0:T(8,128)(2,1)S(1)} collective-permute-done((bf16[128,1024]{1,0:T(8,128)(2,1)S(1)}, bf16[128,1024]{1,0:T(8,128)(2,1)S(1)}, u32[]{:S(2)}, u32[]{:S(2)}) %collective-permute-start.52) | collective-permute-done | bytes 262176 | tf_op jit(solution)/shard_map/ppermute | solution.py:36
  452.5 8.8 %collective-permute-done.54.refs_8_ = bf16[128,1024]{1,0:T(8,128)(2,1)S(1)} collective-permute-done((bf16[128,1024]{1,0:T(8,128)(2,1)S(1)}, bf16[128,1024]{1,0:T(8,128)(2,1)S(1)}, u32[]{:S(2)}, u32[]{:S(2)}) %collective-permute-start.54) | collective-permute-done | bytes 262176 | tf_op jit(solution)/shard_map/ppermute | solution.py:28
  461.4 11.8 %collective-permute-done.46.refs_4_ = bf16[128,1024]{1,0:T(8,128)(2,1)S(1)} collective-permute-done((bf16[128,1024]{1,0:T(8,128)(2,1)S(1)}, bf16[128,1024]{1,0:T(8,128)(2,1)S(1)}, u32[]{:S(2)}, u32[]{:S(2)}) %collective-permute-start.46) | collective-permute-done | bytes 262176 | tf_op jit(solution)/shard_map/ppermute | solution.py:28
  494.2 9.6 %collective-permute-done.59 = bf16[4,64,1024]{2,1,0:T(8,128)(2,1)S(1)} collective-permute-done((bf16[4,64,1024]{2,1,0:T(8,128)(2,1)S(1)}, bf16[4,64,1024]{2,1,0:T(8,128)(2,1)S(1)}, u32[]{:S(2)}, u32[]{:S(2)}) %collective-permute-start.59) | collective-permute-done | bytes 524320 | tf_op jit(solution)/shard_map/ppermute | solution.py:36
  508.3 9.8 %collective-permute-done.57 = bf16[4,64,1024]{2,1,0:T(8,128)(2,1)S(1)} collective-permute-done((bf16[4,64,1024]{2,1,0:T(8,128)(2,1)S(1)}, bf16[4,64,1024]{2,1,0:T(8,128)(2,1)S(1)}, u32[]{:S(2)}, u32[]{:S(2)}) %collective-permute-start.57) | collective-permute-done | bytes 524320 | tf_op jit(solution)/shard_map/ppermute | solution.py:36
  526.9 7.7 %collective-permute-start.63 = (bf16[128,1024]{1,0:T(8,128)(2,1)S(1)}, bf16[128,1024]{1,0:T(8,128)(2,1)S(1)}, u32[]{:S(2)}, u32[]{:S(2)}) collective-permute-start(bf16[128,1024]{1,0:T(8,128)(2,1)S(1)} %get-tuple-element.43), channel_id=1, source_target_pairs={{0,4},{4,0},{8,12},{12,8},{1,5},{5,1},{9,13},{13,9},{2,6},{6,2},{1... | collective-permute-start | bytes 786440 | tf_op jit(solution)/shard_map/ppermute | solution.py:28
  544.3 11.0 %collective-permute-done.63.refs_5_ = bf16[128,1024]{1,0:T(8,128)(2,1)S(1)} collective-permute-done((bf16[128,1024]{1,0:T(8,128)(2,1)S(1)}, bf16[128,1024]{1,0:T(8,128)(2,1)S(1)}, u32[]{:S(2)}, u32[]{:S(2)}) %collective-permute-start.63) | collective-permute-done | bytes 262176 | tf_op jit(solution)/shard_map/ppermute | solution.py:28
  555.3 8.0 %collective-permute-done.61.refs_3_ = bf16[128,1024]{1,0:T(8,128)(2,1)S(1)} collective-permute-done((bf16[128,1024]{1,0:T(8,128)(2,1)S(1)}, bf16[128,1024]{1,0:T(8,128)(2,1)S(1)}, u32[]{:S(2)}, u32[]{:S(2)}) %collective-permute-start.61) | collective-permute-done | bytes 262176 | tf_op jit(solution)/shard_map/ppermute | solution.py:28
  594.2 5.8 collective-permute-start.66
  612.1 19.1 %weight_gradient.2.base = f32[1024,4,1024]{2,1,0:T(4,128)} custom-call(f32[4]{0:T(128)} %get-tuple-element.107.clip, s32[1]{0:T(128)} %bitcast.103.info, bf16[512,1024]{1,0:T(8,128)(2,1)} %get-tuple-element.33.x1, bf16[512,1024]{1,0:T(8,128)(2,1)} %get-tuple-element.32.xa, bf16[512,1024]{1,0:T(8,128)(2,1)} %broadcast_select_fusion.1.xb, ...), custom_call_target="tpu_custom_call" | custom-call | flops 4294967296 | bytes 37748736 | tf_op jit(solution)/shard_map/weight_gradient/pallas_call | solution.py:314
  635.1 18.7 %weight_gradient.3 = f32[1024,4,1024]{2,1,0:T(4,128)} custom-call(f32[4]{0:T(128)} %get-tuple-element.108.clip, s32[1]{0:T(128)} %bitcast.103.info, bf16[512,1024]{1,0:T(8,128)(2,1)} %get-tuple-element.98.x1, bf16[512,1024]{1,0:T(8,128)(2,1)} %get-tuple-element.97.xa, bf16[512,1024]{1,0:T(8,128)(2,1)} %broadcast_select_fusion.3.xb, ...), custom_call_target="tpu_custom_call" | custom-call | flops 4294967296 | bytes 37748736 | tf_op jit(solution)/shard_map/weight_gradient/pallas_call | solution.py:314
  (423 shorter events, 302.8 us)
Async XLA Ops:
  7.2 180.1 %reduce-scatter.3.cloned.1.call-start = ((), (), s32[]{:S(2)}) async-start(), calls=%async_computation.2 | async-start | bytes 3932160 | tf_op jit(solution)/shard_map/reduce_scatter | solution.py:385
  46.7 235.0 %reduce-scatter.5.cloned.1.call-start = ((), (), s32[]{:S(2)}) async-start(), calls=%async_computation.3 | async-start | bytes 3932160 | tf_op jit(solution)/shard_map/reduce_scatter | solution.py:385
  52.8 25.7 %collective-permute-start.21 = (bf16[1,64,1024]{2,1,0:T(8,128)(2,1)S(1)}, bf16[1,64,1024]{2,1,0:T(8,128)(2,1)S(1)}, u32[]{:S(2)}, u32[]{:S(2)}) collective-permute-start(bf16[1,64,1024]{2,1,0:T(8,128)(2,1)S(1)} %get-tuple-element.91), channel_id=1, source_target_pairs={{0,8},{4,12},{8,0},{12,4},{16,24},{20,28},{24,16},{28,20},{1,9},{5... | collective-permute-start | bytes 393224 | tf_op jit(solution)/shard_map/ppermute | solution.py:28
  52.8 25.7 %collective-permute-start.20 = (bf16[1,64,1024]{2,1,0:T(8,128)(2,1)S(1)}, bf16[1,64,1024]{2,1,0:T(8,128)(2,1)S(1)}, u32[]{:S(2)}, u32[]{:S(2)}) collective-permute-start(bf16[1,64,1024]{2,1,0:T(8,128)(2,1)S(1)} %get-tuple-element.92), channel_id=1, source_target_pairs={{0,4},{4,0},{8,12},{12,8},{16,20},{20,16},{24,28},{28,24},{1,5},{5... | collective-permute-start | bytes 393224 | tf_op jit(solution)/shard_map/ppermute | solution.py:28
  85.0 99.9 %collective-permute-start.7 = (bf16[1024,1024]{1,0:T(8,128)(2,1)}, bf16[1024,1024]{1,0:T(8,128)(2,1)}, u32[]{:S(2)}, u32[]{:S(2)}) collective-permute-start(bf16[1024,1024]{1,0:T(8,128)(2,1)} %slice_bitcast_fusion.3), channel_id=1, source_target_pairs={{16,0},{17,1},{18,2},{19,3},{20,4},{21,5},{22,6},{23,7},{24,8},{25... | collective-permute-start | bytes 6291464 | tf_op jit(solution)/shard_map/ppermute | solution.py:36
  101.9 510.2 %all-gather.5.cloned.1.call-start = ((), (), s32[]{:S(2)}) async-start(), calls=%async_computation.5 | async-start | bytes 3932160 | tf_op jit(solution)/shard_map/all_gather | solution.py:440
  192.1 42.0 %collective-permute-start.9 = (bf16[128,1024]{1,0:T(8,128)(2,1)S(1)}, bf16[128,1024]{1,0:T(8,128)(2,1)S(1)}, u32[]{:S(2)}, u32[]{:S(2)}) collective-permute-start(bf16[128,1024]{1,0:T(8,128)(2,1)S(1)} %attend.2), channel_id=1, source_target_pairs={{0,8},{4,12},{8,0},{12,4},{1,9},{5,13},{9,1},{13,5},{2,10},{6,14},... | collective-permute-start | bytes 786440 | tf_op jit(solution)/shard_map/ppermute | solution.py:28
  194.0 40.1 %collective-permute-start.8 = (bf16[128,1024]{1,0:T(8,128)(2,1)S(1)}, bf16[128,1024]{1,0:T(8,128)(2,1)S(1)}, u32[]{:S(2)}, u32[]{:S(2)}) collective-permute-start(bf16[128,1024]{1,0:T(8,128)(2,1)S(1)} %attend.2), channel_id=1, source_target_pairs={{0,4},{4,0},{8,12},{12,8},{1,5},{5,1},{9,13},{13,9},{2,6},{6,2},{1... | collective-permute-start | bytes 786440 | tf_op jit(solution)/shard_map/ppermute | solution.py:28
  278.1 34.2 %collective-permute-start.17 = (bf16[128,1024]{1,0:T(8,128)(2,1)}, bf16[128,1024]{1,0:T(8,128)(2,1)}, u32[]{:S(2)}, u32[]{:S(2)}) collective-permute-start(bf16[128,1024]{1,0:T(8,128)(2,1)} %get-tuple-element.64), channel_id=1, source_target_pairs={{0,8},{4,12},{8,0},{12,4},{16,24},{20,28},{24,16},{28,20},{1,9},{5... | collective-permute-start | bytes 786440 | tf_op jit(solution)/shard_map/ppermute | solution.py:28
  285.0 30.5 %collective-permute-start.30 = (bf16[128,1024]{1,0:T(8,128)(2,1)S(1)}, bf16[128,1024]{1,0:T(8,128)(2,1)S(1)}, u32[]{:S(2)}, u32[]{:S(2)}) collective-permute-start(bf16[128,1024]{1,0:T(8,128)(2,1)S(1)} %attend.3), channel_id=1, source_target_pairs={{0,12},{4,8},{8,4},{12,0},{1,13},{5,9},{9,5},{13,1},{2,14},{6,10},... | collective-permute-start | bytes 786440 | tf_op jit(solution)/shard_map/ppermute | solution.py:28
  288.3 34.3 %collective-permute-start.29 = (bf16[128,1024]{1,0:T(8,128)(2,1)S(1)}, bf16[128,1024]{1,0:T(8,128)(2,1)S(1)}, u32[]{:S(2)}, u32[]{:S(2)}) collective-permute-start(bf16[128,1024]{1,0:T(8,128)(2,1)S(1)} %attend.3), channel_id=1, source_target_pairs={{0,8},{4,12},{8,0},{12,4},{1,9},{5,13},{9,1},{13,5},{2,10},{6,14},... | collective-permute-start | bytes 786440 | tf_op jit(solution)/shard_map/ppermute | solution.py:28
  290.3 32.3 %collective-permute-start.28 = (bf16[128,1024]{1,0:T(8,128)(2,1)S(1)}, bf16[128,1024]{1,0:T(8,128)(2,1)S(1)}, u32[]{:S(2)}, u32[]{:S(2)}) collective-permute-start(bf16[128,1024]{1,0:T(8,128)(2,1)S(1)} %attend.3), channel_id=1, source_target_pairs={{0,4},{4,0},{8,12},{12,8},{1,5},{5,1},{9,13},{13,9},{2,6},{6,2},{1... | collective-permute-start | bytes 786440 | tf_op jit(solution)/shard_map/ppermute | solution.py:28
  334.6 26.5 %collective-permute-start.42 = (bf16[4,64,1024]{2,1,0:T(8,128)(2,1)S(1)}, bf16[4,64,1024]{2,1,0:T(8,128)(2,1)}, u32[]{:S(2)}, u32[]{:S(2)}) collective-permute-start(bf16[4,64,1024]{2,1,0:T(8,128)(2,1)S(1)} %add_convert_fusion.5.refs_8_), channel_id=1, source_target_pairs={{0,16},{1,17},{2,18},{3,19},{4,20},{5,21},{6,22},{7,23},{8,24},{9,... | collective-permute-start | bytes 1572872 | tf_op jit(solution)/shard_map/ppermute | solution.py:36
  336.6 24.4 %collective-permute-start.41 = (bf16[4,64,1024]{2,1,0:T(8,128)(2,1)S(1)}, bf16[4,64,1024]{2,1,0:T(8,128)(2,1)}, u32[]{:S(2)}, u32[]{:S(2)}) collective-permute-start(bf16[4,64,1024]{2,1,0:T(8,128)(2,1)S(1)} %add_convert_fusion.5.refs_8_), channel_id=1, source_target_pairs={{0,18},{1,19},{2,16},{3,17},{4,22},{5,23},{6,20},{7,21},{8,26},{9,... | collective-permute-start | bytes 1572872 | tf_op jit(solution)/shard_map/ppermute | solution.py:36
  386.1 29.2 %collective-permute-start.40 = (bf16[4,64,1024]{2,1,0:T(8,128)(2,1)}, bf16[4,64,1024]{2,1,0:T(8,128)(2,1)}, u32[]{:S(2)}, u32[]{:S(2)}) collective-permute-start(bf16[4,64,1024]{2,1,0:T(8,128)(2,1)} %add_convert_fusion.4), channel_id=1, source_target_pairs={{0,2},{1,3},{2,0},{3,1},{4,6},{5,7},{6,4},{7,5},{8,10},{9,11},{10,... | collective-permute-start | bytes 1572872 | tf_op jit(solution)/shard_map/ppermute | solution.py:36
  389.4 25.8 %collective-permute-start.39 = (bf16[4,64,1024]{2,1,0:T(8,128)(2,1)}, bf16[4,64,1024]{2,1,0:T(8,128)(2,1)}, u32[]{:S(2)}, u32[]{:S(2)}) collective-permute-start(bf16[4,64,1024]{2,1,0:T(8,128)(2,1)} %add_convert_fusion.4), channel_id=1, source_target_pairs={{16,0},{17,1},{18,2},{19,3},{20,4},{21,5},{22,6},{23,7},{24,8},{25... | collective-permute-start | bytes 1572872 | tf_op jit(solution)/shard_map/ppermute | solution.py:36
  390.7 25.9 %collective-permute-start.38 = (bf16[4,64,1024]{2,1,0:T(8,128)(2,1)}, bf16[4,64,1024]{2,1,0:T(8,128)(2,1)}, u32[]{:S(2)}, u32[]{:S(2)}) collective-permute-start(bf16[4,64,1024]{2,1,0:T(8,128)(2,1)} %add_convert_fusion.4), channel_id=1, source_target_pairs={{16,2},{17,3},{18,0},{19,1},{20,6},{21,7},{22,4},{23,5},{24,10},{2... | collective-permute-start | bytes 1572872 | tf_op jit(solution)/shard_map/ppermute | solution.py:36
  435.8 25.6 %collective-permute-start.54 = (bf16[128,1024]{1,0:T(8,128)(2,1)S(1)}, bf16[128,1024]{1,0:T(8,128)(2,1)S(1)}, u32[]{:S(2)}, u32[]{:S(2)}) collective-permute-start(bf16[128,1024]{1,0:T(8,128)(2,1)S(1)} %broadcast_select_fusion.6), channel_id=1, source_target_pairs={{0,8},{4,12},{8,0},{12,4},{16,24},{20,28},{24,16},{28,20},{1,9},{5... | collective-permute-start | bytes 786440 | tf_op jit(solution)/shard_map/ppermute | solution.py:28
  436.2 25.1 %collective-permute-start.53 = (bf16[128,1024]{1,0:T(8,128)(2,1)S(1)}, bf16[128,1024]{1,0:T(8,128)(2,1)S(1)}, u32[]{:S(2)}, u32[]{:S(2)}) collective-permute-start(bf16[128,1024]{1,0:T(8,128)(2,1)S(1)} %broadcast_select_fusion.6), channel_id=1, source_target_pairs={{0,4},{4,0},{8,12},{12,8},{16,20},{20,16},{24,28},{28,24},{1,5},{5... | collective-permute-start | bytes 786440 | tf_op jit(solution)/shard_map/ppermute | solution.py:28
  444.8 28.4 %collective-permute-start.46 = (bf16[128,1024]{1,0:T(8,128)(2,1)S(1)}, bf16[128,1024]{1,0:T(8,128)(2,1)S(1)}, u32[]{:S(2)}, u32[]{:S(2)}) collective-permute-start(bf16[128,1024]{1,0:T(8,128)(2,1)S(1)} %get-tuple-element.48), channel_id=1, source_target_pairs={{0,8},{4,12},{8,0},{12,4},{1,9},{5,13},{9,1},{13,5},{2,10},{6,14},... | collective-permute-start | bytes 786440 | tf_op jit(solution)/shard_map/ppermute | solution.py:28
  480.2 154.9 %all-gather.3.cloned.1.call-start = ((), (), s32[]{:S(2)}) async-start(), calls=%async_computation.4 | async-start | bytes 3932160 | tf_op jit(solution)/shard_map/all_gather | solution.py:440
  492.9 25.2 %collective-permute-start.57 = (bf16[4,64,1024]{2,1,0:T(8,128)(2,1)S(1)}, bf16[4,64,1024]{2,1,0:T(8,128)(2,1)S(1)}, u32[]{:S(2)}, u32[]{:S(2)}) collective-permute-start(bf16[4,64,1024]{2,1,0:T(8,128)(2,1)S(1)} %add_convert_fusion.1), channel_id=1, source_target_pairs={{16,2},{17,3},{18,0},{19,1},{20,6},{21,7},{22,4},{23,5},{24,10},{2... | collective-permute-start | bytes 1572872 | tf_op jit(solution)/shard_map/ppermute | solution.py:36
  526.9 28.5 %collective-permute-start.63 = (bf16[128,1024]{1,0:T(8,128)(2,1)S(1)}, bf16[128,1024]{1,0:T(8,128)(2,1)S(1)}, u32[]{:S(2)}, u32[]{:S(2)}) collective-permute-start(bf16[128,1024]{1,0:T(8,128)(2,1)S(1)} %get-tuple-element.43), channel_id=1, source_target_pairs={{0,4},{4,0},{8,12},{12,8},{1,5},{5,1},{9,13},{13,9},{2,6},{6,2},{1... | collective-permute-start | bytes 786440 | tf_op jit(solution)/shard_map/ppermute | solution.py:28
  536.9 26.4 %collective-permute-start.61 = (bf16[128,1024]{1,0:T(8,128)(2,1)S(1)}, bf16[128,1024]{1,0:T(8,128)(2,1)S(1)}, u32[]{:S(2)}, u32[]{:S(2)}) collective-permute-start(bf16[128,1024]{1,0:T(8,128)(2,1)S(1)} %get-tuple-element.45), channel_id=1, source_target_pairs={{0,12},{4,8},{8,4},{12,0},{1,13},{5,9},{9,5},{13,1},{2,14},{6,10},... | collective-permute-start | bytes 786440 | tf_op jit(solution)/shard_map/ppermute | solution.py:28
  (131 other events, 1383.7 us)
Sparse Core Ops, SparseCore 0:
  46.8 67.9 reduce-scatter.2
  117.1 109.3 reduce-scatter.4
  480.3 70.7 all-gather.4
  569.2 65.8 all-gather.2

commit v7 on v6

--- a/solution.py
+++ b/solution.py
@@ -357,6 +357,7 @@
     own32 = inputs[0].astype(F32)
     inv = lax.rsqrt(jnp.mean(own32 * own32, axis=-1) + 1e-06)
     inv_all = gather(inv, both)
+    w_relay = jnp.where(is_dec, w[2], mp_shift(w[1], 0, dec, flip=True))
     raw_half, x, first, payloads = [], [], [], []
     keep = (jnp.arange(seq)[None] < lengths[1][:, None]).astype(BF16)
     cot = cotangent * keep[:, :, None]
@@ -371,7 +372,7 @@
         if b < mb - 1:
             parts = [mm(x[b], w[s]) for s in range(3)]
         else:
-            cot_half = to_columns(cot, parity, dec, payloads[-1:])
+            cot_half = to_columns(cot, parity, dec, [w_relay])
             cot_cols = halves(cot_half, mp_shift(cot_half, 1, dec), parity)
             cot_cols = [rows_of(cot_cols[:, i]) for i in range(mb)]
             w_k, w_v = jnp.where(is_dec, w[3], w[1]), jnp.where(is_dec, w[3], w[2])
@@ -383,11 +384,10 @@
         parts = jnp.concatenate([p.astype(BF16) for p in parts], axis=1)
         payloads.append(parts.reshape(n, seq, 3 * inner))
         first.append(lax.psum_scatter(payloads[b], "dp", scatter_dimension=0, tiled=False))
-    w_relay = jnp.where(is_dec, w[2], mp_shift(w[1], 0, dec, flip=True))
     ctx_all, enc_out, kv_terms, kv_parts, keys = [], [], [], [], []
     for b in range(mb):
         qkv = [[(first[b], i * inner)] for i in range(3)]
-        ctx = attend(info(section == 0, b), qkv, seq, inner, kv_terms[-1:] or [w_relay])
+        ctx = attend(info(section == 0, b), qkv, seq, inner, kv_terms[-1:])
         ctx = rows_of(gather(ctx, enc))
         ctx_all.append(gate(ctx, keys[-1]) if keys else ctx)
         terms = mm(ctx_all[b], w[3], NT).reshape(n, seq, depth)
@@ -418,7 +418,8 @@
         relay_all.append(gate(rows, ctx_terms[-1]) if ctx_terms else rows)
         terms = mm(relay_all[b], w_relay, NT).reshape(n, seq, depth)
         after = kv_terms[b + 1 : b + 2]
-        grad_enc.append(relay(terms, None, both, 1, enc, after)[0])
+        grad, total, _ = relay(terms, None, both, 1, enc, after)
+        grad_enc.append(grad)
         terms = mm(rows_of(grad_enc[b]), w[3]).astype(BF16)
         ctx_terms.append(terms.reshape(n, seq, inner))
         dec_send.append(send)

time: 671 us -> 606 us (0.903)
  waiting for transfers between devices: 321 us -> 258 us
  starting transfers between devices: 133 us -> 141 us
    ppermute x31, waiting for transfers between devices: 161 us -> 103 us  [mp_shift(): return lax.ppermute(x, ('section', 'mp'), pairs)]
    ppermute x38, waiting for transfers between devices: 156 us -> 110 us  [dp_shift(): return lax.ppermute(x, ('section', 'dp'), pairs)]
    reduce_scatter x2, waiting for transfers between devices: 0.02 us -> 40.4 us  [per_device(): lax.psum_scatter(payloads[b], 'dp', scatter_dimension=0, tiled=False)]
    unnamed x165 -> x143, local copies, waits for them, and re-layouts: 24.7 us -> 21.3 us
  transfers between devices with their start and end apart: 73 -> 73, of which waited for: 37 -> 38; matrix products, arithmetic and copies ran while one was open for 15% -> 18% of each run, Pallas kernels for 5% -> 5%
where the time goes in v7:
time: 606 us; the launch traced here: 597 us
  waiting for transfers between devices  258 us (43%)
  starting transfers between devices  141 us (23%)
  Pallas kernels  54.2 us (9%)
  other arithmetic  52.5 us (9%)
  matrix products  40 us (7%)
  local copies, waits for them, and re-layouts  33 us (5%)
  between operations  18.5 us (3%)
    ppermute x38, waiting for transfers between devices, dp_shift(): return lax.ppermute(x, ('section', 'dp'), pairs)  110 us
    ppermute x31, waiting for transfers between devices, mp_shift(): return lax.ppermute(x, ('section', 'mp'), pairs)  103 us
    ppermute x38, starting transfers between devices, dp_shift(): return lax.ppermute(x, ('section', 'dp'), pairs)  89.9 us
    ppermute x31, starting transfers between devices, mp_shift(): return lax.ppermute(x, ('section', 'mp'), pairs)  50.6 us
    reduce_scatter x2, waiting for transfers between devices, per_device(): lax.psum_scatter(payloads[b], 'dp', scatter_dimension=0, tiled=False)  40.4 us
    pallas_call x2, Pallas kernels, wgrad(): pl.pallas_call(functools.partial(wgrad_kernel, tokens // chunk, chunk, 1....  37.8 us
    dot_general x14, matrix products, mm(): return lax.dot_general(left, right, dims, preferred_element_type=F32)  34.3 us
    unnamed x143, local copies, waits for them, and re-layouts  21.3 us
  transfers between devices with their start and end apart: 73, of which 38 were waited for; matrix products, arithmetic and copies ran while one was open for 18% of the time, Pallas kernels for 5%

profile of v7, /device:TPU:0, one launch (start us, length us, event | category | flops | bytes accessed | tf_op | source)
XLA Modules:
  0.0 596.6 jit_solution(1151633945119810431)
XLA Ops:
  19.5 9.6 %copy.26 = bf16[1,1024,4,1024]{3,1,2,0:T(8,128)(2,1)} copy(bf16[1,1024,4,1024]{3,2,1,0:T(4,128)(2,1)} %param.8) | data formatting | bytes 16777216 | tf_op args[2]
  59.8 21.5 %collective-permute-done.15 = bf16[1024,1024]{1,0:T(8,128)(2,1)} collective-permute-done((bf16[1024,1024]{1,0:T(8,128)(2,1)}, bf16[1024,1024]{1,0:T(8,128)(2,1)}, u32[]{:S(2)}, u32[]{:S(2)}) %collective-permute-start.15) | collective-permute-done | bytes 2097184 | tf_op jit(solution)/shard_map/ppermute | solution.py:36
  106.0 14.2 %reduce-scatter.3.cloned.1.call-done = bf16[1,128,3072]{2,1,0:T(8,128)(2,1)} async-done(((bf16[4,128,3072]{2,1,0:T(8,128)(2,1)}), bf16[1,128,3072]{2,1,0:T(8,128)(2,1)}) %reduce-scatter.3.cloned.1.call-update) | async-done | bytes 786448 | tf_op jit(solution)/shard_map/reduce_scatter | solution.py:386
  136.0 15.9 %collective-permute-done.8 = bf16[128,1024]{1,0:T(8,128)(2,1)S(1)} collective-permute-done((bf16[128,1024]{1,0:T(8,128)(2,1)S(1)}, bf16[128,1024]{1,0:T(8,128)(2,1)S(1)}, u32[]{:S(2)}, u32[]{:S(2)}) %collective-permute-start.8) | collective-permute-done | bytes 262176 | tf_op jit(solution)/shard_map/ppermute | solution.py:28
  163.2 5.9 collective-permute-start.12
  181.3 10.7 %collective-permute-done.11 = bf16[4,64,1024]{2,1,0:T(8,128)(2,1)S(1)} collective-permute-done((bf16[4,64,1024]{2,1,0:T(8,128)(2,1)S(1)}, bf16[4,64,1024]{2,1,0:T(8,128)(2,1)S(1)}, u32[]{:S(2)}, u32[]{:S(2)}) %collective-permute-start.11) | collective-permute-done | bytes 524320 | tf_op jit(solution)/shard_map/ppermute | solution.py:36
  201.4 26.1 %reduce-scatter.5.cloned.1.call-done = bf16[1,128,3072]{2,1,0:T(8,128)(2,1)} async-done(((bf16[4,128,3072]{2,1,0:T(8,128)(2,1)}), bf16[1,128,3072]{2,1,0:T(8,128)(2,1)}) %reduce-scatter.5.cloned.1.call-update) | async-done | bytes 786448 | tf_op jit(solution)/shard_map/reduce_scatter | solution.py:386
  236.2 7.6 %collective-permute-start.29 = (bf16[128,1024]{1,0:T(8,128)(2,1)S(1)}, bf16[128,1024]{1,0:T(8,128)(2,1)S(1)}, u32[]{:S(2)}, u32[]{:S(2)}) collective-permute-start(bf16[128,1024]{1,0:T(8,128)(2,1)S(1)} %attend.3), channel_id=1, source_target_pairs={{0,8},{4,12},{8,0},{12,4},{1,9},{5,13},{9,1},{13,5},{2,10},{6,14},... | collective-permute-start | bytes 786440 | tf_op jit(solution)/shard_map/ppermute | solution.py:28
  247.3 11.9 %collective-permute-done.29 = bf16[128,1024]{1,0:T(8,128)(2,1)S(1)} collective-permute-done((bf16[128,1024]{1,0:T(8,128)(2,1)S(1)}, bf16[128,1024]{1,0:T(8,128)(2,1)S(1)}, u32[]{:S(2)}, u32[]{:S(2)}) %collective-permute-start.29) | collective-permute-done | bytes 262176 | tf_op jit(solution)/shard_map/ppermute | solution.py:28
  281.5 8.7 %collective-permute-done.32 = bf16[128,1024]{1,0:T(8,128)(2,1)S(1)} collective-permute-done((bf16[128,1024]{1,0:T(8,128)(2,1)S(1)}, bf16[128,1024]{1,0:T(8,128)(2,1)S(1)}, u32[]{:S(2)}, u32[]{:S(2)}) %collective-permute-start.32) | collective-permute-done | bytes 262176 | tf_op jit(solution)/shard_map/ppermute | solution.py:36
  302.7 13.2 %collective-permute-done.35 = bf16[128,1024]{1,0:T(8,128)(2,1)S(1)} collective-permute-done((bf16[128,1024]{1,0:T(8,128)(2,1)}, bf16[128,1024]{1,0:T(8,128)(2,1)S(1)}, u32[]{:S(2)}, u32[]{:S(2)}) %collective-permute-start.35) | collective-permute-done | bytes 262176 | tf_op jit(solution)/shard_map/ppermute | solution.py:28
  339.4 7.8 %collective-permute-done.49.refs_5_ = bf16[128,1024]{1,0:T(8,128)(2,1)S(1)} collective-permute-done((bf16[128,1024]{1,0:T(8,128)(2,1)S(1)}, bf16[128,1024]{1,0:T(8,128)(2,1)S(1)}, u32[]{:S(2)}, u32[]{:S(2)}) %collective-permute-start.49) | collective-permute-done | bytes 262176 | tf_op jit(solution)/shard_map/ppermute | solution.py:28
  360.3 10.6 %collective-permute-done.52 = bf16[128,1024]{1,0:T(8,128)(2,1)S(1)} collective-permute-done((bf16[128,1024]{1,0:T(8,128)(2,1)S(1)}, bf16[128,1024]{1,0:T(8,128)(2,1)S(1)}, u32[]{:S(2)}, u32[]{:S(2)}) %collective-permute-start.52) | collective-permute-done | bytes 262176 | tf_op jit(solution)/shard_map/ppermute | solution.py:36
  389.5 16.6 %collective-permute-done.54.refs_8_ = bf16[128,1024]{1,0:T(8,128)(2,1)S(1)} collective-permute-done((bf16[128,1024]{1,0:T(8,128)(2,1)S(1)}, bf16[128,1024]{1,0:T(8,128)(2,1)S(1)}, u32[]{:S(2)}, u32[]{:S(2)}) %collective-permute-start.54) | collective-permute-done | bytes 262176 | tf_op jit(solution)/shard_map/ppermute | solution.py:28
  411.8 5.8 attend_back.6
  432.3 9.6 %collective-permute-done.59 = bf16[4,64,1024]{2,1,0:T(8,128)(2,1)S(1)} collective-permute-done((bf16[4,64,1024]{2,1,0:T(8,128)(2,1)S(1)}, bf16[4,64,1024]{2,1,0:T(8,128)(2,1)S(1)}, u32[]{:S(2)}, u32[]{:S(2)}) %collective-permute-start.59) | collective-permute-done | bytes 524320 | tf_op jit(solution)/shard_map/ppermute | solution.py:36
  446.4 9.8 %collective-permute-done.57 = bf16[4,64,1024]{2,1,0:T(8,128)(2,1)S(1)} collective-permute-done((bf16[4,64,1024]{2,1,0:T(8,128)(2,1)S(1)}, bf16[4,64,1024]{2,1,0:T(8,128)(2,1)S(1)}, u32[]{:S(2)}, u32[]{:S(2)}) %collective-permute-start.57) | collective-permute-done | bytes 524320 | tf_op jit(solution)/shard_map/ppermute | solution.py:36
  465.0 6.5 %collective-permute-start.63 = (bf16[128,1024]{1,0:T(8,128)(2,1)S(1)}, bf16[128,1024]{1,0:T(8,128)(2,1)S(1)}, u32[]{:S(2)}, u32[]{:S(2)}) collective-permute-start(bf16[128,1024]{1,0:T(8,128)(2,1)S(1)} %get-tuple-element.43), channel_id=1, source_target_pairs={{0,4},{4,0},{8,12},{12,8},{1,5},{5,1},{9,13},{13,9},{2,6},{6,2},{1... | collective-permute-start | bytes 786440 | tf_op jit(solution)/shard_map/ppermute | solution.py:28
  481.3 9.9 %collective-permute-done.63.refs_5_ = bf16[128,1024]{1,0:T(8,128)(2,1)S(1)} collective-permute-done((bf16[128,1024]{1,0:T(8,128)(2,1)S(1)}, bf16[128,1024]{1,0:T(8,128)(2,1)S(1)}, u32[]{:S(2)}, u32[]{:S(2)}) %collective-permute-start.63) | collective-permute-done | bytes 262176 | tf_op jit(solution)/shard_map/ppermute | solution.py:28
  491.2 8.0 %collective-permute-done.61.refs_3_ = bf16[128,1024]{1,0:T(8,128)(2,1)S(1)} collective-permute-done((bf16[128,1024]{1,0:T(8,128)(2,1)S(1)}, bf16[128,1024]{1,0:T(8,128)(2,1)S(1)}, u32[]{:S(2)}, u32[]{:S(2)}) %collective-permute-start.61) | collective-permute-done | bytes 262176 | tf_op jit(solution)/shard_map/ppermute | solution.py:28
  499.1 5.7 attend_back.7
  530.0 5.8 collective-permute-start.66
  548.0 19.1 %weight_gradient.2.base = f32[1024,4,1024]{2,1,0:T(4,128)} custom-call(f32[4]{0:T(128)} %get-tuple-element.107.clip, s32[1]{0:T(128)} %bitcast.103.info, bf16[512,1024]{1,0:T(8,128)(2,1)} %get-tuple-element.33.x1, bf16[512,1024]{1,0:T(8,128)(2,1)} %get-tuple-element.32.xa, bf16[512,1024]{1,0:T(8,128)(2,1)} %broadcast_select_fusion.1.xb, ...), custom_call_target="tpu_custom_call" | custom-call | flops 4294967296 | bytes 37748736 | tf_op jit(solution)/shard_map/weight_gradient/pallas_call | solution.py:314
  570.9 18.7 %weight_gradient.3 = f32[1024,4,1024]{2,1,0:T(4,128)} custom-call(f32[4]{0:T(128)} %get-tuple-element.108.clip, s32[1]{0:T(128)} %bitcast.103.info, bf16[512,1024]{1,0:T(8,128)(2,1)} %get-tuple-element.98.x1, bf16[512,1024]{1,0:T(8,128)(2,1)} %get-tuple-element.97.xa, bf16[512,1024]{1,0:T(8,128)(2,1)} %broadcast_select_fusion.3.xb, ...), custom_call_target="tpu_custom_call" | custom-call | flops 4294967296 | bytes 37748736 | tf_op jit(solution)/shard_map/weight_gradient/pallas_call | solution.py:314
  (401 shorter events, 299.0 us)
Async XLA Ops:
  7.2 113.1 %reduce-scatter.3.cloned.1.call-start = ((), (), s32[]{:S(2)}) async-start(), calls=%async_computation.2 | async-start | bytes 3932160 | tf_op jit(solution)/shard_map/reduce_scatter | solution.py:386
  9.5 25.9 %collective-permute-start.6 = (f32[2,128]{1,0:T(2,128)S(1)}, f32[2,128]{1,0:T(2,128)S(1)}, u32[]{:S(2)}, u32[]{:S(2)}) collective-permute-start(f32[2,128]{1,0:T(2,128)S(1)} %add_rsqrt_fusion), channel_id=1, source_target_pairs={{0,12},{4,8},{8,4},{12,0},{16,28},{20,24},{24,20},{28,16},{1,13},{... | collective-permute-start | bytes 3080 | tf_op jit(solution)/shard_map/ppermute | solution.py:28
  33.1 48.2 %collective-permute-start.15 = (bf16[1024,1024]{1,0:T(8,128)(2,1)}, bf16[1024,1024]{1,0:T(8,128)(2,1)}, u32[]{:S(2)}, u32[]{:S(2)}) collective-permute-start(bf16[1024,1024]{1,0:T(8,128)(2,1)} %slice_bitcast_fusion.3), channel_id=1, source_target_pairs={{16,0},{17,1},{18,2},{19,3},{20,4},{21,5},{22,6},{23,7},{24,8},{25... | collective-permute-start | bytes 6291464 | tf_op jit(solution)/shard_map/ppermute | solution.py:36
  49.7 177.8 %reduce-scatter.5.cloned.1.call-start = ((), (), s32[]{:S(2)}) async-start(), calls=%async_computation.3 | async-start | bytes 3932160 | tf_op jit(solution)/shard_map/reduce_scatter | solution.py:386
  55.3 32.4 %collective-permute-start.22 = (bf16[1,64,1024]{2,1,0:T(8,128)(2,1)S(1)}, bf16[1,64,1024]{2,1,0:T(8,128)(2,1)S(1)}, u32[]{:S(2)}, u32[]{:S(2)}) collective-permute-start(bf16[1,64,1024]{2,1,0:T(8,128)(2,1)S(1)} %get-tuple-element.90), channel_id=1, source_target_pairs={{0,12},{4,8},{8,4},{12,0},{16,28},{20,24},{24,20},{28,16},{1,13},{... | collective-permute-start | bytes 393224 | tf_op jit(solution)/shard_map/ppermute | solution.py:28
  58.2 30.2 %collective-permute-start.21 = (bf16[1,64,1024]{2,1,0:T(8,128)(2,1)S(1)}, bf16[1,64,1024]{2,1,0:T(8,128)(2,1)S(1)}, u32[]{:S(2)}, u32[]{:S(2)}) collective-permute-start(bf16[1,64,1024]{2,1,0:T(8,128)(2,1)S(1)} %get-tuple-element.91), channel_id=1, source_target_pairs={{0,8},{4,12},{8,0},{12,4},{16,24},{20,28},{24,16},{28,20},{1,9},{5... | collective-permute-start | bytes 393224 | tf_op jit(solution)/shard_map/ppermute | solution.py:28
  58.2 30.2 %collective-permute-start.20 = (bf16[1,64,1024]{2,1,0:T(8,128)(2,1)S(1)}, bf16[1,64,1024]{2,1,0:T(8,128)(2,1)S(1)}, u32[]{:S(2)}, u32[]{:S(2)}) collective-permute-start(bf16[1,64,1024]{2,1,0:T(8,128)(2,1)S(1)} %get-tuple-element.92), channel_id=1, source_target_pairs={{0,4},{4,0},{8,12},{12,8},{16,20},{20,16},{24,28},{28,24},{1,5},{5... | collective-permute-start | bytes 393224 | tf_op jit(solution)/shard_map/ppermute | solution.py:28
  104.6 443.4 %all-gather.5.cloned.1.call-start = ((), (), s32[]{:S(2)}) async-start(), calls=%async_computation.5 | async-start | bytes 3932160 | tf_op jit(solution)/shard_map/all_gather | solution.py:441
  196.2 47.6 %collective-permute-start.16 = (bf16[128,1024]{1,0:T(8,128)(2,1)S(1)}, bf16[128,1024]{1,0:T(8,128)(2,1)S(1)}, u32[]{:S(2)}, u32[]{:S(2)}) collective-permute-start(bf16[128,1024]{1,0:T(8,128)(2,1)S(1)} %get-tuple-element.62), channel_id=1, source_target_pairs={{0,12},{4,8},{8,4},{12,0},{16,28},{20,24},{24,20},{28,16},{1,13},{... | collective-permute-start | bytes 786440 | tf_op jit(solution)/shard_map/ppermute | solution.py:28
  198.6 47.1 %collective-permute-start.18 = (bf16[128,1024]{1,0:T(8,128)(2,1)S(1)}, bf16[128,1024]{1,0:T(8,128)(2,1)S(1)}, u32[]{:S(2)}, u32[]{:S(2)}) collective-permute-start(bf16[128,1024]{1,0:T(8,128)(2,1)S(1)} %get-tuple-element.63), channel_id=1, source_target_pairs={{0,4},{4,0},{8,12},{12,8},{16,20},{20,16},{24,28},{28,24},{1,5},{5... | collective-permute-start | bytes 786440 | tf_op jit(solution)/shard_map/ppermute | solution.py:28
  198.6 47.2 %collective-permute-start.17 = (bf16[128,1024]{1,0:T(8,128)(2,1)S(1)}, bf16[128,1024]{1,0:T(8,128)(2,1)S(1)}, u32[]{:S(2)}, u32[]{:S(2)}) collective-permute-start(bf16[128,1024]{1,0:T(8,128)(2,1)S(1)} %get-tuple-element.64), channel_id=1, source_target_pairs={{0,8},{4,12},{8,0},{12,4},{16,24},{20,28},{24,16},{28,20},{1,9},{5... | collective-permute-start | bytes 786440 | tf_op jit(solution)/shard_map/ppermute | solution.py:28
  271.1 24.6 %collective-permute-start.42 = (bf16[4,64,1024]{2,1,0:T(8,128)(2,1)S(1)}, bf16[4,64,1024]{2,1,0:T(8,128)(2,1)}, u32[]{:S(2)}, u32[]{:S(2)}) collective-permute-start(bf16[4,64,1024]{2,1,0:T(8,128)(2,1)S(1)} %add_convert_fusion.5.refs_8_), channel_id=1, source_target_pairs={{0,16},{1,17},{2,18},{3,19},{4,20},{5,21},{6,22},{7,23},{8,24},{9,... | collective-permute-start | bytes 1572872 | tf_op jit(solution)/shard_map/ppermute | solution.py:36
  322.7 27.8 %collective-permute-start.40 = (bf16[4,64,1024]{2,1,0:T(8,128)(2,1)S(1)}, bf16[4,64,1024]{2,1,0:T(8,128)(2,1)}, u32[]{:S(2)}, u32[]{:S(2)}) collective-permute-start(bf16[4,64,1024]{2,1,0:T(8,128)(2,1)S(1)} %add_convert_fusion.4), channel_id=1, source_target_pairs={{0,2},{1,3},{2,0},{3,1},{4,6},{5,7},{6,4},{7,5},{8,10},{9,11},{10,... | collective-permute-start | bytes 1572872 | tf_op jit(solution)/shard_map/ppermute | solution.py:36
  326.1 24.5 %collective-permute-start.39 = (bf16[4,64,1024]{2,1,0:T(8,128)(2,1)S(1)}, bf16[4,64,1024]{2,1,0:T(8,128)(2,1)}, u32[]{:S(2)}, u32[]{:S(2)}) collective-permute-start(bf16[4,64,1024]{2,1,0:T(8,128)(2,1)S(1)} %add_convert_fusion.4), channel_id=1, source_target_pairs={{16,0},{17,1},{18,2},{19,3},{20,4},{21,5},{22,6},{23,7},{24,8},{25... | collective-permute-start | bytes 1572872 | tf_op jit(solution)/shard_map/ppermute | solution.py:36
  327.4 25.7 %collective-permute-start.38 = (bf16[4,64,1024]{2,1,0:T(8,128)(2,1)S(1)}, bf16[4,64,1024]{2,1,0:T(8,128)(2,1)}, u32[]{:S(2)}, u32[]{:S(2)}) collective-permute-start(bf16[4,64,1024]{2,1,0:T(8,128)(2,1)S(1)} %add_convert_fusion.4), channel_id=1, source_target_pairs={{16,2},{17,3},{18,0},{19,1},{20,6},{21,7},{22,4},{23,5},{24,10},{2... | collective-permute-start | bytes 1572872 | tf_op jit(solution)/shard_map/ppermute | solution.py:36
  373.5 32.7 %collective-permute-start.54 = (bf16[128,1024]{1,0:T(8,128)(2,1)S(1)}, bf16[128,1024]{1,0:T(8,128)(2,1)S(1)}, u32[]{:S(2)}, u32[]{:S(2)}) collective-permute-start(bf16[128,1024]{1,0:T(8,128)(2,1)S(1)} %broadcast_select_fusion.6), channel_id=1, source_target_pairs={{0,8},{4,12},{8,0},{12,4},{16,24},{20,28},{24,16},{28,20},{1,9},{5... | collective-permute-start | bytes 786440 | tf_op jit(solution)/shard_map/ppermute | solution.py:28
  373.5 32.7 %collective-permute-start.53 = (bf16[128,1024]{1,0:T(8,128)(2,1)S(1)}, bf16[128,1024]{1,0:T(8,128)(2,1)S(1)}, u32[]{:S(2)}, u32[]{:S(2)}) collective-permute-start(bf16[128,1024]{1,0:T(8,128)(2,1)S(1)} %broadcast_select_fusion.6), channel_id=1, source_target_pairs={{0,4},{4,0},{8,12},{12,8},{16,20},{20,16},{24,28},{28,24},{1,5},{5... | collective-permute-start | bytes 786440 | tf_op jit(solution)/shard_map/ppermute | solution.py:28
  379.2 26.9 %collective-permute-start.47 = (bf16[128,1024]{1,0:T(8,128)(2,1)S(1)}, bf16[128,1024]{1,0:T(8,128)(2,1)S(1)}, u32[]{:S(2)}, u32[]{:S(2)}) collective-permute-start(bf16[128,1024]{1,0:T(8,128)(2,1)S(1)} %get-tuple-element.47), channel_id=1, source_target_pairs={{0,4},{4,0},{8,12},{12,8},{1,5},{5,1},{9,13},{13,9},{2,6},{6,2},{1... | collective-permute-start | bytes 786440 | tf_op jit(solution)/shard_map/ppermute | solution.py:28
  381.5 30.3 %collective-permute-start.46 = (bf16[128,1024]{1,0:T(8,128)(2,1)S(1)}, bf16[128,1024]{1,0:T(8,128)(2,1)S(1)}, u32[]{:S(2)}, u32[]{:S(2)}) collective-permute-start(bf16[128,1024]{1,0:T(8,128)(2,1)S(1)} %get-tuple-element.48), channel_id=1, source_target_pairs={{0,8},{4,12},{8,0},{12,4},{1,9},{5,13},{9,1},{13,5},{2,10},{6,14},... | collective-permute-start | bytes 786440 | tf_op jit(solution)/shard_map/ppermute | solution.py:28
  386.3 25.4 %collective-permute-start.45 = (bf16[128,1024]{1,0:T(8,128)(2,1)S(1)}, bf16[128,1024]{1,0:T(8,128)(2,1)S(1)}, u32[]{:S(2)}, u32[]{:S(2)}) collective-permute-start(bf16[128,1024]{1,0:T(8,128)(2,1)S(1)} %get-tuple-element.49), channel_id=1, source_target_pairs={{0,12},{4,8},{8,4},{12,0},{1,13},{5,9},{9,5},{13,1},{2,14},{6,10},... | collective-permute-start | bytes 786440 | tf_op jit(solution)/shard_map/ppermute | solution.py:28
  417.5 153.4 %all-gather.3.cloned.1.call-start = ((), (), s32[]{:S(2)}) async-start(), calls=%async_computation.4 | async-start | bytes 3932160 | tf_op jit(solution)/shard_map/all_gather | solution.py:441
  431.0 25.2 %collective-permute-start.57 = (bf16[4,64,1024]{2,1,0:T(8,128)(2,1)S(1)}, bf16[4,64,1024]{2,1,0:T(8,128)(2,1)S(1)}, u32[]{:S(2)}, u32[]{:S(2)}) collective-permute-start(bf16[4,64,1024]{2,1,0:T(8,128)(2,1)S(1)} %add_convert_fusion.1), channel_id=1, source_target_pairs={{16,2},{17,3},{18,0},{19,1},{20,6},{21,7},{22,4},{23,5},{24,10},{2... | collective-permute-start | bytes 1572872 | tf_op jit(solution)/shard_map/ppermute | solution.py:36
  465.0 26.2 %collective-permute-start.63 = (bf16[128,1024]{1,0:T(8,128)(2,1)S(1)}, bf16[128,1024]{1,0:T(8,128)(2,1)S(1)}, u32[]{:S(2)}, u32[]{:S(2)}) collective-permute-start(bf16[128,1024]{1,0:T(8,128)(2,1)S(1)} %get-tuple-element.43), channel_id=1, source_target_pairs={{0,4},{4,0},{8,12},{12,8},{1,5},{5,1},{9,13},{13,9},{2,6},{6,2},{1... | collective-permute-start | bytes 786440 | tf_op jit(solution)/shard_map/ppermute | solution.py:28
  473.4 25.7 %collective-permute-start.61 = (bf16[128,1024]{1,0:T(8,128)(2,1)S(1)}, bf16[128,1024]{1,0:T(8,128)(2,1)S(1)}, u32[]{:S(2)}, u32[]{:S(2)}) collective-permute-start(bf16[128,1024]{1,0:T(8,128)(2,1)S(1)} %get-tuple-element.45), channel_id=1, source_target_pairs={{0,12},{4,8},{8,4},{12,0},{1,13},{5,9},{9,5},{13,1},{2,14},{6,10},... | collective-permute-start | bytes 786440 | tf_op jit(solution)/shard_map/ppermute | solution.py:28
  (120 other events, 1219.1 us)
Sparse Core Ops, SparseCore 0:
  49.8 70.3 reduce-scatter.2
  122.5 104.9 reduce-scatter.4
  417.7 69.3 all-gather.4
  505.0 65.8 all-gather.2

commit v8 on v6

--- a/solution.py
+++ b/solution.py
@@ -118,7 +118,7 @@
     own = jnp.where(lax.axis_index("section") == 0, total.astype(F32), 0.0)
     mine = functools.reduce(jnp.add, [g.astype(F32) for g in got], own).astype(BF16)
     other = mp_shift(mine, 1, targets)
-    return halves(mine, other, parity), total, got[-1]
+    return halves(mine, other, parity), total, got
 
 
 def add_up(sources, start):
@@ -357,84 +357,75 @@
     own32 = inputs[0].astype(F32)
     inv = lax.rsqrt(jnp.mean(own32 * own32, axis=-1) + 1e-06)
     inv_all = gather(inv, both)
-    raw_half, x, first, payloads = [], [], [], []
-    keep = (jnp.arange(seq)[None] < lengths[1][:, None]).astype(BF16)
-    cot = cotangent * keep[:, :, None]
-    cot_cols = []
-    for b in range(mb):
-        mine = to_columns(inputs[0, b : b + 1], parity, both, payloads[-1:])[:, 0]
-        if b == 0:
-            mine = gate(mine, w)
+    raw_half, x = [], []
+    for b in range(mb):
+        mine = to_columns(inputs[0, b : b + 1], parity, both, raw_half[-1:])[:, 0]
         raw = halves(mine, mp_shift(mine, 1, both), parity)
         raw_half.append(mine)
         x.append(rows_of((raw.astype(F32) * inv_all[:, b, :, None] * gain_cols).astype(BF16)))
-        if b < mb - 1:
-            parts = [mm(x[b], w[s]) for s in range(3)]
-        else:
-            cot_half = to_columns(cot, parity, dec, payloads[-1:])
-            cot_cols = halves(cot_half, mp_shift(cot_half, 1, dec), parity)
-            cot_cols = [rows_of(cot_cols[:, i]) for i in range(mb)]
-            w_k, w_v = jnp.where(is_dec, w[3], w[1]), jnp.where(is_dec, w[3], w[2])
-            parts = [
-                mm(x[b], w[0]),
-                mm(jnp.where(is_dec, cot_cols[0], x[b]), w_k),
-                mm(jnp.where(is_dec, cot_cols[1], x[b]), w_v),
-            ]
-        parts = jnp.concatenate([p.astype(BF16) for p in parts], axis=1)
-        payloads.append(parts.reshape(n, seq, 3 * inner))
-        first.append(lax.psum_scatter(payloads[b], "dp", scatter_dimension=0, tiled=False))
+    keep = (jnp.arange(seq)[None] < lengths[1][:, None]).astype(BF16)
+    cot = cotangent * keep[:, :, None]
+    first = []
+    for b in range(mb):
+        parts = [mm(x[b], w[s]).astype(BF16) for s in range(3)]
+        parts = jnp.concatenate(parts, axis=1).reshape(n, seq, 3 * inner)
+        first.append(lax.psum_scatter(parts, "dp", scatter_dimension=0, tiled=False))
+    cot_half = to_columns(cot, parity, dec, first[:1])
+    cot_cols = halves(cot_half, mp_shift(cot_half, 1, dec), parity)
+    cot_cols = [rows_of(cot_cols[:, b]) for b in range(mb)]
+    cot_terms = jnp.concatenate([mm(c, w[3]).astype(BF16) for c in cot_cols], axis=1)
+    dec_gctx = to_owner(cot_terms.reshape(n, seq, mb * inner), dec)
     w_relay = jnp.where(is_dec, w[2], mp_shift(w[1], 0, dec, flip=True))
     ctx_all, enc_out, kv_terms, kv_parts, keys = [], [], [], [], []
     for b in range(mb):
         qkv = [[(first[b], i * inner)] for i in range(3)]
-        ctx = attend(info(section == 0, b), qkv, seq, inner, kv_terms[-1:] or [w_relay])
+        after = [*kv_terms[-1:], *dec_gctx[1:]] if b else []
+        ctx = attend(info(section == 0, b), qkv, seq, inner, after)
         ctx = rows_of(gather(ctx, enc))
         ctx_all.append(gate(ctx, keys[-1]) if keys else ctx)
         terms = mm(ctx_all[b], w[3], NT).reshape(n, seq, depth)
-        out, total, posted = relay(terms, raw_half[b], enc, 0, both)
+        out, total, _ = relay(terms, raw_half[b], enc, 0, both)
         enc_out.append(out)
         terms = mm(rows_of(enc_out[b]), w_relay).astype(BF16).reshape(n, seq, inner)
         kv_terms.append(terms)
         kv_parts.append(to_owner(terms, both))
         key = functools.reduce(jnp.add, [k.astype(F32) for k in kv_parts[b]]).astype(BF16)
         keys.append(mp_shift(key, 0, enc, flip=True))
-    relay_all, grad_enc, dec_send, dec_gram, ctx_terms = [], [], [], [], []
+    relay_all, grad_enc, dec_send, dec_gram, dec_grads, ctx_terms = [], [], [], [], [], []
     for b in range(mb):
         operands = [
             [(first[b], 0)],
             [(keys[b], 0)],
             [(part, 0) for part in kv_parts[b]],
-            [(first[mb - 1], (1 + b) * inner)],
+            [(part, b * inner) for part in dec_gctx],
         ]
         after = (total,) if b == 0 else ()
         gk, gv, send, gram = attend_back(
             info(section == 1, b), operands, seq, inner, True, (), after
         )
-        rows = jnp.where(is_dec, gv, mp_shift(gk, 0, dec, flip=True))
-        if b == 0:
-            rows = gate(rows, posted)
-        slots = exchange(rows, both)
-        rows = rows_of(in_order(slots))
-        relay_all.append(gate(rows, ctx_terms[-1]) if ctx_terms else rows)
+        dec_grads.append(jnp.where(is_dec, gv, mp_shift(gk, 0, dec, flip=True)))
+        dec_send.append(send)
+        dec_gram.append(gram)
+    slots = []
+    for b in range(mb):
+        rows = gate(dec_grads[b], *kv_parts[-1][1:]) if b == 0 else dec_grads[b]
+        slots.append(exchange(rows, both))
+    for b in range(mb):
+        rows = rows_of(in_order(slots[b]))
+        relay_all.append(gate(rows, dec_grads[-1]) if b == 0 else rows)
         terms = mm(relay_all[b], w_relay, NT).reshape(n, seq, depth)
-        after = kv_terms[b + 1 : b + 2]
-        grad_enc.append(relay(terms, None, both, 1, enc, after)[0])
+        after = slots[-1][1:] if b < mb - 1 else ()
+        grad, _, got = relay(terms, None, both, 1, enc, after)
+        grad_enc.append(grad)
         terms = mm(rows_of(grad_enc[b]), w[3]).astype(BF16)
         ctx_terms.append(terms.reshape(n, seq, inner))
-        dec_send.append(send)
-        dec_gram.append(gram)
     send_all, enc_gram = [], []
     for b in range(mb):
         gctx = to_owner(ctx_terms[b], enc)
         operands = [[(first[b], i * inner)] for i in range(3)] + [[(part, 0) for part in gctx]]
+        after = got if b < mb - 1 else ()
         _, _, send, gram = attend_back(
-            info(section == 0, b),
-            operands,
-            seq,
-            inner,
-            False,
-            (dec_send[b],),
-            slots[1:] if b < mb - 1 else (),
+            info(section == 0, b), operands, seq, inner, False, (dec_send[b],), after
         )
         enc_gram.append(gram)
         send_all.append(lax.all_gather(send, "dp", axis=0, tiled=True))

time: 671 us -> 693 us (1.033)
  starting transfers between devices: 133 us -> 187 us
  waiting for transfers between devices: 321 us -> 285 us
  other arithmetic: 57.6 us -> 41.9 us
  local copies, waits for them, and re-layouts: 37.6 us -> 49.4 us
  matrix products: 39 us -> 46.1 us
    ppermute x31, waiting for transfers between devices: 161 us -> 83 us  [mp_shift(): return lax.ppermute(x, ('section', 'mp'), pairs)]
    reduce_scatter x2, waiting for transfers between devices: 0.02 us -> 41 us  [per_device(): lax.psum_scatter(parts, 'dp', scatter_dimension=0, tiled=False)]
    ppermute x31, starting transfers between devices: 46.2 us -> 82.9 us  [mp_shift(): return lax.ppermute(x, ('section', 'mp'), pairs)]
    ppermute x38 -> x41, starting transfers between devices: 86.3 us -> 104 us  [dp_shift(): return lax.ppermute(x, ('section', 'dp'), pairs)]
    all_gather x2, waiting for transfers between devices: 3.9 us -> 14.3 us  [per_device(): send_all.append(lax.all_gather(send, 'dp', axis=0, tiled=True))]
    ppermute x38 -> x41, waiting for transfers between devices: 156 us -> 147 us  [dp_shift(): return lax.ppermute(x, ('section', 'dp'), pairs)]
    unnamed x165 -> x191, local copies, waits for them, and re-layouts: 24.7 us -> 32.5 us
    dot_general x14 -> x16, matrix products: 33.3 us -> 36.7 us  [mm(): return lax.dot_general(left, right, dims, preferred_element_type=F32)]
  transfers between devices with their start and end apart: 73 -> 76, of which waited for: 37 -> 37; matrix products, arithmetic and copies ran while one was open for 15% -> 14% of each run, Pallas kernels for 5% -> 4%
where the time goes in v8:
time: 693 us; the launch traced here: 683 us
  waiting for transfers between devices  285 us (41%)
  starting transfers between devices  187 us (27%)
  Pallas kernels  54.8 us (8%)
  local copies, waits for them, and re-layouts  49.4 us (7%)
  matrix products  46.1 us (7%)
  other arithmetic  41.9 us (6%)
  between operations  18.7 us (3%)
    ppermute x41, waiting for transfers between devices, dp_shift(): return lax.ppermute(x, ('section', 'dp'), pairs)  147 us
    ppermute x41, starting transfers between devices, dp_shift(): return lax.ppermute(x, ('section', 'dp'), pairs)  104 us
    ppermute x31, waiting for transfers between devices, mp_shift(): return lax.ppermute(x, ('section', 'mp'), pairs)  83 us
    ppermute x31, starting transfers between devices, mp_shift(): return lax.ppermute(x, ('section', 'mp'), pairs)  82.9 us
    reduce_scatter x2, waiting for transfers between devices, per_device(): lax.psum_scatter(parts, 'dp', scatter_dimension=0, tiled=False)  41 us
    pallas_call x2, Pallas kernels, wgrad(): pl.pallas_call(functools.partial(wgrad_kernel, tokens // chunk, chunk, 1....  37.7 us
    dot_general x16, matrix products, mm(): return lax.dot_general(left, right, dims, preferred_element_type=F32)  36.7 us
    unnamed x191, local copies, waits for them, and re-layouts  32.5 us
  transfers between devices with their start and end apart: 76, of which 37 were waited for; matrix products, arithmetic and copies ran while one was open for 14% of the time, Pallas kernels for 4%

profile of v8, /device:TPU:0, one launch (start us, length us, event | category | flops | bytes accessed | tf_op | source)
XLA Modules:
  0.0 683.4 jit_solution(1660883234235307416)
XLA Ops:
  18.6 6.6 collective-permute-done.1
  35.1 9.7 %copy.25 = bf16[1,1024,4,1024]{3,1,2,0:T(8,128)(2,1)} copy(bf16[1,1024,4,1024]{3,2,1,0:T(4,128)(2,1)} %param.8) | data formatting | bytes 16777216 | tf_op args[2]
  77.8 41.0 %reduce-scatter.3.cloned.1.call-done = bf16[1,128,3072]{2,1,0:T(8,128)(2,1)} async-done(((bf16[4,128,3072]{2,1,0:T(8,128)(2,1)}), bf16[1,128,3072]{2,1,0:T(8,128)(2,1)}) %reduce-scatter.3.cloned.1.call-update) | async-done | bytes 786448 | tf_op jit(solution)/shard_map/reduce_scatter | solution.py:372
  143.5 37.5 %collective-permute-done.8 = bf16[128,1024]{1,0:T(8,128)(2,1)S(1)} collective-permute-done((bf16[128,1024]{1,0:T(8,128)(2,1)S(1)}, bf16[128,1024]{1,0:T(8,128)(2,1)S(1)}, u32[]{:S(2)}, u32[]{:S(2)}) %collective-permute-start.8) | collective-permute-done | bytes 262176 | tf_op jit(solution)/shard_map/ppermute | solution.py:28
  207.8 10.8 %collective-permute-done.11 = bf16[4,64,1024]{2,1,0:T(8,128)(2,1)S(1)} collective-permute-done((bf16[4,64,1024]{2,1,0:T(8,128)(2,1)S(1)}, bf16[4,64,1024]{2,1,0:T(8,128)(2,1)S(1)}, u32[]{:S(2)}, u32[]{:S(2)}) %collective-permute-start.11) | collective-permute-done | bytes 524320 | tf_op jit(solution)/shard_map/ppermute | solution.py:36
  245.1 17.8 %collective-permute-done.17.refs_5_ = bf16[128,1024]{1,0:T(8,128)(2,1)} collective-permute-done((bf16[128,1024]{1,0:T(8,128)(2,1)}, bf16[128,1024]{1,0:T(8,128)(2,1)}, u32[]{:S(2)}, u32[]{:S(2)}) %collective-permute-start.17) | collective-permute-done | bytes 262176 | tf_op jit(solution)/shard_map/ppermute | solution.py:28
  264.8 38.1 %collective-permute-start.19 = (bf16[128,1024]{1,0:T(8,128)(2,1)S(1)}, bf16[128,1024]{1,0:T(8,128)(2,1)S(1)}, u32[]{:S(2)}, u32[]{:S(2)}) collective-permute-start(bf16[128,1024]{1,0:T(8,128)(2,1)S(1)} %get-tuple-element.38), channel_id=1, source_target_pairs={{0,16},{1,17},{2,18},{3,19},{4,20},{5,21},{6,22},{7,23},{8,24},{9,... | collective-permute-start | bytes 786440 | tf_op jit(solution)/shard_map/ppermute | solution.py:36
  322.6 9.8 %collective-permute-done.38 = bf16[4,64,1024]{2,1,0:T(8,128)(2,1)S(1)} collective-permute-done((bf16[4,64,1024]{2,1,0:T(8,128)(2,1)S(1)}, bf16[4,64,1024]{2,1,0:T(8,128)(2,1)S(1)}, u32[]{:S(2)}, u32[]{:S(2)}) %collective-permute-start.38) | collective-permute-done | bytes 524320 | tf_op jit(solution)/shard_map/ppermute | solution.py:36
  333.6 10.4 %collective-permute-done.36 = bf16[4,64,1024]{2,1,0:T(8,128)(2,1)S(1)} collective-permute-done((bf16[4,64,1024]{2,1,0:T(8,128)(2,1)S(1)}, bf16[4,64,1024]{2,1,0:T(8,128)(2,1)S(1)}, u32[]{:S(2)}, u32[]{:S(2)}) %collective-permute-start.36) | collective-permute-done | bytes 524320 | tf_op jit(solution)/shard_map/ppermute | solution.py:36
  362.4 6.8 collective-permute-done.42.refs_3_.refs_6_
  394.0 11.0 %collective-permute-done.44 = bf16[128,1024]{1,0:T(8,128)(2,1)S(1)} collective-permute-done((bf16[128,1024]{1,0:T(8,128)(2,1)}, bf16[128,1024]{1,0:T(8,128)(2,1)S(1)}, u32[]{:S(2)}, u32[]{:S(2)}) %collective-permute-start.44) | collective-permute-done | bytes 262176 | tf_op jit(solution)/shard_map/ppermute | solution.py:28
  418.5 11.3 %collective-permute-done.53.refs_2_ = bf16[128,1024]{1,0:T(8,128)(2,1)S(1)} collective-permute-done((bf16[128,1024]{1,0:T(8,128)(2,1)}, bf16[128,1024]{1,0:T(8,128)(2,1)S(1)}, u32[]{:S(2)}, u32[]{:S(2)}) %collective-permute-start.53) | collective-permute-done | bytes 262176 | tf_op jit(solution)/shard_map/ppermute | solution.py:28
  447.8 5.5 collective-permute-done.50
  453.3 7.4 %collective-permute-done.49 = bf16[4,64,1024]{2,1,0:T(8,128)(2,1)} collective-permute-done((bf16[4,64,1024]{2,1,0:T(8,128)(2,1)}, bf16[4,64,1024]{2,1,0:T(8,128)(2,1)}, u32[]{:S(2)}, u32[]{:S(2)}) %collective-permute-start.49) | collective-permute-done | bytes 524320 | tf_op jit(solution)/shard_map/ppermute | solution.py:36
  486.1 10.3 %collective-permute-done.60.refs_7_ = bf16[4,64,1024]{2,1,0:T(8,128)(2,1)S(1)} collective-permute-done((bf16[4,64,1024]{2,1,0:T(8,128)(2,1)S(1)}, bf16[4,64,1024]{2,1,0:T(8,128)(2,1)S(1)}, u32[]{:S(2)}, u32[]{:S(2)}) %collective-permute-start.60) | collective-permute-done | bytes 524320 | tf_op jit(solution)/shard_map/ppermute | solution.py:36
  501.0 5.6 attend_back.6
  521.7 7.4 %collective-permute-start.66 = (bf16[128,1024]{1,0:T(8,128)(2,1)S(1)}, bf16[128,1024]{1,0:T(8,128)(2,1)S(1)}, u32[]{:S(2)}, u32[]{:S(2)}) collective-permute-start(bf16[128,1024]{1,0:T(8,128)(2,1)S(1)} %get-tuple-element.46), channel_id=1, source_target_pairs={{0,4},{4,0},{8,12},{12,8},{1,5},{5,1},{9,13},{13,9},{2,6},{6,2},{1... | collective-permute-start | bytes 786440 | tf_op jit(solution)/shard_map/ppermute | solution.py:28
  538.1 15.5 %collective-permute-done.66.refs_5_ = bf16[128,1024]{1,0:T(8,128)(2,1)S(1)} collective-permute-done((bf16[128,1024]{1,0:T(8,128)(2,1)S(1)}, bf16[128,1024]{1,0:T(8,128)(2,1)S(1)}, u32[]{:S(2)}, u32[]{:S(2)}) %collective-permute-start.66) | collective-permute-done | bytes 262176 | tf_op jit(solution)/shard_map/ppermute | solution.py:28
  553.6 9.0 %collective-permute-done.65.refs_4_ = bf16[128,1024]{1,0:T(8,128)(2,1)S(1)} collective-permute-done((bf16[128,1024]{1,0:T(8,128)(2,1)S(1)}, bf16[128,1024]{1,0:T(8,128)(2,1)S(1)}, u32[]{:S(2)}, u32[]{:S(2)}) %collective-permute-start.65) | collective-permute-done | bytes 262176 | tf_op jit(solution)/shard_map/ppermute | solution.py:28
  566.3 6.0 attend_back.7
  590.6 22.4 %collective-permute-start.69 = (f32[2,4]{1,0:T(2,128)S(1)}, f32[2,4]{1,0:T(2,128)S(1)}, u32[]{:S(2)}, u32[]{:S(2)}) collective-permute-start(f32[2,4]{1,0:T(2,128)S(1)} %fusion.125), channel_id=1, source_target_pairs={{0,4},{4,0},{8,12},{12,8},{16,20},{20,16},{24,28},{28,24},{1,5},{5... | collective-permute-start | bytes 104 | tf_op jit(solution)/shard_map/ppermute | solution.py:28
  624.5 18.9 %weight_gradient.2.base = f32[1024,4,1024]{2,1,0:T(4,128)} custom-call(f32[4]{0:T(128)} %get-tuple-element.112.clip, s32[1]{0:T(128)} %bitcast.105.info, bf16[512,1024]{1,0:T(8,128)(2,1)} %get-tuple-element.33.x1, bf16[512,1024]{1,0:T(8,128)(2,1)} %get-tuple-element.32.xa, bf16[512,1024]{1,0:T(8,128)(2,1)} %broadcast_select_fusion.1.xb, ...), custom_call_target="tpu_custom_call" | custom-call | flops 4294967296 | bytes 37748736 | tf_op jit(solution)/shard_map/weight_gradient/pallas_call | solution.py:314
  643.4 14.3 %all-gather.3.cloned.1.call-done.send = bf16[512,3072]{1,0:T(8,128)(2,1)} async-done(((bf16[128,3072]{1,0:T(8,128)(2,1)}), bf16[512,3072]{1,0:T(8,128)(2,1)}) %all-gather.3.cloned.1.call-update) | async-done | bytes 3145744 | tf_op jit(solution)/shard_map/all_gather | solution.py:431
  657.7 18.7 %weight_gradient.3 = f32[1024,4,1024]{2,1,0:T(4,128)} custom-call(f32[4]{0:T(128)} %get-tuple-element.113.clip, s32[1]{0:T(128)} %bitcast.105.info, bf16[512,1024]{1,0:T(8,128)(2,1)} %get-tuple-element.101.x1, bf16[512,1024]{1,0:T(8,128)(2,1)} %get-tuple-element.100.xa, bf16[512,1024]{1,0:T(8,128)(2,1)} %broadcast_select_fusion.3.xb, ...), custom_call_target="tpu_custom_call" | custom-call | flops 4294967296 | bytes 37748736 | tf_op jit(solution)/shard_map/weight_gradient/pallas_call | solution.py:314
  (459 shorter events, 312.7 us)
Async XLA Ops:
  7.2 111.6 %reduce-scatter.3.cloned.1.call-start = ((), (), s32[]{:S(2)}) async-start(), calls=%async_computation.2 | async-start | bytes 3932160 | tf_op jit(solution)/shard_map/reduce_scatter | solution.py:372
  58.2 172.7 %reduce-scatter.5.cloned.1.call-start = ((), (), s32[]{:S(2)}) async-start(), calls=%async_computation.3 | async-start | bytes 3932160 | tf_op jit(solution)/shard_map/reduce_scatter | solution.py:372
  61.5 126.2 %collective-permute-start.15 = (bf16[1024,1024]{1,0:T(8,128)(2,1)}, bf16[1024,1024]{1,0:T(8,128)(2,1)}, u32[]{:S(2)}, u32[]{:S(2)}) collective-permute-start(bf16[1024,1024]{1,0:T(8,128)(2,1)} %slice_bitcast_fusion.1), channel_id=1, source_target_pairs={{16,0},{17,1},{18,2},{19,3},{20,4},{21,5},{22,6},{23,7},{24,8},{25... | collective-permute-start | bytes 6291464 | tf_op jit(solution)/shard_map/ppermute | solution.py:36
  73.6 550.9 %all-gather.5.cloned.1.call-start = ((), (), s32[]{:S(2)}) async-start(), calls=%async_computation.5 | async-start | bytes 3932160 | tf_op jit(solution)/shard_map/all_gather | solution.py:431
  129.3 51.7 %collective-permute-start.8 = (bf16[128,1024]{1,0:T(8,128)(2,1)S(1)}, bf16[128,1024]{1,0:T(8,128)(2,1)S(1)}, u32[]{:S(2)}, u32[]{:S(2)}) collective-permute-start(bf16[128,1024]{1,0:T(8,128)(2,1)S(1)} %attend.2), channel_id=1, source_target_pairs={{0,8},{4,12},{8,0},{12,4},{1,9},{5,13},{9,1},{13,5},{2,10},{6,14},... | collective-permute-start | bytes 786440 | tf_op jit(solution)/shard_map/ppermute | solution.py:28
  131.6 49.4 %collective-permute-start.7 = (bf16[128,1024]{1,0:T(8,128)(2,1)S(1)}, bf16[128,1024]{1,0:T(8,128)(2,1)S(1)}, u32[]{:S(2)}, u32[]{:S(2)}) collective-permute-start(bf16[128,1024]{1,0:T(8,128)(2,1)S(1)} %attend.2), channel_id=1, source_target_pairs={{0,4},{4,0},{8,12},{12,8},{1,5},{5,1},{9,13},{13,9},{2,6},{6,2},{1... | collective-permute-start | bytes 786440 | tf_op jit(solution)/shard_map/ppermute | solution.py:28
  136.8 60.2 %collective-permute-start.23 = (bf16[4,2,64,1024]{3,2,1,0:T(8,128)(2,1)}, bf16[4,2,64,1024]{3,2,1,0:T(8,128)(2,1)}, u32[]{:S(2)}, u32[]{:S(2)}) collective-permute-start(bf16[4,2,64,1024]{3,2,1,0:T(8,128)(2,1)} %pad_maximum_fusion.6), channel_id=1, source_target_pairs={{16,17},{17,16},{18,19},{19,18},{20,21},{21,20},{22,23},{23,22},{2... | collective-permute-start | bytes 3145736 | tf_op jit(solution)/shard_map/ppermute | solution.py:36
  195.6 23.0 %collective-permute-start.11 = (bf16[4,64,1024]{2,1,0:T(8,128)(2,1)S(1)}, bf16[4,64,1024]{2,1,0:T(8,128)(2,1)S(1)}, u32[]{:S(2)}, u32[]{:S(2)}) collective-permute-start(bf16[4,64,1024]{2,1,0:T(8,128)(2,1)S(1)} %add_convert_fusion.7), channel_id=1, source_target_pairs={{0,18},{1,19},{2,16},{3,17},{4,22},{5,23},{6,20},{7,21},{8,26},{9,... | collective-permute-start | bytes 1572872 | tf_op jit(solution)/shard_map/ppermute | solution.py:36
  228.7 34.2 %collective-permute-start.17 = (bf16[128,1024]{1,0:T(8,128)(2,1)}, bf16[128,1024]{1,0:T(8,128)(2,1)}, u32[]{:S(2)}, u32[]{:S(2)}) collective-permute-start(bf16[128,1024]{1,0:T(8,128)(2,1)} %get-tuple-element.67), channel_id=1, source_target_pairs={{0,8},{4,12},{8,0},{12,4},{16,24},{20,28},{24,16},{28,20},{1,9},{5... | collective-permute-start | bytes 786440 | tf_op jit(solution)/shard_map/ppermute | solution.py:28
  235.0 68.0 %collective-permute-start.33 = (bf16[128,1024]{1,0:T(8,128)(2,1)S(1)}, bf16[128,1024]{1,0:T(8,128)(2,1)S(1)}, u32[]{:S(2)}, u32[]{:S(2)}) collective-permute-start(bf16[128,1024]{1,0:T(8,128)(2,1)S(1)} %attend.3), channel_id=1, source_target_pairs={{0,12},{4,8},{8,4},{12,0},{1,13},{5,9},{9,5},{13,1},{2,14},{6,10},... | collective-permute-start | bytes 786440 | tf_op jit(solution)/shard_map/ppermute | solution.py:28
  239.8 63.1 %collective-permute-start.32 = (bf16[128,1024]{1,0:T(8,128)(2,1)S(1)}, bf16[128,1024]{1,0:T(8,128)(2,1)S(1)}, u32[]{:S(2)}, u32[]{:S(2)}) collective-permute-start(bf16[128,1024]{1,0:T(8,128)(2,1)S(1)} %attend.3), channel_id=1, source_target_pairs={{0,8},{4,12},{8,0},{12,4},{1,9},{5,13},{9,1},{13,5},{2,10},{6,14},... | collective-permute-start | bytes 786440 | tf_op jit(solution)/shard_map/ppermute | solution.py:28
  241.8 61.2 %collective-permute-start.31 = (bf16[128,1024]{1,0:T(8,128)(2,1)S(1)}, bf16[128,1024]{1,0:T(8,128)(2,1)S(1)}, u32[]{:S(2)}, u32[]{:S(2)}) collective-permute-start(bf16[128,1024]{1,0:T(8,128)(2,1)S(1)} %attend.3), channel_id=1, source_target_pairs={{0,4},{4,0},{8,12},{12,8},{1,5},{5,1},{9,13},{13,9},{2,6},{6,2},{1... | collective-permute-start | bytes 786440 | tf_op jit(solution)/shard_map/ppermute | solution.py:28
  264.8 43.5 %collective-permute-start.19 = (bf16[128,1024]{1,0:T(8,128)(2,1)S(1)}, bf16[128,1024]{1,0:T(8,128)(2,1)S(1)}, u32[]{:S(2)}, u32[]{:S(2)}) collective-permute-start(bf16[128,1024]{1,0:T(8,128)(2,1)S(1)} %get-tuple-element.38), channel_id=1, source_target_pairs={{0,16},{1,17},{2,18},{3,19},{4,20},{5,21},{6,22},{7,23},{8,24},{9,... | collective-permute-start | bytes 786440 | tf_op jit(solution)/shard_map/ppermute | solution.py:36
  321.3 22.7 %collective-permute-start.36 = (bf16[4,64,1024]{2,1,0:T(8,128)(2,1)S(1)}, bf16[4,64,1024]{2,1,0:T(8,128)(2,1)S(1)}, u32[]{:S(2)}, u32[]{:S(2)}) collective-permute-start(bf16[4,64,1024]{2,1,0:T(8,128)(2,1)S(1)} %add_convert_fusion.5.refs_11_), channel_id=1, source_target_pairs={{0,18},{1,19},{2,16},{3,17},{4,22},{5,23},{6,20},{7,21},{8,26},{9,... | collective-permute-start | bytes 1572872 | tf_op jit(solution)/shard_map/ppermute | solution.py:36
  352.4 22.2 %collective-permute-start.41 = (bf16[128,1024]{1,0:T(8,128)(2,1)}, bf16[128,1024]{1,0:T(8,128)(2,1)}, u32[]{:S(2)}, u32[]{:S(2)}) collective-permute-start(bf16[128,1024]{1,0:T(8,128)(2,1)} %get-tuple-element.64), channel_id=1, source_target_pairs={{0,8},{4,12},{8,0},{12,4},{16,24},{20,28},{24,16},{28,20},{1,9},{5... | collective-permute-start | bytes 786440 | tf_op jit(solution)/shard_map/ppermute | solution.py:28
  437.6 23.2 %collective-permute-start.49 = (bf16[4,64,1024]{2,1,0:T(8,128)(2,1)}, bf16[4,64,1024]{2,1,0:T(8,128)(2,1)}, u32[]{:S(2)}, u32[]{:S(2)}) collective-permute-start(bf16[4,64,1024]{2,1,0:T(8,128)(2,1)} %add_convert_fusion.3), channel_id=1, source_target_pairs={{16,2},{17,3},{18,0},{19,1},{20,6},{21,7},{22,4},{23,5},{24,10},{2... | collective-permute-start | bytes 1572872 | tf_op jit(solution)/shard_map/ppermute | solution.py:36
  441.5 23.0 %collective-permute-start.59 = (bf16[4,64,1024]{2,1,0:T(8,128)(2,1)}, bf16[4,64,1024]{2,1,0:T(8,128)(2,1)}, u32[]{:S(2)}, u32[]{:S(2)}) collective-permute-start(bf16[4,64,1024]{2,1,0:T(8,128)(2,1)} %constant_dynamic-slice_fusion.1), channel_id=1, source_target_pairs={{0,1},{1,0},{2,3},{3,2},{16,17},{17,16},{18,19},{19,18},{4,5},{5,4... | collective-permute-start | bytes 1572872 | tf_op jit(solution)/shard_map/ppermute | solution.py:36
  470.6 25.8 %collective-permute-start.60 = (bf16[4,64,1024]{2,1,0:T(8,128)(2,1)S(1)}, bf16[4,64,1024]{2,1,0:T(8,128)(2,1)S(1)}, u32[]{:S(2)}, u32[]{:S(2)}) collective-permute-start(bf16[4,64,1024]{2,1,0:T(8,128)(2,1)S(1)} %add_convert_fusion.1), channel_id=1, source_target_pairs={{16,2},{17,3},{18,0},{19,1},{20,6},{21,7},{22,4},{23,5},{24,10},{2... | collective-permute-start | bytes 1572872 | tf_op jit(solution)/shard_map/ppermute | solution.py:36
  477.8 23.2 %collective-permute-start.57 = (bf16[128,1024]{1,0:T(8,128)(2,1)S(1)}, bf16[128,1024]{1,0:T(8,128)(2,1)S(1)}, u32[]{:S(2)}, u32[]{:S(2)}) collective-permute-start(bf16[128,1024]{1,0:T(8,128)(2,1)S(1)} %get-tuple-element.51), channel_id=1, source_target_pairs={{0,8},{4,12},{8,0},{12,4},{1,9},{5,13},{9,1},{13,5},{2,10},{6,14},... | collective-permute-start | bytes 786440 | tf_op jit(solution)/shard_map/ppermute | solution.py:28
  507.5 150.2 %all-gather.3.cloned.1.call-start = ((), (), s32[]{:S(2)}) async-start(), calls=%async_computation.4 | async-start | bytes 3932160 | tf_op jit(solution)/shard_map/all_gather | solution.py:431
  521.7 31.9 %collective-permute-start.66 = (bf16[128,1024]{1,0:T(8,128)(2,1)S(1)}, bf16[128,1024]{1,0:T(8,128)(2,1)S(1)}, u32[]{:S(2)}, u32[]{:S(2)}) collective-permute-start(bf16[128,1024]{1,0:T(8,128)(2,1)S(1)} %get-tuple-element.46), channel_id=1, source_target_pairs={{0,4},{4,0},{8,12},{12,8},{1,5},{5,1},{9,13},{13,9},{2,6},{6,2},{1... | collective-permute-start | bytes 786440 | tf_op jit(solution)/shard_map/ppermute | solution.py:28
  529.1 33.5 %collective-permute-start.65 = (bf16[128,1024]{1,0:T(8,128)(2,1)S(1)}, bf16[128,1024]{1,0:T(8,128)(2,1)S(1)}, u32[]{:S(2)}, u32[]{:S(2)}) collective-permute-start(bf16[128,1024]{1,0:T(8,128)(2,1)S(1)} %get-tuple-element.47), channel_id=1, source_target_pairs={{0,8},{4,12},{8,0},{12,4},{1,9},{5,13},{9,1},{13,5},{2,10},{6,14},... | collective-permute-start | bytes 786440 | tf_op jit(solution)/shard_map/ppermute | solution.py:28
  531.7 34.6 %collective-permute-start.64 = (bf16[128,1024]{1,0:T(8,128)(2,1)S(1)}, bf16[128,1024]{1,0:T(8,128)(2,1)S(1)}, u32[]{:S(2)}, u32[]{:S(2)}) collective-permute-start(bf16[128,1024]{1,0:T(8,128)(2,1)S(1)} %get-tuple-element.48), channel_id=1, source_target_pairs={{0,12},{4,8},{8,4},{12,0},{1,13},{5,9},{9,5},{13,1},{2,14},{6,10},... | collective-permute-start | bytes 786440 | tf_op jit(solution)/shard_map/ppermute | solution.py:28
  590.6 24.6 %collective-permute-start.69 = (f32[2,4]{1,0:T(2,128)S(1)}, f32[2,4]{1,0:T(2,128)S(1)}, u32[]{:S(2)}, u32[]{:S(2)}) collective-permute-start(f32[2,4]{1,0:T(2,128)S(1)} %fusion.125), channel_id=1, source_target_pairs={{0,4},{4,0},{8,12},{12,8},{16,20},{20,16},{24,28},{28,24},{1,5},{5... | collective-permute-start | bytes 104 | tf_op jit(solution)/shard_map/ppermute | solution.py:28
  (147 other events, 1389.5 us)
Sparse Core Ops, SparseCore 0:
  58.3 60.4 reduce-scatter.2
  121.1 78.5 reduce-scatter.4
  507.6 87.4 all-gather.4
  596.5 61.1 all-gather.2

commit v9 on v7

--- a/solution.py
+++ b/solution.py
@@ -357,24 +357,22 @@
     own32 = inputs[0].astype(F32)
     inv = lax.rsqrt(jnp.mean(own32 * own32, axis=-1) + 1e-06)
     inv_all = gather(inv, both)
-    w_relay = jnp.where(is_dec, w[2], mp_shift(w[1], 0, dec, flip=True))
-    raw_half, x, first, payloads = [], [], [], []
-    keep = (jnp.arange(seq)[None] < lengths[1][:, None]).astype(BF16)
-    cot = cotangent * keep[:, :, None]
-    cot_cols = []
-    for b in range(mb):
-        mine = to_columns(inputs[0, b : b + 1], parity, both, payloads[-1:])[:, 0]
-        if b == 0:
-            mine = gate(mine, w)
+    raw_half, x = [], []
+    for b in range(mb):
+        mine = to_columns(inputs[0, b : b + 1], parity, both, raw_half[-1:])[:, 0]
         raw = halves(mine, mp_shift(mine, 1, both), parity)
         raw_half.append(mine)
         x.append(rows_of((raw.astype(F32) * inv_all[:, b, :, None] * gain_cols).astype(BF16)))
+    keep = (jnp.arange(seq)[None] < lengths[1][:, None]).astype(BF16)
+    cot = cotangent * keep[:, :, None]
+    cot_half = to_columns(cot, parity, dec)
+    cot_cols = halves(cot_half, mp_shift(cot_half, 1, dec), parity)
+    cot_cols = [rows_of(cot_cols[:, b]) for b in range(mb)]
+    first = []
+    for b in range(mb):
         if b < mb - 1:
             parts = [mm(x[b], w[s]) for s in range(3)]
         else:
-            cot_half = to_columns(cot, parity, dec, [w_relay])
-            cot_cols = halves(cot_half, mp_shift(cot_half, 1, dec), parity)
-            cot_cols = [rows_of(cot_cols[:, i]) for i in range(mb)]
             w_k, w_v = jnp.where(is_dec, w[3], w[1]), jnp.where(is_dec, w[3], w[2])
             parts = [
                 mm(x[b], w[0]),
@@ -382,8 +380,12 @@
                 mm(jnp.where(is_dec, cot_cols[1], x[b]), w_v),
             ]
         parts = jnp.concatenate([p.astype(BF16) for p in parts], axis=1)
-        payloads.append(parts.reshape(n, seq, 3 * inner))
-        first.append(lax.psum_scatter(payloads[b], "dp", scatter_dimension=0, tiled=False))
+        first.append(
+            lax.psum_scatter(
+                parts.reshape(n, seq, 3 * inner), "dp", scatter_dimension=0, tiled=False
+            )
+        )
+    w_relay = jnp.where(is_dec, w[2], mp_shift(w[1], 0, dec, flip=True))
     ctx_all, enc_out, kv_terms, kv_parts, keys = [], [], [], [], []
     for b in range(mb):
         qkv = [[(first[b], i * inner)] for i in range(3)]

time: 606 us -> 592 us (0.977)
  waiting for transfers between devices: 258 us -> 248 us
  starting transfers between devices: 141 us -> 133 us
    ppermute x31, waiting for transfers between devices: 103 us -> 83.6 us  [mp_shift(): return lax.ppermute(x, ('section', 'mp'), pairs)]
    ppermute x38, waiting for transfers between devices: 110 us -> 127 us  [dp_shift(): return lax.ppermute(x, ('section', 'dp'), pairs)]
    reduce_scatter x2, waiting for transfers between devices: 40.4 us -> 32.4 us  [per_device(): lax.psum_scatter(parts.reshape(n, seq, 3 * inner), 'dp', scatter_dimensio...]
    unnamed x143 -> x169, local copies, waits for them, and re-layouts: 21.3 us -> 24.3 us
  transfers between devices with their start and end apart: 73 -> 73, of which waited for: 38 -> 37; matrix products, arithmetic and copies ran while one was open for 18% -> 17% of each run, Pallas kernels for 5% -> 5%
where the time goes in v9:
time: 592 us; the launch traced here: 583 us
  waiting for transfers between devices  248 us (42%)
  starting transfers between devices  133 us (22%)
  Pallas kernels  54.2 us (9%)
  other arithmetic  51.1 us (9%)
  matrix products  42.1 us (7%)
  local copies, waits for them, and re-layouts  35.6 us (6%)
  between operations  18.7 us (3%)
    ppermute x38, waiting for transfers between devices, dp_shift(): return lax.ppermute(x, ('section', 'dp'), pairs)  127 us
    ppermute x38, starting transfers between devices, dp_shift(): return lax.ppermute(x, ('section', 'dp'), pairs)  85.8 us
    ppermute x31, waiting for transfers between devices, mp_shift(): return lax.ppermute(x, ('section', 'mp'), pairs)  83.6 us
    ppermute x31, starting transfers between devices, mp_shift(): return lax.ppermute(x, ('section', 'mp'), pairs)  46.7 us
    pallas_call x2, Pallas kernels, wgrad(): pl.pallas_call(functools.partial(wgrad_kernel, tokens // chunk, chunk, 1....  37.9 us
    dot_general x14, matrix products, mm(): return lax.dot_general(left, right, dims, preferred_element_type=F32)  35 us
    reduce_scatter x2, waiting for transfers between devices, per_device(): lax.psum_scatter(parts.reshape(n, seq, 3 * inner), 'dp', scatter_dimensio...  32.4 us
    unnamed x169, local copies, waits for them, and re-layouts  24.3 us
  transfers between devices with their start and end apart: 73, of which 37 were waited for; matrix products, arithmetic and copies ran while one was open for 17% of the time, Pallas kernels for 5%

profile of v9, /device:TPU:0, one launch (start us, length us, event | category | flops | bytes accessed | tf_op | source)
XLA Modules:
  0.0 582.8 jit_solution(12693502878729326549)
XLA Ops:
  18.6 6.6 %collective-permute-done.1 = bf16[1,64,1024]{2,1,0:T(8,128)(2,1)S(1)} collective-permute-done((bf16[1,64,1024]{2,1,0:T(8,128)(2,1)S(1)}, bf16[1,64,1024]{2,1,0:T(8,128)(2,1)S(1)}, u32[]{:S(2)}, u32[]{:S(2)}) %collective-permute-start.1) | collective-permute-done | bytes 131104 | tf_op jit(solution)/shard_map/ppermute | solution.py:28
  35.1 9.7 %copy.28 = bf16[1,1024,4,1024]{3,1,2,0:T(8,128)(2,1)} copy(bf16[1,1024,4,1024]{3,2,1,0:T(4,128)(2,1)} %param.8) | data formatting | bytes 16777216 | tf_op args[2]
  86.8 32.4 %reduce-scatter.3.cloned.1.call-done = bf16[1,128,3072]{2,1,0:T(8,128)(2,1)} async-done(((bf16[4,128,3072]{2,1,0:T(8,128)(2,1)}), bf16[1,128,3072]{2,1,0:T(8,128)(2,1)}) %reduce-scatter.3.cloned.1.call-update) | async-done | bytes 786448 | tf_op jit(solution)/shard_map/reduce_scatter | solution.py:384
  136.5 13.0 %collective-permute-done.8 = bf16[128,1024]{1,0:T(8,128)(2,1)S(1)} collective-permute-done((bf16[128,1024]{1,0:T(8,128)(2,1)S(1)}, bf16[128,1024]{1,0:T(8,128)(2,1)S(1)}, u32[]{:S(2)}, u32[]{:S(2)}) %collective-permute-start.8) | collective-permute-done | bytes 262176 | tf_op jit(solution)/shard_map/ppermute | solution.py:28
  167.8 9.8 %collective-permute-done.13 = bf16[4,64,1024]{2,1,0:T(8,128)(2,1)S(1)} collective-permute-done((bf16[4,64,1024]{2,1,0:T(8,128)(2,1)S(1)}, bf16[4,64,1024]{2,1,0:T(8,128)(2,1)S(1)}, u32[]{:S(2)}, u32[]{:S(2)}) %collective-permute-start.13) | collective-permute-done | bytes 524320 | tf_op jit(solution)/shard_map/ppermute | solution.py:36
  178.7 10.4 %collective-permute-done.11 = bf16[4,64,1024]{2,1,0:T(8,128)(2,1)S(1)} collective-permute-done((bf16[4,64,1024]{2,1,0:T(8,128)(2,1)S(1)}, bf16[4,64,1024]{2,1,0:T(8,128)(2,1)S(1)}, u32[]{:S(2)}, u32[]{:S(2)}) %collective-permute-start.11) | collective-permute-done | bytes 524320 | tf_op jit(solution)/shard_map/ppermute | solution.py:36
  216.5 19.3 %collective-permute-done.17.refs_5_ = bf16[128,1024]{1,0:T(8,128)(2,1)S(1)} collective-permute-done((bf16[128,1024]{1,0:T(8,128)(2,1)S(1)}, bf16[128,1024]{1,0:T(8,128)(2,1)S(1)}, u32[]{:S(2)}, u32[]{:S(2)}) %collective-permute-start.17) | collective-permute-done | bytes 262176 | tf_op jit(solution)/shard_map/ppermute | solution.py:28
  237.4 8.9 %collective-permute-done.29 = bf16[128,1024]{1,0:T(8,128)(2,1)S(1)} collective-permute-done((bf16[128,1024]{1,0:T(8,128)(2,1)S(1)}, bf16[128,1024]{1,0:T(8,128)(2,1)S(1)}, u32[]{:S(2)}, u32[]{:S(2)}) %collective-permute-start.29) | collective-permute-done | bytes 262176 | tf_op jit(solution)/shard_map/ppermute | solution.py:28
  268.6 8.7 %collective-permute-done.32 = bf16[128,1024]{1,0:T(8,128)(2,1)S(1)} collective-permute-done((bf16[128,1024]{1,0:T(8,128)(2,1)S(1)}, bf16[128,1024]{1,0:T(8,128)(2,1)S(1)}, u32[]{:S(2)}, u32[]{:S(2)}) %collective-permute-start.32) | collective-permute-done | bytes 262176 | tf_op jit(solution)/shard_map/ppermute | solution.py:36
  289.7 12.3 %collective-permute-done.35 = bf16[128,1024]{1,0:T(8,128)(2,1)S(1)} collective-permute-done((bf16[128,1024]{1,0:T(8,128)(2,1)}, bf16[128,1024]{1,0:T(8,128)(2,1)S(1)}, u32[]{:S(2)}, u32[]{:S(2)}) %collective-permute-start.35) | collective-permute-done | bytes 262176 | tf_op jit(solution)/shard_map/ppermute | solution.py:28
  325.6 7.7 %collective-permute-done.49.refs_5_ = bf16[128,1024]{1,0:T(8,128)(2,1)S(1)} collective-permute-done((bf16[128,1024]{1,0:T(8,128)(2,1)S(1)}, bf16[128,1024]{1,0:T(8,128)(2,1)S(1)}, u32[]{:S(2)}, u32[]{:S(2)}) %collective-permute-start.49) | collective-permute-done | bytes 262176 | tf_op jit(solution)/shard_map/ppermute | solution.py:28
  346.5 10.4 %collective-permute-done.52 = bf16[128,1024]{1,0:T(8,128)(2,1)S(1)} collective-permute-done((bf16[128,1024]{1,0:T(8,128)(2,1)S(1)}, bf16[128,1024]{1,0:T(8,128)(2,1)S(1)}, u32[]{:S(2)}, u32[]{:S(2)}) %collective-permute-start.52) | collective-permute-done | bytes 262176 | tf_op jit(solution)/shard_map/ppermute | solution.py:36
  375.7 16.5 %collective-permute-done.54.refs_8_ = bf16[128,1024]{1,0:T(8,128)(2,1)S(1)} collective-permute-done((bf16[128,1024]{1,0:T(8,128)(2,1)S(1)}, bf16[128,1024]{1,0:T(8,128)(2,1)S(1)}, u32[]{:S(2)}, u32[]{:S(2)}) %collective-permute-start.54) | collective-permute-done | bytes 262176 | tf_op jit(solution)/shard_map/ppermute | solution.py:28
  392.2 5.6 collective-permute-done.46.refs_4_
  397.8 5.7 attend_back.6
  418.5 9.6 %collective-permute-done.59 = bf16[4,64,1024]{2,1,0:T(8,128)(2,1)S(1)} collective-permute-done((bf16[4,64,1024]{2,1,0:T(8,128)(2,1)S(1)}, bf16[4,64,1024]{2,1,0:T(8,128)(2,1)S(1)}, u32[]{:S(2)}, u32[]{:S(2)}) %collective-permute-start.59) | collective-permute-done | bytes 524320 | tf_op jit(solution)/shard_map/ppermute | solution.py:36
  432.6 9.8 %collective-permute-done.57 = bf16[4,64,1024]{2,1,0:T(8,128)(2,1)S(1)} collective-permute-done((bf16[4,64,1024]{2,1,0:T(8,128)(2,1)S(1)}, bf16[4,64,1024]{2,1,0:T(8,128)(2,1)S(1)}, u32[]{:S(2)}, u32[]{:S(2)}) %collective-permute-start.57) | collective-permute-done | bytes 524320 | tf_op jit(solution)/shard_map/ppermute | solution.py:36
  451.7 6.5 %collective-permute-start.63 = (bf16[128,1024]{1,0:T(8,128)(2,1)S(1)}, bf16[128,1024]{1,0:T(8,128)(2,1)S(1)}, u32[]{:S(2)}, u32[]{:S(2)}) collective-permute-start(bf16[128,1024]{1,0:T(8,128)(2,1)S(1)} %get-tuple-element.47), channel_id=1, source_target_pairs={{0,4},{4,0},{8,12},{12,8},{1,5},{5,1},{9,13},{13,9},{2,6},{6,2},{1... | collective-permute-start | bytes 786440 | tf_op jit(solution)/shard_map/ppermute | solution.py:28
  467.9 9.4 %collective-permute-done.63.refs_5_ = bf16[128,1024]{1,0:T(8,128)(2,1)S(1)} collective-permute-done((bf16[128,1024]{1,0:T(8,128)(2,1)S(1)}, bf16[128,1024]{1,0:T(8,128)(2,1)S(1)}, u32[]{:S(2)}, u32[]{:S(2)}) %collective-permute-start.63) | collective-permute-done | bytes 262176 | tf_op jit(solution)/shard_map/ppermute | solution.py:28
  477.3 8.0 %collective-permute-done.61.refs_3_ = bf16[128,1024]{1,0:T(8,128)(2,1)S(1)} collective-permute-done((bf16[128,1024]{1,0:T(8,128)(2,1)S(1)}, bf16[128,1024]{1,0:T(8,128)(2,1)S(1)}, u32[]{:S(2)}, u32[]{:S(2)}) %collective-permute-start.61) | collective-permute-done | bytes 262176 | tf_op jit(solution)/shard_map/ppermute | solution.py:28
  485.3 5.7 attend_back.7
  515.9 5.8 collective-permute-start.66
  532.6 19.1 %weight_gradient.2.base = f32[1024,4,1024]{2,1,0:T(4,128)} custom-call(f32[4]{0:T(128)} %get-tuple-element.109.clip, s32[1]{0:T(128)} %bitcast.105.info, bf16[512,1024]{1,0:T(8,128)(2,1)} %get-tuple-element.33.x1, bf16[512,1024]{1,0:T(8,128)(2,1)} %get-tuple-element.32.xa, bf16[512,1024]{1,0:T(8,128)(2,1)} %broadcast_select_fusion.1.xb, ...), custom_call_target="tpu_custom_call" | custom-call | flops 4294967296 | bytes 37748736 | tf_op jit(solution)/shard_map/weight_gradient/pallas_call | solution.py:314
  557.1 18.7 %weight_gradient.3 = f32[1024,4,1024]{2,1,0:T(4,128)} custom-call(f32[4]{0:T(128)} %get-tuple-element.110.clip, s32[1]{0:T(128)} %bitcast.105.info, bf16[512,1024]{1,0:T(8,128)(2,1)} %get-tuple-element.98.x1, bf16[512,1024]{1,0:T(8,128)(2,1)} %get-tuple-element.97.xa, bf16[512,1024]{1,0:T(8,128)(2,1)} %broadcast_select_fusion.3.xb, ...), custom_call_target="tpu_custom_call" | custom-call | flops 4294967296 | bytes 37748736 | tf_op jit(solution)/shard_map/weight_gradient/pallas_call | solution.py:314
  (423 shorter events, 294.2 us)
Async XLA Ops:
  7.2 112.0 %reduce-scatter.3.cloned.1.call-start = ((), (), s32[]{:S(2)}) async-start(), calls=%async_computation.2 | async-start | bytes 3932160 | tf_op jit(solution)/shard_map/reduce_scatter | solution.py:384
  58.5 143.9 %reduce-scatter.5.cloned.1.call-start = ((), (), s32[]{:S(2)}) async-start(), calls=%async_computation.3 | async-start | bytes 3932160 | tf_op jit(solution)/shard_map/reduce_scatter | solution.py:384
  85.3 447.3 %all-gather.5.cloned.1.call-start = ((), (), s32[]{:S(2)}) async-start(), calls=%async_computation.5 | async-start | bytes 3932160 | tf_op jit(solution)/shard_map/all_gather | solution.py:443
  126.0 23.6 %collective-permute-start.8 = (bf16[128,1024]{1,0:T(8,128)(2,1)S(1)}, bf16[128,1024]{1,0:T(8,128)(2,1)S(1)}, u32[]{:S(2)}, u32[]{:S(2)}) collective-permute-start(bf16[128,1024]{1,0:T(8,128)(2,1)S(1)} %attend.2), channel_id=1, source_target_pairs={{0,8},{4,12},{8,0},{12,4},{1,9},{5,13},{9,1},{13,5},{2,10},{6,14},... | collective-permute-start | bytes 786440 | tf_op jit(solution)/shard_map/ppermute | solution.py:28
  135.2 58.3 %collective-permute-start.15 = (bf16[1024,1024]{1,0:T(8,128)(2,1)}, bf16[1024,1024]{1,0:T(8,128)(2,1)S(1)}, u32[]{:S(2)}, u32[]{:S(2)}) collective-permute-start(bf16[1024,1024]{1,0:T(8,128)(2,1)} %slice_bitcast_fusion.3), channel_id=1, source_target_pairs={{16,0},{17,1},{18,2},{19,3},{20,4},{21,5},{22,6},{23,7},{24,8},{25... | collective-permute-start | bytes 6291464 | tf_op jit(solution)/shard_map/ppermute | solution.py:36
  166.5 22.7 %collective-permute-start.11 = (bf16[4,64,1024]{2,1,0:T(8,128)(2,1)S(1)}, bf16[4,64,1024]{2,1,0:T(8,128)(2,1)S(1)}, u32[]{:S(2)}, u32[]{:S(2)}) collective-permute-start(bf16[4,64,1024]{2,1,0:T(8,128)(2,1)S(1)} %add_convert_fusion.7), channel_id=1, source_target_pairs={{0,18},{1,19},{2,16},{3,17},{4,22},{5,23},{6,20},{7,21},{8,26},{9,... | collective-permute-start | bytes 1572872 | tf_op jit(solution)/shard_map/ppermute | solution.py:36
  201.1 34.8 %collective-permute-start.17 = (bf16[128,1024]{1,0:T(8,128)(2,1)S(1)}, bf16[128,1024]{1,0:T(8,128)(2,1)S(1)}, u32[]{:S(2)}, u32[]{:S(2)}) collective-permute-start(bf16[128,1024]{1,0:T(8,128)(2,1)S(1)} %get-tuple-element.68), channel_id=1, source_target_pairs={{0,8},{4,12},{8,0},{12,4},{16,24},{20,28},{24,16},{28,20},{1,9},{5... | collective-permute-start | bytes 786440 | tf_op jit(solution)/shard_map/ppermute | solution.py:28
  205.7 31.7 %collective-permute-start.30 = (bf16[128,1024]{1,0:T(8,128)(2,1)S(1)}, bf16[128,1024]{1,0:T(8,128)(2,1)S(1)}, u32[]{:S(2)}, u32[]{:S(2)}) collective-permute-start(bf16[128,1024]{1,0:T(8,128)(2,1)S(1)} %attend.3), channel_id=1, source_target_pairs={{0,12},{4,8},{8,4},{12,0},{1,13},{5,9},{9,5},{13,1},{2,14},{6,10},... | collective-permute-start | bytes 786440 | tf_op jit(solution)/shard_map/ppermute | solution.py:28
  210.2 36.1 %collective-permute-start.29 = (bf16[128,1024]{1,0:T(8,128)(2,1)S(1)}, bf16[128,1024]{1,0:T(8,128)(2,1)S(1)}, u32[]{:S(2)}, u32[]{:S(2)}) collective-permute-start(bf16[128,1024]{1,0:T(8,128)(2,1)S(1)} %attend.3), channel_id=1, source_target_pairs={{0,8},{4,12},{8,0},{12,4},{1,9},{5,13},{9,1},{13,5},{2,10},{6,14},... | collective-permute-start | bytes 786440 | tf_op jit(solution)/shard_map/ppermute | solution.py:28
  212.3 34.0 %collective-permute-start.28 = (bf16[128,1024]{1,0:T(8,128)(2,1)S(1)}, bf16[128,1024]{1,0:T(8,128)(2,1)S(1)}, u32[]{:S(2)}, u32[]{:S(2)}) collective-permute-start(bf16[128,1024]{1,0:T(8,128)(2,1)S(1)} %attend.3), channel_id=1, source_target_pairs={{0,4},{4,0},{8,12},{12,8},{1,5},{5,1},{9,13},{13,9},{2,6},{6,2},{1... | collective-permute-start | bytes 786440 | tf_op jit(solution)/shard_map/ppermute | solution.py:28
  258.2 24.5 %collective-permute-start.42 = (bf16[4,64,1024]{2,1,0:T(8,128)(2,1)S(1)}, bf16[4,64,1024]{2,1,0:T(8,128)(2,1)}, u32[]{:S(2)}, u32[]{:S(2)}) collective-permute-start(bf16[4,64,1024]{2,1,0:T(8,128)(2,1)S(1)} %add_convert_fusion.5.refs_8_), channel_id=1, source_target_pairs={{0,16},{1,17},{2,18},{3,19},{4,20},{5,21},{6,22},{7,23},{8,24},{9,... | collective-permute-start | bytes 1572872 | tf_op jit(solution)/shard_map/ppermute | solution.py:36
  260.3 22.4 %collective-permute-start.41 = (bf16[4,64,1024]{2,1,0:T(8,128)(2,1)S(1)}, bf16[4,64,1024]{2,1,0:T(8,128)(2,1)}, u32[]{:S(2)}, u32[]{:S(2)}) collective-permute-start(bf16[4,64,1024]{2,1,0:T(8,128)(2,1)S(1)} %add_convert_fusion.5.refs_8_), channel_id=1, source_target_pairs={{0,18},{1,19},{2,16},{3,17},{4,22},{5,23},{6,20},{7,21},{8,26},{9,... | collective-permute-start | bytes 1572872 | tf_op jit(solution)/shard_map/ppermute | solution.py:36
  309.0 27.8 %collective-permute-start.40 = (bf16[4,64,1024]{2,1,0:T(8,128)(2,1)S(1)}, bf16[4,64,1024]{2,1,0:T(8,128)(2,1)}, u32[]{:S(2)}, u32[]{:S(2)}) collective-permute-start(bf16[4,64,1024]{2,1,0:T(8,128)(2,1)S(1)} %add_convert_fusion.4), channel_id=1, source_target_pairs={{0,2},{1,3},{2,0},{3,1},{4,6},{5,7},{6,4},{7,5},{8,10},{9,11},{10,... | collective-permute-start | bytes 1572872 | tf_op jit(solution)/shard_map/ppermute | solution.py:36
  312.4 24.4 %collective-permute-start.39 = (bf16[4,64,1024]{2,1,0:T(8,128)(2,1)S(1)}, bf16[4,64,1024]{2,1,0:T(8,128)(2,1)}, u32[]{:S(2)}, u32[]{:S(2)}) collective-permute-start(bf16[4,64,1024]{2,1,0:T(8,128)(2,1)S(1)} %add_convert_fusion.4), channel_id=1, source_target_pairs={{16,0},{17,1},{18,2},{19,3},{20,4},{21,5},{22,6},{23,7},{24,8},{25... | collective-permute-start | bytes 1572872 | tf_op jit(solution)/shard_map/ppermute | solution.py:36
  313.7 25.6 %collective-permute-start.38 = (bf16[4,64,1024]{2,1,0:T(8,128)(2,1)S(1)}, bf16[4,64,1024]{2,1,0:T(8,128)(2,1)}, u32[]{:S(2)}, u32[]{:S(2)}) collective-permute-start(bf16[4,64,1024]{2,1,0:T(8,128)(2,1)S(1)} %add_convert_fusion.4), channel_id=1, source_target_pairs={{16,2},{17,3},{18,0},{19,1},{20,6},{21,7},{22,4},{23,5},{24,10},{2... | collective-permute-start | bytes 1572872 | tf_op jit(solution)/shard_map/ppermute | solution.py:36
  359.0 33.1 %collective-permute-start.54 = (bf16[128,1024]{1,0:T(8,128)(2,1)S(1)}, bf16[128,1024]{1,0:T(8,128)(2,1)S(1)}, u32[]{:S(2)}, u32[]{:S(2)}) collective-permute-start(bf16[128,1024]{1,0:T(8,128)(2,1)S(1)} %broadcast_select_fusion.6), channel_id=1, source_target_pairs={{0,8},{4,12},{8,0},{12,4},{16,24},{20,28},{24,16},{28,20},{1,9},{5... | collective-permute-start | bytes 786440 | tf_op jit(solution)/shard_map/ppermute | solution.py:28
  359.5 32.7 %collective-permute-start.53 = (bf16[128,1024]{1,0:T(8,128)(2,1)S(1)}, bf16[128,1024]{1,0:T(8,128)(2,1)S(1)}, u32[]{:S(2)}, u32[]{:S(2)}) collective-permute-start(bf16[128,1024]{1,0:T(8,128)(2,1)S(1)} %broadcast_select_fusion.6), channel_id=1, source_target_pairs={{0,4},{4,0},{8,12},{12,8},{16,20},{20,16},{24,28},{28,24},{1,5},{5... | collective-permute-start | bytes 786440 | tf_op jit(solution)/shard_map/ppermute | solution.py:28
  365.4 26.8 %collective-permute-start.47 = (bf16[128,1024]{1,0:T(8,128)(2,1)S(1)}, bf16[128,1024]{1,0:T(8,128)(2,1)S(1)}, u32[]{:S(2)}, u32[]{:S(2)}) collective-permute-start(bf16[128,1024]{1,0:T(8,128)(2,1)S(1)} %get-tuple-element.51), channel_id=1, source_target_pairs={{0,4},{4,0},{8,12},{12,8},{1,5},{5,1},{9,13},{13,9},{2,6},{6,2},{1... | collective-permute-start | bytes 786440 | tf_op jit(solution)/shard_map/ppermute | solution.py:28
  367.5 30.3 %collective-permute-start.46 = (bf16[128,1024]{1,0:T(8,128)(2,1)S(1)}, bf16[128,1024]{1,0:T(8,128)(2,1)S(1)}, u32[]{:S(2)}, u32[]{:S(2)}) collective-permute-start(bf16[128,1024]{1,0:T(8,128)(2,1)S(1)} %get-tuple-element.52), channel_id=1, source_target_pairs={{0,8},{4,12},{8,0},{12,4},{1,9},{5,13},{9,1},{13,5},{2,10},{6,14},... | collective-permute-start | bytes 786440 | tf_op jit(solution)/shard_map/ppermute | solution.py:28
  371.9 25.9 %collective-permute-start.45 = (bf16[128,1024]{1,0:T(8,128)(2,1)S(1)}, bf16[128,1024]{1,0:T(8,128)(2,1)S(1)}, u32[]{:S(2)}, u32[]{:S(2)}) collective-permute-start(bf16[128,1024]{1,0:T(8,128)(2,1)S(1)} %get-tuple-element.53), channel_id=1, source_target_pairs={{0,12},{4,8},{8,4},{12,0},{1,13},{5,9},{9,5},{13,1},{2,14},{6,10},... | collective-permute-start | bytes 786440 | tf_op jit(solution)/shard_map/ppermute | solution.py:28
  403.5 153.5 %all-gather.3.cloned.1.call-start = ((), (), s32[]{:S(2)}) async-start(), calls=%async_computation.4 | async-start | bytes 3932160 | tf_op jit(solution)/shard_map/all_gather | solution.py:443
  417.2 25.2 %collective-permute-start.57 = (bf16[4,64,1024]{2,1,0:T(8,128)(2,1)S(1)}, bf16[4,64,1024]{2,1,0:T(8,128)(2,1)S(1)}, u32[]{:S(2)}, u32[]{:S(2)}) collective-permute-start(bf16[4,64,1024]{2,1,0:T(8,128)(2,1)S(1)} %add_convert_fusion.1), channel_id=1, source_target_pairs={{16,2},{17,3},{18,0},{19,1},{20,6},{21,7},{22,4},{23,5},{24,10},{2... | collective-permute-start | bytes 1572872 | tf_op jit(solution)/shard_map/ppermute | solution.py:36
  451.7 25.6 %collective-permute-start.63 = (bf16[128,1024]{1,0:T(8,128)(2,1)S(1)}, bf16[128,1024]{1,0:T(8,128)(2,1)S(1)}, u32[]{:S(2)}, u32[]{:S(2)}) collective-permute-start(bf16[128,1024]{1,0:T(8,128)(2,1)S(1)} %get-tuple-element.47), channel_id=1, source_target_pairs={{0,4},{4,0},{8,12},{12,8},{1,5},{5,1},{9,13},{13,9},{2,6},{6,2},{1... | collective-permute-start | bytes 786440 | tf_op jit(solution)/shard_map/ppermute | solution.py:28
  460.1 25.2 %collective-permute-start.61 = (bf16[128,1024]{1,0:T(8,128)(2,1)S(1)}, bf16[128,1024]{1,0:T(8,128)(2,1)S(1)}, u32[]{:S(2)}, u32[]{:S(2)}) collective-permute-start(bf16[128,1024]{1,0:T(8,128)(2,1)S(1)} %get-tuple-element.49), channel_id=1, source_target_pairs={{0,12},{4,8},{8,4},{12,0},{1,13},{5,9},{9,5},{13,1},{2,14},{6,10},... | collective-permute-start | bytes 786440 | tf_op jit(solution)/shard_map/ppermute | solution.py:28
  (133 other events, 1252.2 us)
Sparse Core Ops, SparseCore 0:
  58.6 60.5 reduce-scatter.2
  121.5 79.9 reduce-scatter.4
  403.7 70.0 all-gather.4
  491.2 65.8 all-gather.2
